TPU v7x, 32 devices: a whole 2x2x4 slice. The times are simulated.
32 devices in a mesh: expert: 8 (over z, y), shard: 4 (over x, core).
Axes of the slice: x: 2, y: 2, z: 4, core: 2. Of those that a mesh axis runs over, the one named last changes fastest.
Arguments:
- tokens: bfloat16 [5120, 2048], P('expert'), may hold values from -6 to 6
- norm_attn: bfloat16 [2048], replicated, may hold values from 0.5 to 1.5
- w_query: bfloat16 [2048, 2048], P('expert', 'shard'), may hold values from -0.125 to 0.125
- b_query: bfloat16 [2048], replicated, may hold values from -3 to 3
- w_key: bfloat16 [2048, 2048], P('expert', 'shard'), may hold values from -0.125 to 0.125
- b_key: bfloat16 [2048], replicated, may hold values from -3 to 3
- w_value: bfloat16 [2048, 2048], P('expert', 'shard'), may hold values from -0.125 to 0.125
- b_value: bfloat16 [2048], replicated, may hold values from -3 to 3
- w_output: bfloat16 [2048, 2048], P('shard', 'expert'), may hold values from -1 to 1
- norm_ffn: bfloat16 [2048], replicated, may hold values from 0.5 to 1.5
- w_router: bfloat16 [2048, 8], replicated, may hold values from -0.0625 to 0.0625
- shared_mix: bfloat16 [2048], replicated, may hold values from -0.125 to 0.125
- shared_gate: bfloat16 [2048, 5632], P('expert', 'shard'), may hold values from -0.125 to 0.125
- shared_up: bfloat16 [2048, 5632], P('expert', 'shard'), may hold values from -0.125 to 0.125
- shared_down: bfloat16 [5632, 2048], P('shard', 'expert'), may hold values from -0.15625 to 0.15625
- expert_gate: bfloat16 [8, 2048, 1408], P('expert', None, 'shard'), may hold values from -0.125 to 0.125
- expert_up: bfloat16 [8, 2048, 1408], P('expert', None, 'shard'), may hold values from -0.125 to 0.125
- expert_down: bfloat16 [8, 1408, 2048], P('expert', 'shard'), may hold values from -1.25 to 1.25
- routes: int32 [5120, 4], P(('expert', 'shard')), may hold values from 0 to 7, all different within a row; in each aligned block of 160 rows (0 to 159, 160 to 319, ...) at most 100 rows name the same one
- seq_lengths: int32 [32, 8], P('expert'), may hold values from 0 to 160, as said below
- cotangent: bfloat16 [5120, 2048], P('expert'), may hold values from -6 to 6
Outputs:
- block_out: bfloat16 [5120, 2048], P(('expert', 'shard'))
- grad_tokens: float32 [5120, 2048], P(('expert', 'shard'))
- grad_norm_attn: float32 [2048], replicated
- grad_w_query: float32 [2048, 2048], P('expert', 'shard')
- grad_b_query: float32 [2048], replicated
- grad_w_key: float32 [2048, 2048], P('expert', 'shard')
- grad_b_key: float32 [2048], replicated
- grad_w_value: float32 [2048, 2048], P('expert', 'shard')
- grad_b_value: float32 [2048], replicated
- grad_w_output: float32 [2048, 2048], P('shard', 'expert')
- grad_norm_ffn: float32 [2048], replicated
- grad_w_router: float32 [2048, 8], replicated
- grad_shared_mix: float32 [2048], replicated
- grad_shared_gate: float32 [2048, 5632], P('expert', 'shard')
- grad_shared_up: float32 [2048, 5632], P('expert', 'shard')
- grad_shared_down: float32 [5632, 2048], P('shard', 'expert')
- grad_expert_gate: float32 [8, 2048, 1408], P('expert', None, 'shard')
- grad_expert_up: float32 [8, 2048, 1408], P('expert', None, 'shard')
- grad_expert_down: float32 [8, 1408, 2048], P('expert', 'shard')
Inputs may be any that keep to these rules, and one draw needn't show every extreme that they name: `routes`: A row names 4 different experts; in every aligned block of 160 rows (the rows of one device) no expert is named by more than 100 rows, and one is named by exactly 100 in some block. `seq_lengths`: row d holds the lengths of device block d's sequences in order: they sum to 160, positive ones first and zeros after; in every draw some device holds a single sequence of 160.
All inputs are finite; a program needn't handle non-finite values.
Results may differ from a plain program's by a relative error of at most 0.025.
Values may be sent and summed in bfloat16 or wider, within the bound.
No kernel may reach another device: no remote copies, remote signals or barrier semaphores. Data moves between devices by JAX's collectives and lax.ppermute only.
A program may use at most 256 MiB of HBM per device.

v0:
```python
import jax
import jax.numpy as jnp
from jax import lax
from jax.sharding import PartitionSpec as P

HD = 128
TOP = 4
SLOTS = 8


epsilon = 1e-06
rope_base = 1000000.0


def rotate_half(values_in):
    half_size = values_in.shape[-1] // 2
    return jnp.concatenate([-values_in[..., half_size:], values_in[..., :half_size]], axis=-1)


def rope_tables(positions, head_size):
    exponent = jnp.arange(0, head_size, 2, dtype=jnp.float32) / head_size
    frequency = rope_base ** (-exponent)
    angles = positions.astype(jnp.float32)[:, None] * frequency[None, :]
    angles = jnp.concatenate([angles, angles], axis=-1)
    return (jnp.cos(angles)[:, None, :], jnp.sin(angles)[:, None, :])


def seq_layout(lengths, length_total):
    seq_ends = jnp.cumsum(lengths)
    starts = seq_ends - lengths
    places = jnp.arange(length_total, dtype=jnp.int32)
    member = (places[:, None] >= starts[None, :]) & (places[:, None] < seq_ends[None, :])
    seq_id = jnp.sum((places[:, None] >= seq_ends[None, :]).astype(jnp.int32), axis=1)
    offset = jnp.sum(jnp.where(member, starts[None, :], 0), axis=1)
    return (seq_id, places - offset)


def silu_slope(values_in):
    logistic = jax.nn.sigmoid(values_in)
    return logistic * (1.0 + values_in * (1.0 - logistic))


def norm_back(grad_normed, values_in, inverse, gain_wide, upstream_rows):
    normed = grad_normed * gain_wide
    return (
        upstream_rows
        + inverse * normed
        - values_in * inverse**3 * jnp.mean(normed * values_in, axis=1, keepdims=True)
    )


def local(
    tokens,
    norm_attn,
    w_query,
    b_query,
    w_key,
    b_key,
    w_value,
    b_value,
    w_output,
    norm_ffn,
    w_router,
    shared_mix,
    shared_gate,
    shared_up,
    shared_down,
    expert_gate,
    expert_up,
    expert_down,
    routes,
    seq_lengths,
    cotangent,
):
    group_rows, model_width = tokens.shape
    blocks_here = seq_lengths.shape[0]
    row_total = group_rows // blocks_here
    experts = w_router.shape[1]
    capacity = row_total * TOP * 5 // (4 * experts)
    slot_rows = experts * capacity
    assigned = row_total * TOP
    scale = HD ** (-0.5)
    own_start = lax.axis_index("shard") * row_total
    query_w, key_w, value_w, output_w, shared_gate_w, shared_up_w, shared_down_w = (
        lax.all_gather(w_query, "expert", axis=0, tiled=True),
        lax.all_gather(w_key, "expert", axis=0, tiled=True),
        lax.all_gather(w_value, "expert", axis=0, tiled=True),
        lax.all_gather(w_output, "expert", axis=1, tiled=True),
        lax.all_gather(shared_gate, "expert", axis=0, tiled=True),
        lax.all_gather(shared_up, "expert", axis=0, tiled=True),
        lax.all_gather(shared_down, "expert", axis=1, tiled=True),
    )
    full_gate, full_up, full_down = (
        lax.all_gather(expert_gate, "shard", axis=2, tiled=True),
        lax.all_gather(expert_up, "shard", axis=2, tiled=True),
        lax.all_gather(expert_down, "shard", axis=1, tiled=True),
    )
    gate_w, up_w, down_w = (full_gate[0], full_up[0], full_down[0])
    width_here = query_w.shape[1]
    heads_here = width_here // HD
    head_start = lax.axis_index("shard") * width_here
    total_width = b_query.shape[0]

    def own_rows(values_in):
        return lax.dynamic_slice_in_dim(values_in, own_start, row_total, 0)

    def head_part(vector):
        return lax.dynamic_slice_in_dim(vector.astype(jnp.float32), head_start, width_here, 0)

    def head_place(vector):
        return lax.dynamic_update_slice_in_dim(
            jnp.zeros((total_width,), jnp.float32), vector, head_start, 0
        )

    seq_id, positions = jax.vmap(lambda lengths: seq_layout(lengths, row_total))(seq_lengths)
    seq_id = (seq_id + jnp.arange(blocks_here, dtype=jnp.int32)[:, None] * SLOTS).reshape(-1)
    positions = positions.reshape(-1)
    cosine, sine = rope_tables(positions, HD)
    allowed = (seq_id[:, None] == seq_id[None, :]) & (positions[None, :] <= positions[:, None])
    resid_all = tokens.astype(jnp.float32)
    gain_one = norm_attn.astype(jnp.float32)
    inv_one_all = lax.rsqrt(jnp.mean(resid_all * resid_all, axis=1, keepdims=True) + epsilon)
    h_one = (resid_all * inv_one_all * gain_one).astype(jnp.bfloat16)
    query_pre = jnp.dot(h_one, query_w, preferred_element_type=jnp.float32) + head_part(b_query)
    key_pre = jnp.dot(h_one, key_w, preferred_element_type=jnp.float32) + head_part(b_key)
    value_pre = jnp.dot(h_one, value_w, preferred_element_type=jnp.float32) + head_part(b_value)
    query_pre = query_pre.reshape(group_rows, heads_here, HD)
    key_pre = key_pre.reshape(group_rows, heads_here, HD)
    query_rot = (query_pre * cosine + rotate_half(query_pre) * sine).astype(jnp.bfloat16)
    key_rot = (key_pre * cosine + rotate_half(key_pre) * sine).astype(jnp.bfloat16)
    value_low = value_pre.astype(jnp.bfloat16).reshape(group_rows, heads_here, HD)
    raw_scores = (
        jnp.einsum("qhd,khd->hqk", query_rot, key_rot, preferred_element_type=jnp.float32) * scale
    )
    masked = jnp.where(allowed[None], raw_scores, -1e30)
    row_top = jnp.max(masked, axis=-1, keepdims=True)
    log_total = row_top + jnp.log(jnp.sum(jnp.exp(masked - row_top), axis=-1, keepdims=True))
    probs_low = jnp.exp(masked - log_total).astype(jnp.bfloat16)
    attended = jnp.einsum("hqk,khd->qhd", probs_low, value_low, preferred_element_type=jnp.float32)
    attended_low = attended.reshape(group_rows, width_here).astype(jnp.bfloat16)
    attn_out = lax.psum(
        jnp.dot(attended_low, output_w, preferred_element_type=jnp.float32), "shard"
    )
    x_two_all = resid_all + attn_out
    gain_two = norm_ffn.astype(jnp.float32)
    inv_two_all = lax.rsqrt(jnp.mean(x_two_all * x_two_all, axis=1, keepdims=True) + epsilon)
    h_two_all = (x_two_all * inv_two_all * gain_two).astype(jnp.bfloat16)
    gate_shared = jnp.dot(h_two_all, shared_gate_w, preferred_element_type=jnp.float32)
    up_shared = jnp.dot(h_two_all, shared_up_w, preferred_element_type=jnp.float32)
    hidden_shared = (jax.nn.silu(gate_shared) * up_shared).astype(jnp.bfloat16)
    out_shared = lax.psum_scatter(
        jnp.dot(hidden_shared, shared_down_w, preferred_element_type=jnp.float32),
        "shard",
        scatter_dimension=0,
        tiled=True,
    )
    mix_all = jax.nn.sigmoid(jnp.dot(h_two_all, shared_mix, preferred_element_type=jnp.float32))
    x_two = own_rows(x_two_all)
    h_two = own_rows(h_two_all)
    inv_two = own_rows(inv_two_all)
    mix_gate = own_rows(mix_all)
    router_probs = jax.nn.softmax(
        jnp.dot(h_two, w_router, preferred_element_type=jnp.float32), axis=-1
    )
    choose = (routes[:, :, None] == jnp.arange(experts, dtype=jnp.int32)[None, None, :]).astype(
        jnp.float32
    )
    gates = jnp.sum(choose * router_probs[:, None, :], axis=-1)
    flat_routes = routes.reshape(-1)
    hits = (flat_routes[:, None] == jnp.arange(experts, dtype=jnp.int32)[None, :]).astype(jnp.int32)
    slots = jnp.sum((jnp.cumsum(hits, axis=0) - 1) * hits, axis=1)
    place_at = flat_routes * capacity + slots
    table = (
        jnp.full((slot_rows,), assigned, jnp.int32)
        .at[place_at]
        .set(jnp.arange(assigned, dtype=jnp.int32))
    )
    h_padded = jnp.concatenate([h_two, jnp.zeros((1, model_width), jnp.bfloat16)], axis=0)
    send_rows = h_padded[table // TOP].reshape(experts, capacity, model_width)
    rows_in = lax.all_to_all(send_rows, "expert", split_axis=0, concat_axis=0, tiled=True).reshape(
        slot_rows, model_width
    )
    gate_e = jnp.dot(rows_in, gate_w, preferred_element_type=jnp.float32)
    up_e = jnp.dot(rows_in, up_w, preferred_element_type=jnp.float32)
    hidden_e = (jax.nn.silu(gate_e) * up_e).astype(jnp.bfloat16)
    out_rows = jnp.dot(hidden_e, down_w, preferred_element_type=jnp.float32).astype(jnp.bfloat16)
    returned = lax.all_to_all(
        out_rows.reshape(experts, capacity, model_width),
        "expert",
        split_axis=0,
        concat_axis=0,
        tiled=True,
    )
    picked = returned.reshape(slot_rows, model_width)[place_at].reshape(row_total, TOP, model_width)
    routed = jnp.einsum("tk,tkd->td", gates, picked.astype(jnp.float32))
    block_out = (x_two + routed + mix_gate[:, None] * out_shared).astype(jnp.bfloat16)
    upstream_all = cotangent.astype(jnp.float32)
    upstream = own_rows(upstream_all)
    grad_pick = (gates[:, :, None] * upstream[:, None, :]).astype(jnp.bfloat16)
    grad_gates = jnp.einsum("td,tkd->tk", upstream, picked.astype(jnp.float32))
    grad_probs = jnp.sum(choose * grad_gates[:, :, None], axis=1)
    grad_logit = router_probs * (
        grad_probs - jnp.sum(router_probs * grad_probs, axis=1, keepdims=True)
    )
    h_two_wide = h_two.astype(jnp.float32)
    grad_router = jnp.dot(h_two_wide.T, grad_logit, precision=lax.Precision.HIGHEST)
    grad_mix = jnp.sum(upstream * out_shared, axis=1) * mix_gate * (1.0 - mix_gate)
    grad_mix_w = jnp.dot(grad_mix, h_two_wide, precision=lax.Precision.HIGHEST)
    grad_shared_out = (mix_all[:, None] * upstream_all).astype(jnp.bfloat16)
    grad_hidden_shared = jnp.dot(
        grad_shared_out, shared_down_w.T, preferred_element_type=jnp.float32
    )
    grad_gate_shared = (grad_hidden_shared * up_shared * silu_slope(gate_shared)).astype(
        jnp.bfloat16
    )
    grad_up_shared = (grad_hidden_shared * jax.nn.silu(gate_shared)).astype(jnp.bfloat16)
    grad_shared_down = jnp.dot(hidden_shared.T, grad_shared_out, preferred_element_type=jnp.float32)
    grad_shared_gate = jnp.dot(h_two_all.T, grad_gate_shared, preferred_element_type=jnp.float32)
    grad_shared_up = jnp.dot(h_two_all.T, grad_up_shared, preferred_element_type=jnp.float32)
    grad_padded = jnp.concatenate(
        [grad_pick.reshape(assigned, model_width), jnp.zeros((1, model_width), jnp.bfloat16)],
        axis=0,
    )
    grad_send = grad_padded[table].reshape(experts, capacity, model_width)
    grad_rows_in = lax.all_to_all(
        grad_send, "expert", split_axis=0, concat_axis=0, tiled=True
    ).reshape(slot_rows, model_width)
    grad_hidden_e = jnp.dot(grad_rows_in, down_w.T, preferred_element_type=jnp.float32)
    grad_gate_e = (grad_hidden_e * up_e * silu_slope(gate_e)).astype(jnp.bfloat16)
    grad_up_e = (grad_hidden_e * jax.nn.silu(gate_e)).astype(jnp.bfloat16)
    term_down = jnp.dot(hidden_e.T, grad_rows_in, preferred_element_type=jnp.float32)
    term_gate = jnp.dot(rows_in.T, grad_gate_e, preferred_element_type=jnp.float32)
    term_up = jnp.dot(rows_in.T, grad_up_e, preferred_element_type=jnp.float32)
    grad_inputs = jnp.dot(grad_gate_e, gate_w.T, preferred_element_type=jnp.float32) + jnp.dot(
        grad_up_e, up_w.T, preferred_element_type=jnp.float32
    )
    grad_back = lax.all_to_all(
        grad_inputs.astype(jnp.bfloat16).reshape(experts, capacity, model_width),
        "expert",
        split_axis=0,
        concat_axis=0,
        tiled=True,
    )
    grad_expert_gate, grad_expert_up, grad_expert_down = (
        lax.psum_scatter(
            term_gate[None].astype(jnp.bfloat16), "shard", scatter_dimension=2, tiled=True
        ).astype(jnp.float32),
        lax.psum_scatter(
            term_up[None].astype(jnp.bfloat16), "shard", scatter_dimension=2, tiled=True
        ).astype(jnp.float32),
        lax.psum_scatter(
            term_down[None].astype(jnp.bfloat16), "shard", scatter_dimension=1, tiled=True
        ).astype(jnp.float32),
    )
    grad_taken = grad_back.reshape(slot_rows, model_width)[place_at].reshape(
        row_total, TOP, model_width
    )
    own_extra = (
        jnp.sum(grad_taken.astype(jnp.float32), axis=1)
        + grad_mix[:, None] * shared_mix.astype(jnp.float32)[None, :]
        + jnp.dot(grad_logit, w_router.astype(jnp.float32).T, precision=lax.Precision.HIGHEST)
    )
    placed = lax.dynamic_update_slice_in_dim(
        jnp.zeros((group_rows, model_width), jnp.float32), own_extra, own_start, 0
    )
    grad_h_two_all = lax.psum(
        jnp.dot(grad_gate_shared, shared_gate_w.T, preferred_element_type=jnp.float32)
        + jnp.dot(grad_up_shared, shared_up_w.T, preferred_element_type=jnp.float32)
        + placed,
        "shard",
    )
    grad_x_two_all = norm_back(grad_h_two_all, x_two_all, inv_two_all, gain_two, upstream_all)
    grad_attn = grad_x_two_all.astype(jnp.bfloat16)
    grad_h_two = own_rows(grad_h_two_all)
    grad_x_two = own_rows(grad_x_two_all)
    grad_norm_ffn = jnp.sum(grad_h_two * x_two * inv_two, axis=0)
    grad_output_w = jnp.dot(attended_low.T, grad_attn, preferred_element_type=jnp.float32)
    grad_attended = jnp.dot(grad_attn, output_w.T, preferred_element_type=jnp.float32).astype(
        jnp.bfloat16
    )
    grad_attended = grad_attended.reshape(group_rows, heads_here, HD)
    raw_again = (
        jnp.einsum("qhd,khd->hqk", query_rot, key_rot, preferred_element_type=jnp.float32) * scale
    )
    probs = jnp.exp(jnp.where(allowed[None], raw_again, -1e30) - log_total)
    grad_probs_attn = jnp.einsum(
        "qhd,khd->hqk", grad_attended, value_low, preferred_element_type=jnp.float32
    )
    grad_value = jnp.einsum(
        "hqk,qhd->khd", probs_low, grad_attended, preferred_element_type=jnp.float32
    ).astype(jnp.bfloat16)
    row_delta = jnp.sum(probs * grad_probs_attn, axis=-1, keepdims=True)
    grad_scores = (probs * (grad_probs_attn - row_delta) * scale).astype(jnp.bfloat16)
    grad_query = jnp.einsum(
        "hqk,khd->qhd", grad_scores, key_rot, preferred_element_type=jnp.float32
    )
    grad_key = jnp.einsum(
        "hqk,qhd->khd", grad_scores, query_rot, preferred_element_type=jnp.float32
    )
    grad_query_pre = (
        (grad_query * cosine - rotate_half(grad_query * sine))
        .reshape(group_rows, width_here)
        .astype(jnp.bfloat16)
    )
    grad_key_pre = (
        (grad_key * cosine - rotate_half(grad_key * sine))
        .reshape(group_rows, width_here)
        .astype(jnp.bfloat16)
    )
    grad_value_pre = grad_value.reshape(group_rows, width_here)
    grad_query_w = jnp.dot(h_one.T, grad_query_pre, preferred_element_type=jnp.float32)
    grad_key_w = jnp.dot(h_one.T, grad_key_pre, preferred_element_type=jnp.float32)
    grad_value_w = jnp.dot(h_one.T, grad_value_pre, preferred_element_type=jnp.float32)
    grad_query_b = head_place(jnp.sum(grad_query_pre.astype(jnp.float32), axis=0))
    grad_key_b = head_place(jnp.sum(grad_key_pre.astype(jnp.float32), axis=0))
    grad_value_b = head_place(jnp.sum(grad_value_pre.astype(jnp.float32), axis=0))
    grad_h_one = lax.psum_scatter(
        (
            jnp.dot(grad_query_pre, query_w.T, preferred_element_type=jnp.float32)
            + jnp.dot(grad_key_pre, key_w.T, preferred_element_type=jnp.float32)
            + jnp.dot(grad_value_pre, value_w.T, preferred_element_type=jnp.float32)
        ).astype(jnp.bfloat16),
        "shard",
        scatter_dimension=0,
        tiled=True,
    ).astype(jnp.float32)
    resid_in = own_rows(resid_all)
    inv_one = own_rows(inv_one_all)
    grad_norm_attn = jnp.sum(grad_h_one * resid_in * inv_one, axis=0)
    grad_tokens = norm_back(grad_h_one, resid_in, inv_one, gain_one, grad_x_two)
    small = lax.psum(
        (
            grad_norm_attn,
            grad_query_b,
            grad_key_b,
            grad_value_b,
            grad_norm_ffn,
            grad_router,
            grad_mix_w,
        ),
        ("expert", "shard"),
    )
    weight = (
        lax.psum_scatter(
            grad_query_w.astype(jnp.bfloat16), "expert", scatter_dimension=0, tiled=True
        ).astype(jnp.float32),
        lax.psum_scatter(
            grad_key_w.astype(jnp.bfloat16), "expert", scatter_dimension=0, tiled=True
        ).astype(jnp.float32),
        lax.psum_scatter(
            grad_value_w.astype(jnp.bfloat16), "expert", scatter_dimension=0, tiled=True
        ).astype(jnp.float32),
        lax.psum_scatter(
            grad_output_w.astype(jnp.bfloat16), "expert", scatter_dimension=1, tiled=True
        ).astype(jnp.float32),
        lax.psum_scatter(
            grad_shared_gate.astype(jnp.bfloat16), "expert", scatter_dimension=0, tiled=True
        ).astype(jnp.float32),
        lax.psum_scatter(
            grad_shared_up.astype(jnp.bfloat16), "expert", scatter_dimension=0, tiled=True
        ).astype(jnp.float32),
        lax.psum_scatter(
            grad_shared_down.astype(jnp.bfloat16), "expert", scatter_dimension=1, tiled=True
        ).astype(jnp.float32),
    )
    return (
        block_out,
        grad_tokens,
        small[0],
        weight[0],
        small[1],
        weight[1],
        small[2],
        weight[2],
        small[3],
        weight[3],
        small[4],
        small[5],
        small[6],
        weight[4],
        weight[5],
        weight[6],
        grad_expert_gate,
        grad_expert_up,
        grad_expert_down,
    )


def solution(mesh):
    return jax.shard_map(
        local,
        mesh=mesh,
        in_specs=(
            P("expert", None),
            P(),
            P("expert", "shard"),
            P(),
            P("expert", "shard"),
            P(),
            P("expert", "shard"),
            P(),
            P("shard", "expert"),
            P(),
            P(),
            P(),
            P("expert", "shard"),
            P("expert", "shard"),
            P("shard", "expert"),
            P("expert", None, "shard"),
            P("expert", None, "shard"),
            P("expert", "shard", None),
            P(("expert", "shard"), None),
            P("expert", None),
            P("expert", None),
        ),
        out_specs=(
            P(("expert", "shard"), None),
            P(("expert", "shard"), None),
            P(),
            P("expert", "shard"),
            P(),
            P("expert", "shard"),
            P(),
            P("expert", "shard"),
            P(),
            P("shard", "expert"),
            P(),
            P(),
            P(),
            P("expert", "shard"),
            P("expert", "shard"),
            P("shard", "expert"),
            P("expert", None, "shard"),
            P("expert", None, "shard"),
            P("expert", "shard", None),
        ),
        check_vma=False,
    )
```

profile of v0, /device:TPU:0, one launch (start us, length us, event | category | flops | bytes accessed | tf_op | source)
XLA Modules:
  0.0 2217.0 jit_solution(9978965272790675673)
XLA Ops:
  18.4 43.8 %all-gather.15.cloned.1.call-done = bf16[2048,512]{1,0:T(8,128)(2,1)} async-done(((bf16[256,512]{1,0:T(8,128)(2,1)}), bf16[2048,512]{1,0:T(8,128)(2,1)}) %all-gather.15.cloned.1.call-update) | async-done | bytes 2097168 | tf_op jit(solution)/shard_map/all_gather | solution.py:86
  67.9 44.2 %all-gather.13.cloned.1.call-done = bf16[2048,512]{1,0:T(8,128)(2,1)} async-done(((bf16[256,512]{1,0:T(8,128)(2,1)}), bf16[2048,512]{1,0:T(8,128)(2,1)}) %all-gather.13.cloned.1.call-update) | async-done | bytes 2097168 | tf_op jit(solution)/shard_map/all_gather | solution.py:85
  121.7 40.4 %all-gather.11.cloned.1.call-done = bf16[2048,512]{1,0:T(8,128)(2,1)} async-done(((bf16[256,512]{1,0:T(8,128)(2,1)}), bf16[2048,512]{1,0:T(8,128)(2,1)}) %all-gather.11.cloned.1.call-update) | async-done | bytes 2097168 | tf_op jit(solution)/shard_map/all_gather | solution.py:87
  169.5 44.1 %all-gather.17.cloned.1.call-done = bf16[512,2048]{1,0:T(8,128)(2,1)} async-done(((bf16[512,256]{1,0:T(8,128)(2,1)}), bf16[512,2048]{1,0:T(8,128)(2,1)}) %all-gather.17.cloned.1.call-update) | async-done | bytes 2097168 | tf_op jit(solution)/shard_map/all_gather | solution.py:88
  213.6 6.0 fusion.109
  230.5 90.0 %all-reduce.7.cloned.1.call-done = f32[640,2048]{1,0:T(8,128)} async-done(((f32[640,2048]{1,0:T(8,128)}), f32[640,2048]{1,0:T(8,128)}) %all-reduce.7.cloned.1.call-update) | async-done | bytes 5242896 | tf_op jit(solution)/shard_map/psum | solution.py:141
  327.6 4.9 gather_fusion
  337.0 5.6 all-to-all-start
  345.3 133.1 %all-gather.25.cloned.1.call-done = bf16[2048,1408]{1,0:T(8,128)(2,1)} async-done(((bf16[256,1408]{1,0:T(8,128)(2,1)}), bf16[2048,1408]{1,0:T(8,128)(2,1)}) %all-gather.25.cloned.1.call-update) | async-done | bytes 5767184 | tf_op jit(solution)/shard_map/all_gather | solution.py:89
  478.4 9.4 fusion.111
  487.8 83.4 %all-gather.27.cloned.1.call-done = bf16[2048,1408]{1,0:T(8,128)(2,1)} async-done(((bf16[256,1408]{1,0:T(8,128)(2,1)}), bf16[2048,1408]{1,0:T(8,128)(2,1)}) %all-gather.27.cloned.1.call-update) | async-done | bytes 5767184 | tf_op jit(solution)/shard_map/all_gather | solution.py:90
  571.2 9.5 fusion.112
  580.7 84.4 %all-gather.29.cloned.1.call-done = bf16[1408,2048]{1,0:T(8,128)(2,1)} async-done(((bf16[1408,256]{1,0:T(8,128)(2,1)}), bf16[1408,2048]{1,0:T(8,128)(2,1)}) %all-gather.29.cloned.1.call-update) | async-done | bytes 5767184 | tf_op jit(solution)/shard_map/all_gather | solution.py:91
  665.0 12.8 multiply_convert_fusion.8
  677.9 6.2 fusion.113
  688.7 19.5 all-gather.19.cloned.1.call-done
  708.2 10.0 fusion.15
  718.3 34.8 %all-gather.21.cloned.1.call-done = bf16[1,2048,1408]{1,2,0:T(8,128)(2,1)} async-done(((bf16[1,2048,352]{1,2,0:T(8,128)(2,1)}), bf16[1,2048,1408]{1,2,0:T(8,128)(2,1)}) %all-gather.21.cloned.1.call-update) | async-done | bytes 5767184 | tf_op jit(solution)/shard_map/all_gather | solution.py:95
  753.1 11.2 multiply_convert_fusion.7
  764.3 33.8 %all-gather.23.cloned.1.call-done = bf16[1,1408,2048]{2,1,0:T(8,128)(2,1)} async-done(((bf16[1,352,2048]{2,1,0:T(8,128)(2,1)}), bf16[1,1408,2048]{2,1,0:T(8,128)(2,1)}) %all-gather.23.cloned.1.call-update) | async-done | bytes 5767184 | tf_op jit(solution)/shard_map/all_gather | solution.py:96
  798.1 9.6 fusion.29
  807.7 4.9 reshape.414
  812.6 5.8 all-to-all-start.1
  825.5 69.7 %all-to-all-done.1 = bf16[8,100,2048]{2,1,0:T(8,128)(2,1)} async-done(((bf16[8,100,2048]{2,1,0:T(8,128)(2,1)}), bf16[8,100,2048]{2,1,0:T(8,128)(2,1)}, u32[]{:S(2)}, u32[]{:S(2)}) %all-to-all-start.1) | async-done | bytes 3276832 | tf_op jit(solution)/shard_map/all_to_all | solution.py:187
  915.7 7.3 mul.414
  926.0 4.8 gather_fusion.2
  933.8 80.3 %all_to_all.20 = bf16[8,100,2048]{2,1,0:T(8,128)(2,1)} all-to-all(bf16[8,100,2048]{2,1,0:T(8,128)(2,1)S(1)} %reshape.417), channel_id=1, replica_groups=mesh['expert'=8,'shard'=4] {'expert'}, dimensions={0} | all-to-all | bytes 6553600 | tf_op jit(solution)/shard_map/all_to_all | solution.py:225
  1017.0 11.7 multiply_convert_fusion.6
  1028.7 8.9 fusion.9
  1037.7 8.2 add_convert_fusion
  1053.2 7.6 fusion.114
  1060.8 6.1 convolution_add_fusion
  1067.5 60.9 %all-to-all-done.3 = bf16[8,100,2048]{2,1,0:T(8,128)(2,1)} async-done(((bf16[8,100,2048]{2,1,0:T(8,128)(2,1)}), bf16[8,100,2048]{2,1,0:T(8,128)(2,1)}, u32[]{:S(2)}, u32[]{:S(2)}) %all-to-all-start.3) | async-done | bytes 3276832 | tf_op jit(solution)/shard_map/all_to_all | solution.py:237
  1135.4 5.8 reshape.423
  1141.3 5.8 reduce_sum.197
  1152.1 8.3 convolution_convert_fusion.2
  1160.5 8.6 convolution_convert_fusion.1
  1170.9 8.2 convolution_convert_fusion
  1179.2 10.6 fusion.2
  1189.8 28.1 %copy.116 = bf16[1,2048,1408]{1,0,2:T(2,128)(2,1)} copy(bf16[1,2048,1408]{2,1,0:T(8,128)(2,1)} %fusion.2) | data formatting | bytes 11534336
  1217.8 10.5 copy.128
  1228.4 10.9 fusion.3
  1239.3 28.0 %copy.118 = bf16[1,2048,1408]{1,0,2:T(2,128)(2,1)} copy(bf16[1,2048,1408]{2,1,0:T(8,128)(2,1)} %fusion.3) | data formatting | bytes 11534336
  1267.3 10.5 copy.127
  1277.9 10.2 fusion.4
  1288.8 5.0 multiply_reduce_fusion.1
  1304.8 14.5 fusion.54
  1319.3 15.0 broadcast_multiply_fusion
  1347.0 5.2 convert_reduce_fusion
  1356.6 5.6 convolution_convert_fusion.6
  1381.8 97.3 %reduce-scatter.31.cloned.1.call-done = bf16[256,1408]{1,0:T(8,128)(2,1)} async-done(((bf16[2048,1408]{1,0:T(8,128)(2,1)}), bf16[256,1408]{1,0:T(8,128)(2,1)}) %reduce-scatter.31.cloned.1.call-update) | async-done | bytes 720912 | tf_op jit(solution)/shard_map/reduce_scatter | solution.py:359
  1481.4 111.9 %reduce-scatter.33.cloned.1.call-done = bf16[1408,256]{1,0:T(8,128)(2,1)} async-done(((bf16[1408,2048]{1,0:T(8,128)(2,1)}), bf16[1408,256]{1,0:T(8,128)(2,1)}) %reduce-scatter.33.cloned.1.call-update) | async-done | bytes 720912 | tf_op jit(solution)/shard_map/reduce_scatter | solution.py:362
  1599.6 50.9 %reduce-scatter.37.cloned.1.call-done = bf16[352,2048]{1,0:T(8,128)(2,1)} async-done(((bf16[1408,2048]{1,0:T(8,128)(2,1)}), bf16[352,2048]{1,0:T(8,128)(2,1)}) %reduce-scatter.37.cloned.1.call-update) | async-done | bytes 1441808
  1653.6 5.6 copy.117
  1662.5 45.3 %reduce-scatter.39.cloned.1.call-done = bf16[352,2048]{1,0:T(8,128)(2,1)} async-done(((bf16[1408,2048]{1,0:T(8,128)(2,1)}), bf16[352,2048]{1,0:T(8,128)(2,1)}) %reduce-scatter.39.cloned.1.call-update) | async-done | bytes 1441808
  1710.9 5.6 copy.119
  1720.0 45.5 %reduce-scatter.35.cloned.1.call-done = bf16[1,352,2048]{2,1,0:T(8,128)(2,1)} async-done(((bf16[1,1408,2048]{2,1,0:T(8,128)(2,1)}), bf16[1,352,2048]{2,1,0:T(8,128)(2,1)}) %reduce-scatter.35.cloned.1.call-update) | async-done | bytes 1441808 | tf_op jit(solution)/shard_map/reduce_scatter | solution.py:251
  1768.7 67.8 %reduce-scatter.21.cloned.1.call-done = bf16[256,512]{1,0:T(8,128)(2,1)} async-done(((bf16[2048,512]{1,0:T(8,128)(2,1)}), bf16[256,512]{1,0:T(8,128)(2,1)}) %reduce-scatter.21.cloned.1.call-update) | async-done | bytes 262160 | tf_op jit(solution)/shard_map/reduce_scatter | solution.py:344
  1838.3 68.4 %reduce-scatter.23.cloned.1.call-done = bf16[256,512]{1,0:T(8,128)(2,1)} async-done(((bf16[2048,512]{1,0:T(8,128)(2,1)}), bf16[256,512]{1,0:T(8,128)(2,1)}) %reduce-scatter.23.cloned.1.call-update) | async-done | bytes 262160 | tf_op jit(solution)/shard_map/reduce_scatter | solution.py:347
  1908.5 68.5 %reduce-scatter.25.cloned.1.call-done = bf16[256,512]{1,0:T(8,128)(2,1)} async-done(((bf16[2048,512]{1,0:T(8,128)(2,1)}), bf16[256,512]{1,0:T(8,128)(2,1)}) %reduce-scatter.25.cloned.1.call-update) | async-done | bytes 262160 | tf_op jit(solution)/shard_map/reduce_scatter | solution.py:350
  1978.9 68.9 %reduce-scatter.27.cloned.1.call-done = bf16[512,256]{1,0:T(8,128)(2,1)} async-done(((bf16[512,2048]{1,0:T(8,128)(2,1)}), bf16[512,256]{1,0:T(8,128)(2,1)}) %reduce-scatter.27.cloned.1.call-update) | async-done | bytes 262160 | tf_op jit(solution)/shard_map/reduce_scatter | solution.py:353
  2049.5 34.3 %reduce-scatter.19.cloned.1.call-done = bf16[160,2048]{1,0:T(8,128)(2,1)} async-done(((bf16[640,2048]{1,0:T(8,128)(2,1)}), bf16[160,2048]{1,0:T(8,128)(2,1)}) %reduce-scatter.19.cloned.1.call-update) | async-done | bytes 655376 | tf_op jit(solution)/shard_map/reduce_scatter | solution.py:317
  2089.1 40.6 %all-reduce.2 = (f32[2048]{0:T(1024)}, f32[2048]{0:T(1024)}, f32[2048]{0:T(1024)}, f32[2048]{0:T(1024)}, f32[2048]{0:T(1024)}, /*index=5*/f32[2048]{0:T(1024)}) all-reduce(f32[2048]{0:T(1024)S(1)} %get-tuple-element.95, f32[2048]{0:T(1024)S(1)} %bitcast_dynamic-update-slice_fusion.2, ...), channel_id=1, replica_groups=mesh['expert'=8,'shard'=4] {'expert','shard'}, use_global_device_ids=true, to_apply=%region_26.27 | all-reduce | flops 12288 | bytes 98304 | tf_op jit(solution)/shard_map/psum | solution.py:331
  2129.8 78.8 %all-reduce.11.cloned.1.call-done = f32[2048,8]{0,1:T(8,128)} async-done(((f32[2048,8]{0,1:T(8,128)}), f32[2048,8]{0,1:T(8,128)}) %all-reduce.11.cloned.1.call-update) | async-done | bytes 65552 | tf_op jit(solution)/shard_map/psum | solution.py:331
  (326 shorter events, 207.9 us)
Async XLA Ops:
  7.2 817.9 %copy-start = (bf16[2048,8]{0,1:T(8,128)(2,1)S(1)}, bf16[2048,8]{0,1:T(8,128)(2,1)}, u32[]{:S(2)}) copy-start(bf16[2048,8]{0,1:T(8,128)(2,1)} %param.31) | copy-start | bytes 98308
  7.2 55.0 %copy-start.5 = (bf16[640,2048]{1,0:T(8,128)(2,1)S(1)}, bf16[640,2048]{1,0:T(8,128)(2,1)}, u32[]{:S(2)}) copy-start(bf16[640,2048]{1,0:T(8,128)(2,1)} %param.21) | copy-start | bytes 7864324
  7.2 5.9 copy-start.59
  7.2 55.0 %all-gather.15.cloned.1.call-start = ((), (), s32[]{:S(2)}) async-start(), calls=%async_computation.18 | async-start | bytes 2359296 | tf_op jit(solution)/shard_map/all_gather | solution.py:86
  8.0 104.2 %all-gather.13.cloned.1.call-start = ((), (), s32[]{:S(2)}) async-start(), calls=%async_computation.17 | async-start | bytes 2359296 | tf_op jit(solution)/shard_map/all_gather | solution.py:85
  8.7 153.4 %all-gather.11.cloned.1.call-start = ((), (), s32[]{:S(2)}) async-start(), calls=%async_computation.16 | async-start | bytes 2359296 | tf_op jit(solution)/shard_map/all_gather | solution.py:87
  9.4 204.1 %all-gather.17.cloned.1.call-start = ((), (), s32[]{:S(2)}) async-start(), calls=%async_computation.19 | async-start | bytes 2359296 | tf_op jit(solution)/shard_map/all_gather | solution.py:88
  10.0 310.5 %all-reduce.7.cloned.1.call-start = ((), (), s32[]{:S(2)}) async-start(), calls=%async_computation.20 | async-start | bytes 10485760 | tf_op jit(solution)/shard_map/psum | solution.py:141
  10.8 151.3 %copy-start.47 = (f32[2048]{0:T(1024)}, f32[2048]{0:T(1024)S(1)}, u32[]{:S(2)}) copy-start(f32[2048]{0:T(1024)S(1)} %convert_element_type.228) | copy-start | bytes 24580
  13.1 148.9 %copy-start.60 = (f32[640]{0:T(1024)}, f32[640]{0:T(1024)S(1)}, u32[]{:S(2)}) copy-start(f32[640]{0:T(1024)S(1)} %add_rsqrt_fusion.1) | copy-start | bytes 7684
  14.1 151.7 %copy-start.16 = (pred[640,640]{0,1:T(8,128)(4,1)}, pred[640,640]{0,1:T(8,128)(4,1)S(1)}, u32[]{:S(2)}) copy-start(pred[640,640]{0,1:T(8,128)(4,1)S(1)} %compare_and_fusion) | copy-start | bytes 1228804
  17.7 98.2 %copy-start.21 = (f32[640,128]{0,1:T(8,128)}, f32[640,128]{0,1:T(8,128)S(1)}, u32[]{:S(2)}) copy-start(f32[640,128]{0,1:T(8,128)S(1)} %get-tuple-element.138) | copy-start | bytes 983044
  121.7 44.1 %copy-start.57 = (f32[4,640]{1,0:T(4,128)}, f32[4,640]{1,0:T(4,128)S(1)}, u32[]{:S(2)}) copy-start(f32[4,640]{1,0:T(4,128)S(1)} %log_add_fusion) | copy-start | bytes 30724
  162.1 4.5 copy-start.4
  219.6 4.2 copy-start.51
  219.6 4.5 copy-start.62
  219.6 258.8 %all-gather.25.cloned.1.call-start = ((), (), s32[]{:S(2)}) async-start(), calls=%async_computation.24 | async-start | bytes 6488064 | tf_op jit(solution)/shard_map/all_gather | solution.py:89
  220.2 351.0 %all-gather.27.cloned.1.call-start = ((), (), s32[]{:S(2)}) async-start(), calls=%async_computation.25 | async-start | bytes 6488064 | tf_op jit(solution)/shard_map/all_gather | solution.py:90
  220.9 444.1 %all-gather.29.cloned.1.call-start = ((), (), s32[]{:S(2)}) async-start(), calls=%async_computation.26 | async-start | bytes 6488064 | tf_op jit(solution)/shard_map/all_gather | solution.py:91
  221.7 486.6 %all-gather.19.cloned.1.call-start = ((), (), s32[]{:S(2)}) async-start(), calls=%async_computation.21 | async-start | bytes 7208960 | tf_op jit(solution)/shard_map/all_gather | solution.py:94
  222.4 530.7 %all-gather.21.cloned.1.call-start = ((), (), s32[]{:S(2)}) async-start(), calls=%async_computation.22 | async-start | bytes 7208960 | tf_op jit(solution)/shard_map/all_gather | solution.py:95
  223.0 575.1 %all-gather.23.cloned.1.call-start = ((), (), s32[]{:S(2)}) async-start(), calls=%async_computation.23 | async-start | bytes 7208960 | tf_op jit(solution)/shard_map/all_gather | solution.py:96
  224.1 100.3 %copy-start.45 = (f32[2048]{0:T(1024)}, f32[2048]{0:T(1024)S(1)}, u32[]{:S(2)}) copy-start(f32[2048]{0:T(1024)S(1)} %convert_element_type.242) | copy-start | bytes 24580
  327.6 497.6 %copy-start.7 = (bf16[160,2048]{1,0:T(8,128)(2,1)}, bf16[160,2048]{1,0:T(8,128)(2,1)S(1)}, u32[]{:S(2)}) copy-start(bf16[160,2048]{1,0:T(8,128)(2,1)S(1)} %constant_dynamic-slice_fusion.1) | copy-start | bytes 1966084
  337.0 5.7 copy-start.55
  337.0 347.2 %all-to-all-start = ((bf16[8,100,2048]{2,1,0:T(8,128)(2,1)}), bf16[8,100,2048]{2,1,0:T(8,128)(2,1)}, u32[]{:S(2)}, u32[]{:S(2)}) async-start(bf16[8,100,2048]{2,1,0:T(8,128)(2,1)} %reshape.412), calls=%async_computation | async-start | bytes 6815744 | tf_op jit(solution)/shard_map/all_to_all | solution.py:180
  342.6 567.3 %reduce-scatter.17.cloned.1.call-start = ((), (), s32[]{:S(2)}) async-start(), calls=%async_computation.27 | async-start | bytes 6553600 | tf_op jit(solution)/shard_map/reduce_scatter | solution.py:151
  665.0 12.8 copy-start.64
  677.9 6.3 copy-start.66
  812.6 82.5 %all-to-all-start.1 = ((bf16[8,100,2048]{2,1,0:T(8,128)(2,1)}), bf16[8,100,2048]{2,1,0:T(8,128)(2,1)}, u32[]{:S(2)}, u32[]{:S(2)}) async-start(bf16[8,100,2048]{2,1,0:T(8,128)(2,1)} %reshape.414), calls=%async_computation.1 | async-start | bytes 6815744 | tf_op jit(solution)/shard_map/all_to_all | solution.py:187
  909.7 6.0 copy-start.52
  1017.0 11.7 copy-start.18
  1028.7 9.0 copy-start.65
  1028.7 9.0 copy-start.68
  1048.4 4.7 copy-start.56
  1048.4 12.3 slice-start
  1048.4 80.0 %all-to-all-start.3 = ((bf16[8,100,2048]{2,1,0:T(8,128)(2,1)}), bf16[8,100,2048]{2,1,0:T(8,128)(2,1)}, u32[]{:S(2)}, u32[]{:S(2)}) async-start(bf16[8,100,2048]{2,1,0:T(8,128)(2,1)} %reshape.419), calls=%async_computation.4 | async-start | bytes 6815744 | tf_op jit(solution)/shard_map/all_to_all | solution.py:237
  1053.1 235.2 %all-reduce.9.cloned.1.call-start = ((), (), s32[]{:S(2)}) async-start(), calls=%async_computation.28 | async-start | bytes 10485760 | tf_op jit(solution)/shard_map/psum | solution.py:266
  1053.1 7.6 slice-start.1
  1053.1 7.6 copy-start.67
  1150.4 229.0 %reduce-scatter.29.cloned.1.call-start = ((), (), s32[]{:S(2)}) async-start(), calls=%async_computation.35 | async-start | bytes 6488064 | tf_op jit(solution)/shard_map/reduce_scatter | solution.py:356
  1160.5 318.7 %reduce-scatter.31.cloned.1.call-start = ((), (), s32[]{:S(2)}) async-start(), calls=%async_computation.36 | async-start | bytes 6488064 | tf_op jit(solution)/shard_map/reduce_scatter | solution.py:359
  1169.2 424.1 %reduce-scatter.33.cloned.1.call-start = ((), (), s32[]{:S(2)}) async-start(), calls=%async_computation.37 | async-start | bytes 6488064 | tf_op jit(solution)/shard_map/reduce_scatter | solution.py:362
  1179.1 471.4 %reduce-scatter.37.cloned.1.call-start = ((), (), s32[]{:S(2)}) async-start(), calls=%async_computation.39 | async-start | bytes 7208960
  1228.3 479.5 %reduce-scatter.39.cloned.1.call-start = ((), (), s32[]{:S(2)}) async-start(), calls=%async_computation.40 | async-start | bytes 7208960
  1277.9 487.5 %reduce-scatter.35.cloned.1.call-start = ((), (), s32[]{:S(2)}) async-start(), calls=%async_computation.38 | async-start | bytes 7208960 | tf_op jit(solution)/shard_map/reduce_scatter | solution.py:251
  1288.1 5.7 copy-start.50
  1288.2 5.7 copy-start.54
  1288.2 548.3 %reduce-scatter.21.cloned.1.call-start = ((), (), s32[]{:S(2)}) async-start(), calls=%async_computation.30 | async-start | bytes 2359296 | tf_op jit(solution)/shard_map/reduce_scatter | solution.py:344
  1288.8 5.8 copy-start.2
  1294.6 4.0 copy-start.32
  1300.9 3.8 copy-start.44
  1300.9 3.8 copy-start.17
  1300.9 3.8 copy-start.29
  1300.9 3.8 copy-start.58
  1304.7 14.5 copy-start.27
  1304.8 14.5 copy-start.34
  1342.4 564.3 %reduce-scatter.23.cloned.1.call-start = ((), (), s32[]{:S(2)}) async-start(), calls=%async_computation.31 | async-start | bytes 2359296 | tf_op jit(solution)/shard_map/reduce_scatter | solution.py:347
  1347.0 630.1 %reduce-scatter.25.cloned.1.call-start = ((), (), s32[]{:S(2)}) async-start(), calls=%async_computation.32 | async-start | bytes 2359296 | tf_op jit(solution)/shard_map/reduce_scatter | solution.py:350
  1356.5 691.3 %reduce-scatter.27.cloned.1.call-start = ((), (), s32[]{:S(2)}) async-start(), calls=%async_computation.33 | async-start | bytes 2359296 | tf_op jit(solution)/shard_map/reduce_scatter | solution.py:353
  1362.2 721.6 %reduce-scatter.19.cloned.1.call-start = ((), (), s32[]{:S(2)}) async-start(), calls=%async_computation.29 | async-start | bytes 3276800 | tf_op jit(solution)/shard_map/reduce_scatter | solution.py:317
  1370.9 837.7 %all-reduce.11.cloned.1.call-start = ((), (), s32[]{:S(2)}) async-start(), calls=%async_computation.34 | async-start | bytes 131072 | tf_op jit(solution)/shard_map/psum | solution.py:331
  1379.4 216.7 %copy-start.15 = (f32[160,2048]{1,0:T(8,128)S(1)}, f32[160,2048]{1,0:T(8,128)}, u32[]{:S(2)}) copy-start(f32[160,2048]{1,0:T(8,128)} %reduce-scatter.17.cloned.1.call-done) | copy-start | bytes 3932164
  1379.4 216.8 %copy-start.63 = (f32[160]{0:T(256)S(1)}, f32[160]{0:T(256)}, u32[]{:S(2)}) copy-start(f32[160]{0:T(256)} %get-tuple-element.112) | copy-start | bytes 1924
  (35 other events, 78.6 us)
Sparse Core Ops, SparseCore 0:
  10.2 51.9 all-gather.14
  64.3 47.7 all-gather.12
  114.3 47.7 all-gather.10
  164.0 49.5 all-gather.16
  219.7 100.7 all-reduce.6
  322.5 155.7 all-gather.24
  480.5 90.6 all-gather.26
  573.2 91.7 all-gather.28
  666.6 41.5 all-gather.18
  709.6 43.3 all-gather.20
  754.7 43.3 all-gather.22
  800.5 51.3 reduce-scatter.16
  1150.5 100.6 all-reduce.8
  1255.2 110.1 reduce-scatter.28
  1369.3 109.7 reduce-scatter.30
  1483.1 110.1 reduce-scatter.32
  1595.8 54.6 reduce-scatter.36
  1652.9 54.8 reduce-scatter.38
  1710.5 54.8 reduce-scatter.34
  1768.8 67.6 reduce-scatter.20
  1840.1 66.6 reduce-scatter.22
  1910.3 66.7 reduce-scatter.24
  1980.6 67.0 reduce-scatter.26
  2050.1 33.6 reduce-scatter.18
  2090.9 117.5 all-reduce.10
where the time goes:
time: 2230 us; the launch traced here: 2220 us
  waiting for transfers between devices  1530 us (69%)
  matrix products  269 us (12%)
  local copies, waits for them, and re-layouts  193 us (9%)
  blocking collectives  121 us (5%)
  other arithmetic  74.4 us (3%)
    all_gather x1, waiting for transfers between devices, local(): lax.all_gather(shared_gate, 'expert', axis=0, tiled=True)  133 us
    unnamed x155, local copies, waits for them, and re-layouts  118 us
    reduce_scatter x1, waiting for transfers between devices, local(): lax.psum_scatter(grad_shared_down.astype(jnp.bfloat16), 'expert', scatter...  112 us
    unnamed x27, waiting for transfers between devices  103 us
    reduce_scatter x1, waiting for transfers between devices, local(): lax.psum_scatter(grad_shared_up.astype(jnp.bfloat16), 'expert', scatter_d...  97.3 us
    psum x1, waiting for transfers between devices, local(): lax.psum(jnp.dot(attended_low, output_w, preferred_element_type=jnp.float...  90 us
    all_gather x1, waiting for transfers between devices, local(): lax.all_gather(shared_down, 'expert', axis=1, tiled=True)  84.4 us
    all_gather x1, waiting for transfers between devices, local(): lax.all_gather(shared_up, 'expert', axis=0, tiled=True)  83.4 us
  transfers between devices with their start and end apart: 28, of which 24 were waited for; matrix products, arithmetic and copies ran while one was open for 20% of the time, Pallas kernels for 0%

commit v1 on v0

v1 whole, which is shorter than its diff:
```python
import jax
import jax.numpy as jnp
from jax import lax
from jax.sharding import PartitionSpec as P

HD = 128
TOP = 4

epsilon = 1e-06
rope_base = 1000000.0

RING, PAIR, SHARD = "ring", "pair", "shard"

BF, F32 = jnp.bfloat16, jnp.float32


def rotate_half(values_in):
    half_size = values_in.shape[-1] // 2
    return jnp.concatenate([-values_in[..., half_size:], values_in[..., :half_size]], axis=-1)


def rope_tables(positions, head_size):
    exponent = jnp.arange(0, head_size, 2, dtype=F32) / head_size
    frequency = rope_base ** (-exponent)
    angles = positions.astype(F32)[..., None] * frequency
    angles = jnp.concatenate([angles, angles], axis=-1)
    return (jnp.cos(angles), jnp.sin(angles))


def seq_layout(lengths, length_total):
    seq_ends = jnp.cumsum(lengths)
    starts = seq_ends - lengths
    places = jnp.arange(length_total, dtype=jnp.int32)
    member = (places[:, None] >= starts[None, :]) & (places[:, None] < seq_ends[None, :])
    seq_id = jnp.sum((places[:, None] >= seq_ends[None, :]).astype(jnp.int32), axis=1)
    offset = jnp.sum(jnp.where(member, starts[None, :], 0), axis=1)
    return (seq_id, places - offset)


def silu_slope(values_in):
    logistic = jax.nn.sigmoid(values_in)
    return logistic * (1.0 + values_in * (1.0 - logistic))


def norm_back(grad_normed, values_in, inverse, gain_wide, upstream_rows):
    normed = grad_normed * gain_wide
    return (
        upstream_rows
        + inverse * normed
        - values_in * inverse**3 * jnp.mean(normed * values_in, axis=1, keepdims=True)
    )


def dot(left, right, contract):
    return lax.dot_general(
        left, right, (((contract[0],), (contract[1],)), ((), ())), preferred_element_type=F32
    )


def two_parts(values_in):
    high = values_in.astype(BF)
    return high, (values_in - high.astype(F32)).astype(BF)


def flip(values_in, axis, bit):
    size = lax.axis_size(axis)
    return lax.ppermute(values_in, axis, [(i, i ^ bit) for i in range(size)])


def shift(values_in, step):
    size = lax.axis_size(RING)
    return lax.ppermute(values_in, RING, [(i, (i + step) % size) for i in range(size)])


def shard_bits():
    bits, bit = [], lax.axis_size(SHARD) // 2
    while bit:
        bits.append(bit)
        bit //= 2
    return bits


def team_bits():
    return [(PAIR, 1)] + [(SHARD, bit) for bit in shard_bits()]


def team_order():
    order = [(0, 0)]
    for axis, bit in team_bits():
        order += [(p ^ bit, s) if axis == PAIR else (p, s ^ bit) for p, s in order]
    return order


def team_sum(values_in):
    for axis, bit in reversed(team_bits()):
        half = values_in.shape[0] // 2
        got = flip(values_in[half:].astype(BF), axis, bit)
        values_in = values_in[:half].astype(F32) + got.astype(F32)
    return values_in


def shard_sum(values_in):
    for bit in reversed(shard_bits()):
        half = values_in.shape[0] // 2
        got = flip(values_in[half:].astype(BF), SHARD, bit)
        values_in = values_in[:half].astype(F32) + got.astype(F32)
    return values_in


def ring_gather(block):
    size = lax.axis_size(RING)
    ups, downs = [block], []
    for _ in range(size // 2):
        ups.append(shift(ups[-1], 1))
    last = block
    for _ in range((size - 1) // 2):
        last = shift(last, -1)
        downs.append(last)
    return ups + downs


def ring_sum(blocks):
    size = lax.axis_size(RING)
    back = size // 2
    total = blocks[0].astype(F32)
    running = blocks[back] if back else None
    for k in range(back, 0, -1):
        got = shift(running.astype(BF), -1).astype(F32)
        if k > 1:
            running = got + blocks[k - 1].astype(F32)
        else:
            total = total + got
    ahead = (size - 1) // 2
    running = blocks[back + ahead] if ahead else None
    for k in range(ahead, 0, -1):
        got = shift(running.astype(BF), 1).astype(F32)
        if k > 1:
            running = got + blocks[back + k - 1].astype(F32)
        else:
            total = total + got
    return total


def expert_gather(block):
    return [(b, flip(b, PAIR, 1)) for b in ring_gather(block)]


def expert_sum(pairs):
    return ring_sum(
        [own.astype(F32) + flip(other.astype(BF), PAIR, 1).astype(F32) for own, other in pairs]
    )


def all_sum(values_in):
    for axis in (SHARD, PAIR, RING):
        bit = 1
        while bit < lax.axis_size(axis):
            values_in = values_in + flip(values_in, axis, bit)
            bit *= 2
    return values_in


def local(
    tokens,
    norm_attn,
    w_query,
    b_query,
    w_key,
    b_key,
    w_value,
    b_value,
    w_output,
    norm_ffn,
    w_router,
    shared_mix,
    shared_gate,
    shared_up,
    shared_down,
    expert_gate,
    expert_up,
    expert_down,
    routes,
    seq_lengths,
    cotangent,
):
    n_shard = lax.axis_size(SHARD)
    ring_at, pair_at, shard_at = (lax.axis_index(a) for a in (RING, PAIR, SHARD))
    expert_at = ring_at * 2 + pair_at
    group_rows, model_width = tokens.shape
    rows = group_rows // n_shard
    experts = w_router.shape[1]
    capacity = rows * TOP * 5 // (4 * experts)
    slot_rows = experts * capacity
    scale = HD ** (-0.5)
    order = team_order()

    def block_of(values_in, flipped):
        return lax.dynamic_slice_in_dim(values_in, (shard_at ^ flipped) * rows, rows, 0)

    def team_rows(values_in):
        near = {s: block_of(values_in, s) for p, s in order if p == 0}
        far = [flip(near[0], PAIR, 1)]
        for bit in shard_bits():
            got = flip(jnp.concatenate(far, axis=0), SHARD, bit)
            far += [got[i * rows : (i + 1) * rows] for i in range(len(far))]
        far = dict(zip([s for p, s in order if p == 1], far, strict=True))
        return near, far, jnp.concatenate([far[s] if p else near[s] for p, s in order], axis=0)

    def halves(values_in):
        return values_in.reshape(2, values_in.shape[0] // 2, values_in.shape[1])

    def gather_units(parts):
        pack = jnp.concatenate([halves(part) for part in parts], axis=1)
        mine = lax.dynamic_index_in_dim(pack, pair_at, 0, keepdims=False)
        theirs = lax.dynamic_index_in_dim(pack, 1 - pair_at, 0, keepdims=False)
        got = flip(theirs, PAIR, 1)
        block = jnp.where(
            pair_at == 0,
            jnp.concatenate([mine, got], axis=1),
            jnp.concatenate([got, mine], axis=1),
        )
        return lax.all_gather(block, RING, axis=1, tiled=True)

    def scatter_units(grads):
        summed = lax.psum_scatter(
            jnp.concatenate([g.astype(BF) for g in grads], axis=0),
            RING,
            scatter_dimension=1,
            tiled=True,
        )
        width = summed.shape[1] // 2
        mine = lax.dynamic_slice_in_dim(summed, pair_at * width, width, 1)
        theirs = lax.dynamic_slice_in_dim(summed, (1 - pair_at) * width, width, 1)
        got = flip(theirs, PAIR, 1)
        first, second = jnp.where(pair_at == 0, mine, got), jnp.where(pair_at == 0, got, mine)
        out, at = [], 0
        for g in grads:
            n = g.shape[0]
            out.append(jnp.concatenate([first[at : at + n], second[at : at + n]], axis=0).astype(F32))
            at += n
        return out

    attn_w = gather_units([w_query.T, w_key.T, w_value.T, w_output])
    width_here = attn_w.shape[0] // 4
    heads_here = width_here // HD
    qkv_w, output_w = attn_w[: 3 * width_here], attn_w[3 * width_here :]
    shared_w = gather_units([shared_gate.T, shared_up.T, shared_down])
    units_here = shared_w.shape[0] // 3
    shared_gate_w, shared_up_w, shared_down_w = (
        shared_w[i * units_here : (i + 1) * units_here] for i in range(3)
    )
    expert_pack = [jnp.concatenate([expert_gate[0].T, expert_up[0].T, expert_down[0]], axis=0)]
    for bit in shard_bits():
        expert_pack = expert_pack + [flip(part, SHARD, bit) for part in expert_pack]
    piece = expert_down.shape[1]
    gate_w, up_w, down_w = (
        jnp.concatenate([part[i * piece : (i + 1) * piece] for part in expert_pack], axis=0)
        for i in range(3)
    )

    routes_in = jnp.concatenate([b for pair in expert_gather(routes.T) for b in pair], axis=1)
    chosen = jnp.any(routes_in == expert_at, axis=0)
    hits = chosen.astype(jnp.int32)
    places = jnp.arange(hits.shape[0], dtype=jnp.int32)
    slot = jnp.sum(jnp.where(places[None, :] < places[:, None], hits[None, :], 0), axis=1)
    slot_ids = jnp.arange(slot_rows, dtype=jnp.int32)
    table = jnp.sum(
        jnp.where((slot[None, :] == slot_ids[:, None]) & chosen[None, :], places[None, :], 0), axis=1
    )
    filled = slot_ids < jnp.sum(hits)

    def returned(values_in):
        taken = jnp.where(chosen[:, None], jnp.take(values_in, slot, axis=0, mode="clip"), jnp.zeros((), BF))
        blocks = [taken[i * rows : (i + 1) * rows] for i in range(experts)]
        return [(blocks[2 * i], blocks[2 * i + 1]) for i in range(experts // 2)]

    tokens_near, _, tokens_team = team_rows(tokens)
    far_lengths = flip(seq_lengths, PAIR, 1)
    lengths = jnp.stack(
        [
            lax.dynamic_index_in_dim(far_lengths if p else seq_lengths, shard_at ^ s, 0, False)
            for p, s in order
        ]
    )
    seq_id, positions = jax.vmap(lambda row: seq_layout(row, rows))(lengths)
    cosine, sine = rope_tables(positions, HD)
    cosine, sine = cosine[:, :, None, :], sine[:, :, None, :]
    allowed = (seq_id[:, :, None] == seq_id[:, None, :]) & (
        positions[:, None, :] <= positions[:, :, None]
    )
    resid_team = tokens_team.astype(F32)
    gain_one = norm_attn.astype(F32)
    inv_one_team = lax.rsqrt(jnp.mean(resid_team * resid_team, axis=1, keepdims=True) + epsilon)
    h_one = (resid_team * inv_one_team * gain_one).astype(BF)
    head_start = (shard_at * 2 + pair_at) * width_here
    qkv_b = jnp.concatenate(
        [lax.dynamic_slice_in_dim(b, head_start, width_here, 0) for b in (b_query, b_key, b_value)]
    ).astype(F32)
    qkv = dot(h_one, qkv_w, (1, 1)) + qkv_b
    team = len(order)

    def heads(values_in):
        return values_in.reshape(team, rows, heads_here, HD)

    query_pre, key_pre, value_pre = (
        heads(qkv[:, i * width_here : (i + 1) * width_here]) for i in range(3)
    )
    query_rot = (query_pre * cosine + rotate_half(query_pre) * sine).astype(BF)
    key_rot = (key_pre * cosine + rotate_half(key_pre) * sine).astype(BF)
    value_low = value_pre.astype(BF)
    raw_scores = (
        jnp.einsum("bqhd,bkhd->bhqk", query_rot, key_rot, preferred_element_type=F32) * scale
    )
    masked = jnp.where(allowed[:, None], raw_scores, -1e30)
    probs = jax.nn.softmax(masked, axis=-1)
    probs_low = probs.astype(BF)
    attended = jnp.einsum("bhqk,bkhd->bqhd", probs_low, value_low, preferred_element_type=F32)
    attended_low = attended.reshape(team * rows, width_here).astype(BF)
    attn_out = team_sum(dot(attended_low, output_w, (1, 0)))

    resid_in = tokens_near[0].astype(F32)
    x_two = resid_in + attn_out
    gain_two = norm_ffn.astype(F32)
    inv_two = lax.rsqrt(jnp.mean(x_two * x_two, axis=1, keepdims=True) + epsilon)
    h_two = (x_two * inv_two * gain_two).astype(BF)

    h_routed = expert_gather(h_two)
    h_list = list(h_routed[0])
    for bit in shard_bits():
        got = flip(jnp.concatenate(h_list, axis=0), SHARD, bit)
        h_list += [got[i * rows : (i + 1) * rows] for i in range(len(h_list))]
    h_team = jnp.concatenate(h_list, axis=0)
    rows_in = jnp.concatenate([b for pair in h_routed for b in pair], axis=0)
    rows_in = jnp.take(rows_in, table, axis=0, mode="clip")

    up_near, up_far, up_team = team_rows(cotangent)
    upstream = up_near[0].astype(F32)
    up_ring = ring_gather(up_near[0])
    up_routed = [up_near[0], up_far[0]] + [
        b for block in up_ring[1:] for b in (block, flip(block, PAIR, 1))
    ]
    up_rows = jnp.take(jnp.concatenate(up_routed, axis=0), table, axis=0, mode="clip")

    row_probs = jax.nn.softmax(
        jnp.dot(rows_in, w_router, preferred_element_type=F32), axis=-1
    )
    own_expert = (jnp.arange(experts, dtype=jnp.int32) == expert_at).astype(F32)
    row_gate = jnp.sum(row_probs * own_expert, axis=1) * filled.astype(F32)
    gate_e = dot(rows_in, gate_w, (1, 1))
    up_e = dot(rows_in, up_w, (1, 1))
    hidden_e = (jax.nn.silu(gate_e) * up_e).astype(BF)
    grad_rows = (row_gate[:, None] * up_rows.astype(F32)).astype(BF)
    grad_hidden_e = dot(grad_rows, down_w, (1, 1))
    grad_gate_e = (grad_hidden_e * up_e * silu_slope(gate_e)).astype(BF)
    grad_up_e = (grad_hidden_e * jax.nn.silu(gate_e)).astype(BF)
    gate_share = jnp.sum(hidden_e.astype(F32) * grad_hidden_e, axis=1)
    grad_logit = gate_share[:, None] * (own_expert - row_probs)
    logit_parts = jnp.concatenate(two_parts(grad_logit), axis=1)
    router_twice = jnp.concatenate([w_router, w_router], axis=1)
    grad_inputs = (
        dot(grad_gate_e, gate_w, (1, 0))
        + dot(grad_up_e, up_w, (1, 0))
        + dot(logit_parts, router_twice, (1, 1))
    ).astype(BF)
    grad_router = dot(logit_parts, rows_in, (0, 0))
    grad_router = grad_router[:experts] + grad_router[experts:]

    mix_team = jax.nn.sigmoid(jnp.dot(h_team, shared_mix, preferred_element_type=F32))
    gate_s = dot(h_team, shared_gate_w, (1, 1))
    up_s = dot(h_team, shared_up_w, (1, 1))
    hidden_s = (jax.nn.silu(gate_s) * up_s).astype(BF)
    grad_out_s = (mix_team[:, None] * up_team.astype(F32)).astype(BF)
    grad_hidden_s = dot(grad_out_s, shared_down_w, (1, 1))
    grad_gate_s = (grad_hidden_s * up_s * silu_slope(gate_s)).astype(BF)
    grad_up_s = (grad_hidden_s * jax.nn.silu(gate_s)).astype(BF)
    grad_mix = jnp.sum(hidden_s.astype(F32) * grad_hidden_s, axis=1) * (1.0 - mix_team)
    grad_h_shared = shard_sum(
        dot(grad_gate_s, shared_gate_w, (1, 0))
        + dot(grad_up_s, shared_up_w, (1, 0))
        + grad_mix[:, None] * shared_mix.astype(F32)[None, :]
    )
    mix_parts = jnp.stack(two_parts(grad_mix), axis=1)
    grad_mix_w = jnp.sum(dot(mix_parts, h_team, (0, 0)), axis=0)

    def with_shared(pairs, shared_rows):
        own, other = pairs[0]
        first = (own.astype(F32) + shared_rows[:rows], other.astype(F32) + shared_rows[rows:])
        return [first] + pairs[1:]

    grad_h_two = expert_sum(with_shared(returned(grad_inputs), grad_h_shared))
    grad_x_two = norm_back(grad_h_two, x_two, inv_two, gain_two, upstream)
    grad_norm_ffn = jnp.sum(grad_h_two * x_two * inv_two, axis=0)

    out_e = dot(hidden_e, down_w, (1, 0)).astype(BF)
    out_e = (row_gate[:, None] * out_e.astype(F32)).astype(BF)
    out_s = shard_sum(mix_team[:, None] * dot(hidden_s, shared_down_w, (1, 0)))
    block_out = (x_two + expert_sum(with_shared(returned(out_e), out_s))).astype(BF)

    grad_shared_gate, grad_shared_up, grad_shared_down = scatter_units(
        [
            dot(grad_gate_s, h_team, (0, 0)),
            dot(grad_up_s, h_team, (0, 0)),
            dot(hidden_s, grad_out_s, (0, 0)),
        ]
    )

    def expert_scatter(units, across):
        half = units.shape[1] // 2
        kept = dot(units[:, :half], across, (0, 0))
        given = dot(units[:, half:], across, (0, 0))
        for bit in reversed(shard_bits()):
            kept = kept + flip(given.astype(BF), SHARD, bit).astype(F32)
            half = kept.shape[0] // 2
            kept, given = kept[:half], kept[half:]
        return jnp.concatenate([kept, given], axis=0)

    grad_expert_gate = expert_scatter(grad_gate_e, rows_in)
    grad_expert_up = expert_scatter(grad_up_e, rows_in)
    grad_expert_down = expert_scatter(hidden_e, grad_rows)

    grad_attn = grad_x_two.astype(BF)
    for axis, bit in team_bits():
        grad_attn = jnp.concatenate([grad_attn, flip(grad_attn, axis, bit)], axis=0)
    grad_attended = heads(dot(grad_attn, output_w, (1, 1)).astype(BF))
    grad_probs = jnp.einsum("bqhd,bkhd->bhqk", grad_attended, value_low, preferred_element_type=F32)
    grad_value = jnp.einsum(
        "bhqk,bqhd->bkhd", probs_low, grad_attended, preferred_element_type=F32
    ).astype(BF)
    row_delta = jnp.sum(probs * grad_probs, axis=-1, keepdims=True)
    grad_scores = (probs * (grad_probs - row_delta) * scale).astype(BF)
    grad_query = jnp.einsum("bhqk,bkhd->bqhd", grad_scores, key_rot, preferred_element_type=F32)
    grad_key = jnp.einsum("bhqk,bqhd->bkhd", grad_scores, query_rot, preferred_element_type=F32)
    grad_query = (grad_query * cosine - rotate_half(grad_query * sine)).astype(BF)
    grad_key = (grad_key * cosine - rotate_half(grad_key * sine)).astype(BF)
    grad_qkv = jnp.concatenate(
        [g.reshape(team * rows, width_here) for g in (grad_query, grad_key, grad_value)], axis=1
    )
    grad_h_one = team_sum(dot(grad_qkv, qkv_w, (1, 0)))
    grad_qkv_w = dot(grad_qkv, h_one, (0, 0))
    grad_query_w, grad_key_w, grad_value_w, grad_output_w = scatter_units(
        [grad_qkv_w[i * width_here : (i + 1) * width_here] for i in range(3)]
        + [dot(attended_low, grad_attn, (0, 0))]
    )
    grad_qkv_b = jnp.sum(grad_qkv.astype(F32), axis=0).reshape(3, width_here)
    grad_qkv_b = lax.dynamic_update_slice_in_dim(
        jnp.zeros((3, b_query.shape[0]), F32), grad_qkv_b, head_start, 1
    )
    inv_one = lax.rsqrt(jnp.mean(resid_in * resid_in, axis=1, keepdims=True) + epsilon)
    grad_norm_attn = jnp.sum(grad_h_one * resid_in * inv_one, axis=0)
    grad_tokens = norm_back(grad_h_one, resid_in, inv_one, gain_one, grad_x_two)

    small = all_sum(
        jnp.concatenate(
            [
                grad_qkv_b,
                jnp.stack([grad_norm_attn, grad_norm_ffn, grad_mix_w]),
                grad_router,
            ],
            axis=0,
        )
    )
    return (
        block_out,
        grad_tokens,
        small[3],
        grad_query_w.T,
        small[0],
        grad_key_w.T,
        small[1],
        grad_value_w.T,
        small[2],
        grad_output_w,
        small[4],
        small[6:].T,
        small[5],
        grad_shared_gate.T,
        grad_shared_up.T,
        grad_shared_down,
        grad_expert_gate.T[None],
        grad_expert_up.T[None],
        grad_expert_down[None],
    )


def solution(mesh):
    experts, shards = mesh.shape["expert"], mesh.shape["shard"]
    grid = jax.sharding.Mesh(
        mesh.devices.reshape(experts // 2, 2, shards), (RING, PAIR, SHARD)
    )
    expert = (RING, PAIR)
    every = (RING, PAIR, SHARD)
    return jax.shard_map(
        local,
        mesh=grid,
        in_specs=(
            P(expert, None),
            P(),
            P(expert, SHARD),
            P(),
            P(expert, SHARD),
            P(),
            P(expert, SHARD),
            P(),
            P(SHARD, expert),
            P(),
            P(),
            P(),
            P(expert, SHARD),
            P(expert, SHARD),
            P(SHARD, expert),
            P(expert, None, SHARD),
            P(expert, None, SHARD),
            P(expert, SHARD, None),
            P(every, None),
            P(expert, None),
            P(expert, None),
        ),
        out_specs=(
            P(every, None),
            P(every, None),
            P(),
            P(expert, SHARD),
            P(),
            P(expert, SHARD),
            P(),
            P(expert, SHARD),
            P(),
            P(SHARD, expert),
            P(),
            P(),
            P(),
            P(expert, SHARD),
            P(expert, SHARD),
            P(SHARD, expert),
            P(expert, None, SHARD),
            P(expert, None, SHARD),
            P(expert, SHARD, None),
        ),
        check_vma=False,
    )
```

time: 2230 us -> 1090 us (0.49)
  waiting for transfers between devices: 1530 us -> 431 us
  starting transfers between devices: 17.3 us -> 154 us
  blocking collectives: 121 us -> 0 us
  matrix products: 269 us -> 215 us
  local copies, waits for them, and re-layouts: 193 us -> 164 us
  other arithmetic: 74.4 us -> 97.4 us
    reduce_scatter x10 -> x2, waiting for transfers between devices: 563 us -> 6.48 us  [scatter_units(): lax.psum_scatter(jnp.concatenate([g.astype(BF) for g in grads], axis=0),...]
    all_gather x10 -> x2, waiting for transfers between devices: 561 us -> 51.7 us  [gather_units(): return lax.all_gather(block, RING, axis=1, tiled=True)]
    ppermute x0 -> x74, waiting for transfers between devices: none -> 372 us  [the longest x59 280 us: flip(): return lax.ppermute(values_in, axis, [(i, i ^ bit) for i in range(size)])]
    psum x3 -> x0, waiting for transfers between devices: 169 us -> none  [the longest x1 90 us: local(): lax.psum(jnp.dot(attended_low, output_w, preferred_element_type=jnp.float...]
    ppermute x0 -> x74, starting transfers between devices: none -> 154 us  [the longest x15 103 us: shift(): lax.ppermute(values_in, RING, [(i, (i + step) % size) for i in range(size)])]
    all_to_all x3 -> x0, waiting for transfers between devices: 131 us -> none  [the longest x1 69.7 us: local(): lax.all_to_all(out_rows.reshape(experts, capacity, model_width), 'expert'...]
    unnamed x27 -> x4, waiting for transfers between devices: 103 us -> 0.07 us
    all_to_all x1 -> x0, blocking collectives: 80.3 us -> none  [local(): lax.all_to_all(grad_send, 'expert', split_axis=0, concat_axis=0, tiled=True)]
  transfers between devices with their start and end apart: 28 -> 78, of which waited for: 24 -> 34; matrix products, arithmetic and copies ran while one was open for 20% -> 33% of each run, Pallas kernels for 0% -> 0%
where the time goes in v1:
time: 1090 us; the launch traced here: 1080 us
  waiting for transfers between devices  431 us (40%)
  matrix products  215 us (20%)
  local copies, waits for them, and re-layouts  164 us (15%)
  starting transfers between devices  154 us (14%)
  other arithmetic  97.4 us (9%)
  between operations  16.3 us (1%)
    ppermute x59, waiting for transfers between devices, flip(): return lax.ppermute(values_in, axis, [(i, i ^ bit) for i in range(size)])  280 us
    dot_general x30, matrix products, dot(): lax.dot_general(left, right, (((contract[0],), (contract[1],)), ((), ()))...  185 us
    ppermute x15, starting transfers between devices, shift(): lax.ppermute(values_in, RING, [(i, (i + step) % size) for i in range(size)])  103 us
    ppermute x15, waiting for transfers between devices, shift(): lax.ppermute(values_in, RING, [(i, (i + step) % size) for i in range(size)])  91.9 us
    unnamed x296, local copies, waits for them, and re-layouts  67.8 us
    all_gather x2, waiting for transfers between devices, gather_units(): return lax.all_gather(block, RING, axis=1, tiled=True)  51.7 us
    ppermute x59, starting transfers between devices, flip(): return lax.ppermute(values_in, axis, [(i, i ^ bit) for i in range(size)])  51.6 us
  transfers between devices with their start and end apart: 78, of which 34 were waited for; matrix products, arithmetic and copies ran while one was open for 33% of the time, Pallas kernels for 0%

profile of v1, /device:TPU:0, one launch (start us, length us, event | category | flops | bytes accessed | tf_op | source)
XLA Modules:
  0.0 1077.8 jit_solution(8173089629408857016)
XLA Ops:
  7.2 5.1 collective-permute-start.13
  26.9 5.7 collective-permute-done.3
  78.8 51.7 %all-gather.3.cloned.1.call-done = bf16[1024,2048]{1,0:T(8,128)(2,1)} async-done(((bf16[1024,512]{1,0:T(8,128)(2,1)}), bf16[1024,2048]{1,0:T(8,128)(2,1)}) %all-gather.3.cloned.1.call-update) | async-done | bytes 4194320 | tf_op jit(solution)/shard_map/all_gather | solution.py:222
  130.5 7.6 convolution_add_fusion
  167.2 5.6 copy.165
  183.6 8.3 collective-permute-done.44
  200.4 25.0 %collective-permute-done.40 = bf16[160,2048]{1,0:T(8,128)(2,1)S(1)} collective-permute-done((bf16[160,2048]{1,0:T(8,128)(2,1)}, bf16[160,2048]{1,0:T(8,128)(2,1)S(1)}, u32[]{:S(2)}, u32[]{:S(2)}) %collective-permute-start.40) | collective-permute-done | bytes 655392 | tf_op jit(solution)/shard_map/ppermute | solution.py:72
  234.7 7.8 collective-permute-done.41
  248.9 11.9 %gather_fusion.2 = bf16[800,2048]{1,0:T(8,128)(2,1)} fusion(bf16[1280,2048]{1,0:T(8,128)(2,1)} %constant_dynamic-update-slice_fusion.11, s32[1024]{0:T(1024)S(1)} %pad_clamp_fusion.1), kind=kCustom, calls=%fused_computation.2 | custom fusion | bytes 6556800 | tf_op jit(solution)/shard_map/jit(_take)/gather | solution.py:342
  261.6 11.8 %collective-permute-done.6 = bf16[320,2048]{1,0:T(8,128)(2,1)} collective-permute-done((bf16[320,2048]{1,0:T(8,128)(2,1)}, bf16[320,2048]{1,0:T(8,128)(2,1)}, u32[]{:S(2)}, u32[]{:S(2)}) %collective-permute-start.6) | collective-permute-done | bytes 1310752 | tf_op jit(solution)/shard_map/ppermute | solution.py:67
  280.5 11.1 %collective-permute-done.7 = bf16[160,2048]{1,0:T(8,128)(2,1)S(1)} collective-permute-done((bf16[160,2048]{1,0:T(8,128)(2,1)S(1)}, bf16[160,2048]{1,0:T(8,128)(2,1)S(1)}, u32[]{:S(2)}, u32[]{:S(2)}) %collective-permute-start.7) | collective-permute-done | bytes 655392 | tf_op jit(solution)/shard_map/ppermute | solution.py:67
  294.1 12.6 %collective-permute-start.16 = (bf16[160,2048]{1,0:T(8,128)(2,1)S(1)}, bf16[160,2048]{1,0:T(8,128)(2,1)S(1)}, u32[]{:S(2)}, u32[]{:S(2)}) collective-permute-start(bf16[160,2048]{1,0:T(8,128)(2,1)S(1)} %get-tuple-element.97), channel_id=1, source_target_pairs={{0,8},{8,16},{16,24},{24,0},{1,9},{9,17},{17,25},{25,1},{2,10},{10... | collective-permute-start | bytes 1966088 | tf_op jit(solution)/shard_map/ppermute | solution.py:72
  317.7 18.9 %collective-permute-done.16 = bf16[160,2048]{1,0:T(8,128)(2,1)S(1)} collective-permute-done((bf16[160,2048]{1,0:T(8,128)(2,1)S(1)}, bf16[160,2048]{1,0:T(8,128)(2,1)S(1)}, u32[]{:S(2)}, u32[]{:S(2)}) %collective-permute-start.16) | collective-permute-done | bytes 655392 | tf_op jit(solution)/shard_map/ppermute | solution.py:72
  336.5 25.1 %collective-permute-start.18 = (bf16[160,2048]{1,0:T(8,128)(2,1)S(1)}, bf16[160,2048]{1,0:T(8,128)(2,1)S(1)}, u32[]{:S(2)}, u32[]{:S(2)}) collective-permute-start(bf16[160,2048]{1,0:T(8,128)(2,1)S(1)} %collective-permute-done.16), channel_id=1, source_target_pairs={{0,8},{8,16},{16,24},{24,0},{1,9},{9,17},{17,25},{25,1},{2,10},{10... | collective-permute-start | bytes 1966088 | tf_op jit(solution)/shard_map/ppermute | solution.py:72
  371.9 18.9 %collective-permute-done.18 = bf16[160,2048]{1,0:T(8,128)(2,1)S(1)} collective-permute-done((bf16[160,2048]{1,0:T(8,128)(2,1)S(1)}, bf16[160,2048]{1,0:T(8,128)(2,1)S(1)}, u32[]{:S(2)}, u32[]{:S(2)}) %collective-permute-start.18) | collective-permute-done | bytes 655392 | tf_op jit(solution)/shard_map/ppermute | solution.py:72
  395.0 12.2 %collective-permute-done.19 = bf16[160,2048]{1,0:T(8,128)(2,1)S(1)} collective-permute-done((bf16[160,2048]{1,0:T(8,128)(2,1)S(1)}, bf16[160,2048]{1,0:T(8,128)(2,1)S(1)}, u32[]{:S(2)}, u32[]{:S(2)}) %collective-permute-start.19) | collective-permute-done | bytes 655392 | tf_op jit(solution)/shard_map/ppermute | solution.py:67
  409.9 11.6 %gather_fusion = bf16[800,2048]{1,0:T(8,128)(2,1)S(1)} fusion(bf16[1280,2048]{1,0:T(8,128)(2,1)} %constant_dynamic-update-slice_fusion.3, s32[1024]{0:T(1024)S(1)} %pad_clamp_fusion.1), kind=kCustom, calls=%fused_computation | custom fusion | bytes 6556800 | tf_op jit(solution)/shard_map/jit(_take)/gather | solution.py:334
  421.6 4.7 pad_maximum_fusion.8
  428.5 7.5 fusion.82
  436.0 7.5 fusion.83
  443.5 15.2 %multiply_reduce_fusion = (f32[800]{0:T(1024)S(1)}, bf16[800,1408]{1,0:T(8,128)(2,1)}, bf16[800,1408]{1,0:T(8,128)(2,1)}, bf16[800,1408]{1,0:T(8,128)(2,1)}) fusion(f32[800,1408]{1,0:T(8,128)} %fusion.82, f32[800,1408]{1,0:T(8,128)} %fusion.83, bf16[352,2048]{1,0:T(8,128)(2,1)} %get-tuple-element.123, bf16[352,2048]{1,0:T(8,128)(2,1)} %get-tuple-element.120, ...), kind=kOutput, calls=%fused_computation.38 | convolution fusion | flops 4661992448 | bytes 24819968 | tf_op jit(solution)/shard_map/dot_general | solution.py:55
  458.7 8.0 multiply_convert_fusion.2
  470.5 6.1 gather_fusion.1
  476.7 9.9 fusion.81
  486.6 8.3 add_convert_fusion
  495.0 6.1 gather_fusion.3
  505.0 7.1 fusion.23
  512.1 7.9 fusion.19
  520.0 8.7 multiply_reduce_fusion.1
  534.2 6.9 fusion.21
  541.2 10.6 multiply_add_fusion
  569.3 6.3 collective-permute-done.49
  577.3 12.0 %collective-permute-start.50 = (bf16[160,2048]{1,0:T(8,128)(2,1)S(1)}, bf16[160,2048]{1,0:T(8,128)(2,1)S(1)}, u32[]{:S(2)}, u32[]{:S(2)}) collective-permute-start(bf16[160,2048]{1,0:T(8,128)(2,1)S(1)} %add_convert_fusion.3), channel_id=1, source_target_pairs={{0,24},{8,0},{16,8},{24,16},{1,25},{9,1},{17,9},{25,17},{2,26},{10... | collective-permute-start | bytes 1966088 | tf_op jit(solution)/shard_map/ppermute | solution.py:72
  593.6 23.4 %collective-permute-done.31 = bf16[160,2048]{1,0:T(8,128)(2,1)} collective-permute-done((bf16[160,2048]{1,0:T(8,128)(2,1)}, bf16[160,2048]{1,0:T(8,128)(2,1)}, u32[]{:S(2)}, u32[]{:S(2)}) %collective-permute-start.31) | collective-permute-done | bytes 655392 | tf_op jit(solution)/shard_map/ppermute | solution.py:67
  622.4 11.7 %collective-permute-start.32 = (bf16[160,2048]{1,0:T(8,128)(2,1)S(1)}, bf16[160,2048]{1,0:T(8,128)(2,1)S(1)}, u32[]{:S(2)}, u32[]{:S(2)}) collective-permute-start(bf16[160,2048]{1,0:T(8,128)(2,1)S(1)} %add_convert_fusion.6), channel_id=1, source_target_pairs={{0,24},{8,0},{16,8},{24,16},{1,25},{9,1},{17,9},{25,17},{2,26},{10... | collective-permute-start | bytes 1966088 | tf_op jit(solution)/shard_map/ppermute | solution.py:72
  637.6 8.8 collective-permute-start.54
  647.0 11.5 %collective-permute-start.52 = (bf16[160,2048]{1,0:T(8,128)(2,1)S(1)}, bf16[160,2048]{1,0:T(8,128)(2,1)S(1)}, u32[]{:S(2)}, u32[]{:S(2)}) collective-permute-start(bf16[160,2048]{1,0:T(8,128)(2,1)S(1)} %get-tuple-element.106), channel_id=1, source_target_pairs={{0,24},{8,0},{16,8},{24,16},{1,25},{9,1},{17,9},{25,17},{2,26},{10... | collective-permute-start | bytes 1966088 | tf_op jit(solution)/shard_map/ppermute | solution.py:72
  665.7 11.7 %collective-permute-start.34 = (bf16[160,2048]{1,0:T(8,128)(2,1)S(1)}, bf16[160,2048]{1,0:T(8,128)(2,1)S(1)}, u32[]{:S(2)}, u32[]{:S(2)}) collective-permute-start(bf16[160,2048]{1,0:T(8,128)(2,1)S(1)} %get-tuple-element.112), channel_id=1, source_target_pairs={{0,24},{8,0},{16,8},{24,16},{1,25},{9,1},{17,9},{25,17},{2,26},{10... | collective-permute-start | bytes 1966088 | tf_op jit(solution)/shard_map/ppermute | solution.py:72
  680.7 13.1 %collective-permute-done.36 = bf16[160,2048]{1,0:T(8,128)(2,1)S(1)} collective-permute-done((bf16[160,2048]{1,0:T(8,128)(2,1)S(1)}, bf16[160,2048]{1,0:T(8,128)(2,1)S(1)}, u32[]{:S(2)}, u32[]{:S(2)}) %collective-permute-start.36) | collective-permute-done | bytes 655392 | tf_op jit(solution)/shard_map/ppermute | solution.py:72
  693.8 11.3 %collective-permute-done.34 = bf16[160,2048]{1,0:T(8,128)(2,1)S(1)} collective-permute-done((bf16[160,2048]{1,0:T(8,128)(2,1)S(1)}, bf16[160,2048]{1,0:T(8,128)(2,1)S(1)}, u32[]{:S(2)}, u32[]{:S(2)}) %collective-permute-start.34) | collective-permute-done | bytes 655392 | tf_op jit(solution)/shard_map/ppermute | solution.py:72
  709.8 15.2 %collective-permute-done.55 = bf16[160,2048]{1,0:T(8,128)(2,1)S(1)} collective-permute-done((bf16[160,2048]{1,0:T(8,128)(2,1)S(1)}, bf16[160,2048]{1,0:T(8,128)(2,1)S(1)}, u32[]{:S(2)}, u32[]{:S(2)}) %collective-permute-start.55) | collective-permute-done | bytes 655392 | tf_op jit(solution)/shard_map/ppermute | solution.py:67
  725.5 29.5 %collective-permute-done.56 = bf16[320,2048]{1,0:T(8,128)(2,1)S(1)} collective-permute-done((bf16[320,2048]{1,0:T(8,128)(2,1)S(1)}, bf16[320,2048]{1,0:T(8,128)(2,1)S(1)}, u32[]{:S(2)}, u32[]{:S(2)}) %collective-permute-start.56) | collective-permute-done | bytes 1310752 | tf_op jit(solution)/shard_map/ppermute | solution.py:67
  755.4 4.9 collective-permute-done.57
  774.2 6.6 fusion.36
  780.8 7.9 broadcast_multiply_fusion
  795.2 5.0 convolution_convert_fusion.1
  805.1 7.6 convolution_convert_fusion.5
  812.7 5.8 convolution_convert_fusion.7
  818.4 5.6 convolution_convert_fusion.6
  829.4 6.9 fusion.11
  838.3 4.9 convolution_convert_fusion.3
  843.2 4.9 convolution_convert_fusion.4
  848.6 5.4 convolution_convert_fusion.2
  855.3 5.4 convolution_reduce_fusion
  877.2 18.3 %collective-permute-done.59 = bf16[320,2048]{1,0:T(8,128)(2,1)S(1)} collective-permute-done((bf16[320,2048]{1,0:T(8,128)(2,1)S(1)}, bf16[320,2048]{1,0:T(8,128)(2,1)S(1)}, u32[]{:S(2)}, u32[]{:S(2)}) %collective-permute-start.59) | collective-permute-done | bytes 1310752 | tf_op jit(solution)/shard_map/ppermute | solution.py:67
  897.4 5.2 convert_add_fusion
  906.9 5.2 collective-permute-done.60
  919.0 7.5 collective-permute-done.71
  931.2 26.3 %collective-permute-done.69 = bf16[352,2048]{1,0:T(8,128)(2,1)} collective-permute-done((bf16[352,2048]{1,0:T(8,128)(2,1)}, bf16[352,2048]{1,0:T(8,128)(2,1)}, u32[]{:S(2)}, u32[]{:S(2)}) %collective-permute-start.69) | collective-permute-done | bytes 1441824 | tf_op jit(solution)/shard_map/ppermute | solution.py:67
  960.7 29.9 %collective-permute-done.62 = f32[14,2048]{1,0:T(8,128)S(1)} collective-permute-done((f32[14,2048]{1,0:T(8,128)S(1)}, f32[14,2048]{1,0:T(8,128)S(1)}, u32[]{:S(2)}, u32[]{:S(2)}) %collective-permute-start.62) | collective-permute-done | bytes 114720 | tf_op jit(solution)/shard_map/ppermute | solution.py:67
  996.0 13.5 %collective-permute-done.64 = f32[14,2048]{1,0:T(8,128)S(1)} collective-permute-done((f32[14,2048]{1,0:T(8,128)S(1)}, f32[14,2048]{1,0:T(8,128)S(1)}, u32[]{:S(2)}, u32[]{:S(2)}) %collective-permute-start.64) | collective-permute-done | bytes 114720 | tf_op jit(solution)/shard_map/ppermute | solution.py:67
  1011.2 14.1 %collective-permute-done.65 = f32[14,2048]{1,0:T(8,128)S(1)} collective-permute-done((f32[14,2048]{1,0:T(8,128)S(1)}, f32[14,2048]{1,0:T(8,128)S(1)}, u32[]{:S(2)}, u32[]{:S(2)}) %collective-permute-start.65) | collective-permute-done | bytes 114720 | tf_op jit(solution)/shard_map/ppermute | solution.py:67
  1029.2 6.5 reduce-scatter.5.cloned.1.call-done
  1046.2 18.3 %collective-permute-done.67 = bf16[2112,256]{1,0:T(8,128)(2,1)} collective-permute-done((bf16[2112,256]{1,0:T(8,128)(2,1)}, bf16[2112,256]{1,0:T(8,128)(2,1)}, u32[]{:S(2)}, u32[]{:S(2)}) %collective-permute-start.67) | collective-permute-done | bytes 1081376 | tf_op jit(solution)/shard_map/ppermute | solution.py:67
  (589 shorter events, 325.9 us)
Async XLA Ops:
  7.2 123.3 %all-gather.3.cloned.1.call-start = ((), (), s32[]{:S(2)}) async-start(), calls=%async_computation.2 | async-start | bytes 5242880 | tf_op jit(solution)/shard_map/all_gather | solution.py:222
  7.2 45.0 %collective-permute-start.13 = (s32[4,160]{1,0:T(4,128)}, s32[4,160]{1,0:T(4,128)S(1)}, u32[]{:S(2)}, u32[]{:S(2)}) collective-permute-start(s32[4,160]{1,0:T(4,128)} %bitcast.156), channel_id=1, source_target_pairs={{0,24},{8,0},{16,8},{24,16},{1,25},{9,1},{17,9},{25,17},{2,26},{10... | collective-permute-start | bytes 7688 | tf_op jit(solution)/shard_map/ppermute | solution.py:72
  12.3 38.1 %collective-permute-start.9 = (s32[4,160]{1,0:T(4,128)}, s32[4,160]{1,0:T(4,128)S(1)}, u32[]{:S(2)}, u32[]{:S(2)}) collective-permute-start(s32[4,160]{1,0:T(4,128)} %bitcast.157), channel_id=1, source_target_pairs={{0,8},{8,16},{16,24},{24,0},{1,9},{9,17},{17,25},{25,1},{2,10},{10... | collective-permute-start | bytes 7688 | tf_op jit(solution)/shard_map/ppermute | solution.py:72
  12.3 47.7 %collective-permute-start.8 = (s32[4,160]{1,0:T(4,128)}, s32[4,160]{1,0:T(4,128)S(1)}, u32[]{:S(2)}, u32[]{:S(2)}) collective-permute-start(s32[4,160]{1,0:T(4,128)} %bitcast.158), channel_id=1, source_target_pairs={{0,4},{4,0},{1,5},{5,1},{2,6},{6,2},{3,7},{7,3},{8,12},{12,8},{9,1... | collective-permute-start | bytes 7688 | tf_op jit(solution)/shard_map/ppermute | solution.py:67
  13.9 33.7 %collective-permute-start.4 = (s32[4,8]{1,0:T(4,128)}, s32[4,8]{1,0:T(4,128)}, u32[]{:S(2)}, u32[]{:S(2)}) collective-permute-start(s32[4,8]{1,0:T(4,128)} %param.40), channel_id=1, source_target_pairs={{0,4},{4,0},{1,5},{5,1},{2,6},{6,2},{3,7},{7,3},{8,12},{12,8},{9,1... | collective-permute-start | bytes 392 | tf_op jit(solution)/shard_map/ppermute | solution.py:67
  32.6 16.1 %collective-permute-start = (bf16[160,2048]{1,0:T(8,128)(2,1)S(1)}, bf16[160,2048]{1,0:T(8,128)(2,1)}, u32[]{:S(2)}, u32[]{:S(2)}) collective-permute-start(bf16[160,2048]{1,0:T(8,128)(2,1)S(1)} %get-tuple-element.88), channel_id=1, source_target_pairs={{0,4},{4,0},{1,5},{5,1},{2,6},{6,2},{3,7},{7,3},{8,12},{12,8},{9,1... | collective-permute-start | bytes 1966088 | tf_op jit(solution)/shard_map/ppermute | solution.py:67
  35.3 469.6 %all-gather.5.cloned.1.call-start = ((), (), s32[]{:S(2)}) async-start(), calls=%async_computation.3 | async-start | bytes 10813440 | tf_op jit(solution)/shard_map/all_gather | solution.py:222
  48.7 17.5 %collective-permute-start.1 = (bf16[160,2048]{1,0:T(8,128)(2,1)}, bf16[160,2048]{1,0:T(8,128)(2,1)S(1)}, u32[]{:S(2)}, u32[]{:S(2)}) collective-permute-start(bf16[160,2048]{1,0:T(8,128)(2,1)} %collective-permute-done), channel_id=1, source_target_pairs={{0,2},{1,3},{2,0},{3,1},{4,6},{5,7},{6,4},{7,5},{8,10},{9,11},{10,... | collective-permute-start | bytes 1966088 | tf_op jit(solution)/shard_map/ppermute | solution.py:67
  60.1 114.8 %collective-permute-start.38 = (bf16[160,2048]{1,0:T(8,128)(2,1)}, bf16[160,2048]{1,0:T(8,128)(2,1)}, u32[]{:S(2)}, u32[]{:S(2)}) collective-permute-start(bf16[160,2048]{1,0:T(8,128)(2,1)} %get-tuple-element.95), channel_id=1, source_target_pairs={{0,8},{8,16},{16,24},{24,0},{1,9},{9,17},{17,25},{25,1},{2,10},{10... | collective-permute-start | bytes 1966088 | tf_op jit(solution)/shard_map/ppermute | solution.py:72
  60.1 104.5 %collective-permute-start.37 = (bf16[160,2048]{1,0:T(8,128)(2,1)}, bf16[160,2048]{1,0:T(8,128)(2,1)}, u32[]{:S(2)}, u32[]{:S(2)}) collective-permute-start(bf16[160,2048]{1,0:T(8,128)(2,1)} %get-tuple-element.95), channel_id=1, source_target_pairs={{0,4},{4,0},{1,5},{5,1},{2,6},{6,2},{3,7},{7,3},{8,12},{12,8},{9,1... | collective-permute-start | bytes 1966088 | tf_op jit(solution)/shard_map/ppermute | solution.py:67
  61.7 116.9 %collective-permute-start.27 = (bf16[2112,256]{1,0:T(8,128)(2,1)}, bf16[2112,256]{1,0:T(8,128)(2,1)}, u32[]{:S(2)}, u32[]{:S(2)}) collective-permute-start(bf16[2112,256]{1,0:T(8,128)(2,1)} %get-tuple-element.130), channel_id=1, source_target_pairs={{0,4},{4,0},{1,5},{5,1},{2,6},{6,2},{3,7},{7,3},{8,12},{12,8},{9,1... | collective-permute-start | bytes 3244040 | tf_op jit(solution)/shard_map/ppermute | solution.py:67
  62.2 183.8 %collective-permute-start.22 = (bf16[1056,2048]{1,0:T(8,128)(2,1)}, bf16[1056,2048]{1,0:T(8,128)(2,1)}, u32[]{:S(2)}, u32[]{:S(2)}) collective-permute-start(bf16[1056,2048]{1,0:T(8,128)(2,1)} %pad_maximum_fusion.6), channel_id=1, source_target_pairs={{0,2},{1,3},{2,0},{3,1},{4,6},{5,7},{6,4},{7,5},{8,10},{9,11},{10,... | collective-permute-start | bytes 12976136 | tf_op jit(solution)/shard_map/ppermute | solution.py:67
  163.0 62.4 %collective-permute-start.5 = (bf16[640,2048]{1,0:T(8,128)(2,1)}, bf16[640,2048]{1,0:T(8,128)(2,1)}, u32[]{:S(2)}, u32[]{:S(2)}) collective-permute-start(bf16[640,2048]{1,0:T(8,128)(2,1)} %slice.699), channel_id=1, source_target_pairs={{0,1},{1,0},{2,3},{3,2},{4,5},{5,4},{6,7},{7,6},{8,9},{9,8},{10,11... | collective-permute-start | bytes 7864328 | tf_op jit(solution)/shard_map/ppermute | solution.py:67
  164.6 32.2 %collective-permute-start.42 = (bf16[160,2048]{1,0:T(8,128)(2,1)}, bf16[160,2048]{1,0:T(8,128)(2,1)}, u32[]{:S(2)}, u32[]{:S(2)}) collective-permute-start(bf16[160,2048]{1,0:T(8,128)(2,1)} %get-tuple-element.95), channel_id=1, source_target_pairs={{0,24},{8,0},{16,8},{24,16},{1,25},{9,1},{17,9},{25,17},{2,26},{10... | collective-permute-start | bytes 1966088 | tf_op jit(solution)/shard_map/ppermute | solution.py:72
  174.9 17.1 %collective-permute-start.44 = (bf16[160,2048]{1,0:T(8,128)(2,1)}, bf16[160,2048]{1,0:T(8,128)(2,1)S(1)}, u32[]{:S(2)}, u32[]{:S(2)}) collective-permute-start(bf16[160,2048]{1,0:T(8,128)(2,1)} %collective-permute-done.37), channel_id=1, source_target_pairs={{0,2},{1,3},{2,0},{3,1},{4,6},{5,7},{6,4},{7,5},{8,10},{9,11},{10,... | collective-permute-start | bytes 1966088 | tf_op jit(solution)/shard_map/ppermute | solution.py:67
  178.5 18.3 %collective-permute-start.39 = (bf16[160,2048]{1,0:T(8,128)(2,1)}, bf16[160,2048]{1,0:T(8,128)(2,1)S(1)}, u32[]{:S(2)}, u32[]{:S(2)}) collective-permute-start(bf16[160,2048]{1,0:T(8,128)(2,1)} %collective-permute-done.38), channel_id=1, source_target_pairs={{0,4},{4,0},{1,5},{5,1},{2,6},{6,2},{3,7},{7,3},{8,12},{12,8},{9,1... | collective-permute-start | bytes 1966088 | tf_op jit(solution)/shard_map/ppermute | solution.py:67
  183.6 842.4 %reduce-scatter.3.cloned.1.call-start = ((), (), s32[]{:S(2)}) async-start(), calls=%async_computation.4 | async-start | bytes 5242880 | tf_op jit(solution)/shard_map/reduce_scatter | solution.py:225
  192.0 33.4 %collective-permute-start.40 = (bf16[160,2048]{1,0:T(8,128)(2,1)}, bf16[160,2048]{1,0:T(8,128)(2,1)S(1)}, u32[]{:S(2)}, u32[]{:S(2)}) collective-permute-start(bf16[160,2048]{1,0:T(8,128)(2,1)} %collective-permute-done.38), channel_id=1, source_target_pairs={{0,8},{8,16},{16,24},{24,0},{1,9},{9,17},{17,25},{25,1},{2,10},{10... | collective-permute-start | bytes 1966088 | tf_op jit(solution)/shard_map/ppermute | solution.py:72
  196.8 116.1 %collective-permute-start.23 = (bf16[1056,2048]{1,0:T(8,128)(2,1)}, bf16[1056,2048]{1,0:T(8,128)(2,1)}, u32[]{:S(2)}, u32[]{:S(2)}) collective-permute-start(bf16[1056,2048]{1,0:T(8,128)(2,1)} %pad_maximum_fusion.6), channel_id=1, source_target_pairs={{0,1},{1,0},{2,3},{3,2},{4,5},{5,4},{6,7},{7,6},{8,9},{9,8},{10,11... | collective-permute-start | bytes 12976136 | tf_op jit(solution)/shard_map/ppermute | solution.py:67
  196.8 51.2 %collective-permute-start.43 = (bf16[160,2048]{1,0:T(8,128)(2,1)}, bf16[160,2048]{1,0:T(8,128)(2,1)S(1)}, u32[]{:S(2)}, u32[]{:S(2)}) collective-permute-start(bf16[160,2048]{1,0:T(8,128)(2,1)} %collective-permute-done.42), channel_id=1, source_target_pairs={{0,4},{4,0},{1,5},{5,1},{2,6},{6,2},{3,7},{7,3},{8,12},{12,8},{9,1... | collective-permute-start | bytes 1966088 | tf_op jit(solution)/shard_map/ppermute | solution.py:67
  225.4 35.3 %collective-permute-start.45 = (bf16[320,2048]{1,0:T(8,128)(2,1)S(1)}, bf16[320,2048]{1,0:T(8,128)(2,1)S(1)}, u32[]{:S(2)}, u32[]{:S(2)}) collective-permute-start(bf16[320,2048]{1,0:T(8,128)(2,1)S(1)} %pad_maximum_fusion.13), channel_id=1, source_target_pairs={{0,1},{1,0},{2,3},{3,2},{4,5},{5,4},{6,7},{7,6},{8,9},{9,8},{10,11... | collective-permute-start | bytes 3932168 | tf_op jit(solution)/shard_map/ppermute | solution.py:67
  225.4 17.1 %collective-permute-start.41 = (bf16[160,2048]{1,0:T(8,128)(2,1)S(1)}, bf16[160,2048]{1,0:T(8,128)(2,1)S(1)}, u32[]{:S(2)}, u32[]{:S(2)}) collective-permute-start(bf16[160,2048]{1,0:T(8,128)(2,1)S(1)} %collective-permute-done.40), channel_id=1, source_target_pairs={{0,4},{4,0},{1,5},{5,1},{2,6},{6,2},{3,7},{7,3},{8,12},{12,8},{9,1... | collective-permute-start | bytes 1966088 | tf_op jit(solution)/shard_map/ppermute | solution.py:67
  242.6 30.8 %collective-permute-start.6 = (bf16[320,2048]{1,0:T(8,128)(2,1)}, bf16[320,2048]{1,0:T(8,128)(2,1)}, u32[]{:S(2)}, u32[]{:S(2)}) collective-permute-start(bf16[320,2048]{1,0:T(8,128)(2,1)} %slice.706), channel_id=1, source_target_pairs={{0,2},{1,3},{2,0},{3,1},{4,6},{5,7},{6,4},{7,5},{8,10},{9,11},{10,... | collective-permute-start | bytes 3932168 | tf_op jit(solution)/shard_map/ppermute | solution.py:67
  245.9 115.7 %collective-permute-start.24 = (bf16[1056,2048]{1,0:T(8,128)(2,1)}, bf16[1056,2048]{1,0:T(8,128)(2,1)}, u32[]{:S(2)}, u32[]{:S(2)}) collective-permute-start(bf16[1056,2048]{1,0:T(8,128)(2,1)} %collective-permute-done.22), channel_id=1, source_target_pairs={{0,1},{1,0},{2,3},{3,2},{4,5},{5,4},{6,7},{7,6},{8,9},{9,8},{10,11... | collective-permute-start | bytes 12976136 | tf_op jit(solution)/shard_map/ppermute | solution.py:67
  294.1 42.5 %collective-permute-start.16 = (bf16[160,2048]{1,0:T(8,128)(2,1)S(1)}, bf16[160,2048]{1,0:T(8,128)(2,1)S(1)}, u32[]{:S(2)}, u32[]{:S(2)}) collective-permute-start(bf16[160,2048]{1,0:T(8,128)(2,1)S(1)} %get-tuple-element.97), channel_id=1, source_target_pairs={{0,8},{8,16},{16,24},{24,0},{1,9},{9,17},{17,25},{25,1},{2,10},{10... | collective-permute-start | bytes 1966088 | tf_op jit(solution)/shard_map/ppermute | solution.py:72
  311.1 56.6 %collective-permute-start.15 = (bf16[160,2048]{1,0:T(8,128)(2,1)S(1)}, bf16[160,2048]{1,0:T(8,128)(2,1)S(1)}, u32[]{:S(2)}, u32[]{:S(2)}) collective-permute-start(bf16[160,2048]{1,0:T(8,128)(2,1)S(1)} %get-tuple-element.97), channel_id=1, source_target_pairs={{0,4},{4,0},{1,5},{5,1},{2,6},{6,2},{3,7},{7,3},{8,12},{12,8},{9,1... | collective-permute-start | bytes 1966088 | tf_op jit(solution)/shard_map/ppermute | solution.py:67
  317.4 53.1 %collective-permute-start.20 = (bf16[160,2048]{1,0:T(8,128)(2,1)S(1)}, bf16[160,2048]{1,0:T(8,128)(2,1)S(1)}, u32[]{:S(2)}, u32[]{:S(2)}) collective-permute-start(bf16[160,2048]{1,0:T(8,128)(2,1)S(1)} %get-tuple-element.97), channel_id=1, source_target_pairs={{0,24},{8,0},{16,8},{24,16},{1,25},{9,1},{17,9},{25,17},{2,26},{10... | collective-permute-start | bytes 1966088 | tf_op jit(solution)/shard_map/ppermute | solution.py:72
  336.5 54.3 %collective-permute-start.18 = (bf16[160,2048]{1,0:T(8,128)(2,1)S(1)}, bf16[160,2048]{1,0:T(8,128)(2,1)S(1)}, u32[]{:S(2)}, u32[]{:S(2)}) collective-permute-start(bf16[160,2048]{1,0:T(8,128)(2,1)S(1)} %collective-permute-done.16), channel_id=1, source_target_pairs={{0,8},{8,16},{16,24},{24,0},{1,9},{9,17},{17,25},{25,1},{2,10},{10... | collective-permute-start | bytes 1966088 | tf_op jit(solution)/shard_map/ppermute | solution.py:72
  366.0 27.2 %collective-permute-start.17 = (bf16[160,2048]{1,0:T(8,128)(2,1)S(1)}, bf16[160,2048]{1,0:T(8,128)(2,1)S(1)}, u32[]{:S(2)}, u32[]{:S(2)}) collective-permute-start(bf16[160,2048]{1,0:T(8,128)(2,1)S(1)} %collective-permute-done.16), channel_id=1, source_target_pairs={{0,4},{4,0},{1,5},{5,1},{2,6},{6,2},{3,7},{7,3},{8,12},{12,8},{9,1... | collective-permute-start | bytes 1966088 | tf_op jit(solution)/shard_map/ppermute | solution.py:67
  369.0 52.6 %collective-permute-start.25 = (bf16[320,2048]{1,0:T(8,128)(2,1)}, bf16[320,2048]{1,0:T(8,128)(2,1)}, u32[]{:S(2)}, u32[]{:S(2)}) collective-permute-start(bf16[320,2048]{1,0:T(8,128)(2,1)} %pad_maximum_fusion.12), channel_id=1, source_target_pairs={{0,2},{1,3},{2,0},{3,1},{4,6},{5,7},{6,4},{7,5},{8,10},{9,11},{10,... | collective-permute-start | bytes 3932168 | tf_op jit(solution)/shard_map/ppermute | solution.py:67
  370.4 38.6 %collective-permute-start.21 = (bf16[160,2048]{1,0:T(8,128)(2,1)S(1)}, bf16[160,2048]{1,0:T(8,128)(2,1)S(1)}, u32[]{:S(2)}, u32[]{:S(2)}) collective-permute-start(bf16[160,2048]{1,0:T(8,128)(2,1)S(1)} %collective-permute-done.20), channel_id=1, source_target_pairs={{0,4},{4,0},{1,5},{5,1},{2,6},{6,2},{3,7},{7,3},{8,12},{12,8},{9,1... | collective-permute-start | bytes 1966088 | tf_op jit(solution)/shard_map/ppermute | solution.py:67
  390.8 16.3 %collective-permute-start.19 = (bf16[160,2048]{1,0:T(8,128)(2,1)S(1)}, bf16[160,2048]{1,0:T(8,128)(2,1)S(1)}, u32[]{:S(2)}, u32[]{:S(2)}) collective-permute-start(bf16[160,2048]{1,0:T(8,128)(2,1)S(1)} %collective-permute-done.18), channel_id=1, source_target_pairs={{0,4},{4,0},{1,5},{5,1},{2,6},{6,2},{3,7},{7,3},{8,12},{12,8},{9,1... | collective-permute-start | bytes 1966088 | tf_op jit(solution)/shard_map/ppermute | solution.py:67
  426.3 74.9 %collective-permute-start.26 = (bf16[640,2048]{1,0:T(8,128)(2,1)}, bf16[640,2048]{1,0:T(8,128)(2,1)}, u32[]{:S(2)}, u32[]{:S(2)}) collective-permute-start(bf16[640,2048]{1,0:T(8,128)(2,1)} %pad_maximum_fusion.8), channel_id=1, source_target_pairs={{0,1},{1,0},{2,3},{3,2},{4,5},{5,4},{6,7},{7,6},{8,9},{9,8},{10,11... | collective-permute-start | bytes 7864328 | tf_op jit(solution)/shard_map/ppermute | solution.py:67
  554.9 22.4 %collective-permute-start.28 = (bf16[640,2048]{1,0:T(8,128)(2,1)S(1)}, bf16[640,2048]{1,0:T(8,128)(2,1)}, u32[]{:S(2)}, u32[]{:S(2)}) collective-permute-start(bf16[640,2048]{1,0:T(8,128)(2,1)S(1)} %slice.698), channel_id=1, source_target_pairs={{0,1},{1,0},{2,3},{3,2},{4,5},{5,4},{6,7},{7,6},{8,9},{9,8},{10,11... | collective-permute-start | bytes 7864328 | tf_op jit(solution)/shard_map/ppermute | solution.py:67
  558.0 17.6 %collective-permute-start.49 = (bf16[160,2048]{1,0:T(8,128)(2,1)S(1)}, bf16[160,2048]{1,0:T(8,128)(2,1)S(1)}, u32[]{:S(2)}, u32[]{:S(2)}) collective-permute-start(bf16[160,2048]{1,0:T(8,128)(2,1)S(1)} %get-tuple-element.107), channel_id=1, source_target_pairs={{0,4},{4,0},{1,5},{5,1},{2,6},{6,2},{3,7},{7,3},{8,12},{12,8},{9,1... | collective-permute-start | bytes 1966088 | tf_op jit(solution)/shard_map/ppermute | solution.py:67
  559.5 62.3 %collective-permute-start.53 = (bf16[160,2048]{1,0:T(8,128)(2,1)}, bf16[160,2048]{1,0:T(8,128)(2,1)S(1)}, u32[]{:S(2)}, u32[]{:S(2)}) collective-permute-start(bf16[160,2048]{1,0:T(8,128)(2,1)} %get-tuple-element.108), channel_id=1, source_target_pairs={{0,4},{4,0},{1,5},{5,1},{2,6},{6,2},{3,7},{7,3},{8,12},{12,8},{9,1... | collective-permute-start | bytes 1966088 | tf_op jit(solution)/shard_map/ppermute | solution.py:67
  560.1 62.4 %collective-permute-start.51 = (bf16[160,2048]{1,0:T(8,128)(2,1)}, bf16[160,2048]{1,0:T(8,128)(2,1)S(1)}, u32[]{:S(2)}, u32[]{:S(2)}) collective-permute-start(bf16[160,2048]{1,0:T(8,128)(2,1)} %get-tuple-element.109), channel_id=1, source_target_pairs={{0,4},{4,0},{1,5},{5,1},{2,6},{6,2},{3,7},{7,3},{8,12},{12,8},{9,1... | collective-permute-start | bytes 1966088 | tf_op jit(solution)/shard_map/ppermute | solution.py:67
  564.3 52.7 %collective-permute-start.31 = (bf16[160,2048]{1,0:T(8,128)(2,1)}, bf16[160,2048]{1,0:T(8,128)(2,1)}, u32[]{:S(2)}, u32[]{:S(2)}) collective-permute-start(bf16[160,2048]{1,0:T(8,128)(2,1)} %get-tuple-element.113), channel_id=1, source_target_pairs={{0,4},{4,0},{1,5},{5,1},{2,6},{6,2},{3,7},{7,3},{8,12},{12,8},{9,1... | collective-permute-start | bytes 1966088 | tf_op jit(solution)/shard_map/ppermute | solution.py:67
  575.6 44.2 %collective-permute-start.47 = (bf16[320,2048]{1,0:T(8,128)(2,1)S(1)}, bf16[320,2048]{1,0:T(8,128)(2,1)S(1)}, u32[]{:S(2)}, u32[]{:S(2)}) collective-permute-start(bf16[320,2048]{1,0:T(8,128)(2,1)S(1)} %slice.704), channel_id=1, source_target_pairs={{0,2},{1,3},{2,0},{3,1},{4,6},{5,7},{6,4},{7,5},{8,10},{9,11},{10,... | collective-permute-start | bytes 3932168 | tf_op jit(solution)/shard_map/ppermute | solution.py:67
  577.3 56.9 %collective-permute-start.50 = (bf16[160,2048]{1,0:T(8,128)(2,1)S(1)}, bf16[160,2048]{1,0:T(8,128)(2,1)S(1)}, u32[]{:S(2)}, u32[]{:S(2)}) collective-permute-start(bf16[160,2048]{1,0:T(8,128)(2,1)S(1)} %add_convert_fusion.3), channel_id=1, source_target_pairs={{0,24},{8,0},{16,8},{24,16},{1,25},{9,1},{17,9},{25,17},{2,26},{10... | collective-permute-start | bytes 1966088 | tf_op jit(solution)/shard_map/ppermute | solution.py:72
  617.0 30.0 %collective-permute-start.29 = (bf16[320,2048]{1,0:T(8,128)(2,1)S(1)}, bf16[320,2048]{1,0:T(8,128)(2,1)S(1)}, u32[]{:S(2)}, u32[]{:S(2)}) collective-permute-start(bf16[320,2048]{1,0:T(8,128)(2,1)S(1)} %slice.705), channel_id=1, source_target_pairs={{0,2},{1,3},{2,0},{3,1},{4,6},{5,7},{6,4},{7,5},{8,10},{9,11},{10,... | collective-permute-start | bytes 3932168 | tf_op jit(solution)/shard_map/ppermute | solution.py:67
  619.8 17.7 %collective-permute-start.35 = (bf16[160,2048]{1,0:T(8,128)(2,1)S(1)}, bf16[160,2048]{1,0:T(8,128)(2,1)S(1)}, u32[]{:S(2)}, u32[]{:S(2)}) collective-permute-start(bf16[160,2048]{1,0:T(8,128)(2,1)S(1)} %copy-done.67), channel_id=1, source_target_pairs={{0,4},{4,0},{1,5},{5,1},{2,6},{6,2},{3,7},{7,3},{8,12},{12,8},{9,1... | collective-permute-start | bytes 1966088 | tf_op jit(solution)/shard_map/ppermute | solution.py:67
  621.8 37.1 %collective-permute-start.33 = (bf16[160,2048]{1,0:T(8,128)(2,1)}, bf16[160,2048]{1,0:T(8,128)(2,1)S(1)}, u32[]{:S(2)}, u32[]{:S(2)}) collective-permute-start(bf16[160,2048]{1,0:T(8,128)(2,1)} %get-tuple-element.115), channel_id=1, source_target_pairs={{0,4},{4,0},{1,5},{5,1},{2,6},{6,2},{3,7},{7,3},{8,12},{12,8},{9,1... | collective-permute-start | bytes 1966088 | tf_op jit(solution)/shard_map/ppermute | solution.py:67
  622.4 36.5 %collective-permute-start.32 = (bf16[160,2048]{1,0:T(8,128)(2,1)S(1)}, bf16[160,2048]{1,0:T(8,128)(2,1)S(1)}, u32[]{:S(2)}, u32[]{:S(2)}) collective-permute-start(bf16[160,2048]{1,0:T(8,128)(2,1)S(1)} %add_convert_fusion.6), channel_id=1, source_target_pairs={{0,24},{8,0},{16,8},{24,16},{1,25},{9,1},{17,9},{25,17},{2,26},{10... | collective-permute-start | bytes 1966088 | tf_op jit(solution)/shard_map/ppermute | solution.py:72
  635.0 30.7 %collective-permute-start.48 = (bf16[160,2048]{1,0:T(8,128)(2,1)S(1)}, bf16[160,2048]{1,0:T(8,128)(2,1)S(1)}, u32[]{:S(2)}, u32[]{:S(2)}) collective-permute-start(bf16[160,2048]{1,0:T(8,128)(2,1)S(1)} %get-tuple-element.104), channel_id=1, source_target_pairs={{0,4},{4,0},{1,5},{5,1},{2,6},{6,2},{3,7},{7,3},{8,12},{12,8},{9,1... | collective-permute-start | bytes 1966088 | tf_op jit(solution)/shard_map/ppermute | solution.py:67
  637.6 39.8 %collective-permute-start.54 = (bf16[160,2048]{1,0:T(8,128)(2,1)S(1)}, bf16[160,2048]{1,0:T(8,128)(2,1)S(1)}, u32[]{:S(2)}, u32[]{:S(2)}) collective-permute-start(bf16[160,2048]{1,0:T(8,128)(2,1)S(1)} %get-tuple-element.105), channel_id=1, source_target_pairs={{0,8},{8,16},{16,24},{24,0},{1,9},{9,17},{17,25},{25,1},{2,10},{10... | collective-permute-start | bytes 1966088 | tf_op jit(solution)/shard_map/ppermute | solution.py:72
  647.0 32.7 %collective-permute-start.52 = (bf16[160,2048]{1,0:T(8,128)(2,1)S(1)}, bf16[160,2048]{1,0:T(8,128)(2,1)S(1)}, u32[]{:S(2)}, u32[]{:S(2)}) collective-permute-start(bf16[160,2048]{1,0:T(8,128)(2,1)S(1)} %get-tuple-element.106), channel_id=1, source_target_pairs={{0,24},{8,0},{16,8},{24,16},{1,25},{9,1},{17,9},{25,17},{2,26},{10... | collective-permute-start | bytes 1966088 | tf_op jit(solution)/shard_map/ppermute | solution.py:72
  659.9 20.8 %collective-permute-start.30 = (bf16[160,2048]{1,0:T(8,128)(2,1)S(1)}, bf16[160,2048]{1,0:T(8,128)(2,1)S(1)}, u32[]{:S(2)}, u32[]{:S(2)}) collective-permute-start(bf16[160,2048]{1,0:T(8,128)(2,1)S(1)} %get-tuple-element.110), channel_id=1, source_target_pairs={{0,4},{4,0},{1,5},{5,1},{2,6},{6,2},{3,7},{7,3},{8,12},{12,8},{9,1... | collective-permute-start | bytes 1966088 | tf_op jit(solution)/shard_map/ppermute | solution.py:67
  661.6 32.2 %collective-permute-start.36 = (bf16[160,2048]{1,0:T(8,128)(2,1)S(1)}, bf16[160,2048]{1,0:T(8,128)(2,1)S(1)}, u32[]{:S(2)}, u32[]{:S(2)}) collective-permute-start(bf16[160,2048]{1,0:T(8,128)(2,1)S(1)} %get-tuple-element.111), channel_id=1, source_target_pairs={{0,8},{8,16},{16,24},{24,0},{1,9},{9,17},{17,25},{25,1},{2,10},{10... | collective-permute-start | bytes 1966088 | tf_op jit(solution)/shard_map/ppermute | solution.py:72
  665.7 39.5 %collective-permute-start.34 = (bf16[160,2048]{1,0:T(8,128)(2,1)S(1)}, bf16[160,2048]{1,0:T(8,128)(2,1)S(1)}, u32[]{:S(2)}, u32[]{:S(2)}) collective-permute-start(bf16[160,2048]{1,0:T(8,128)(2,1)S(1)} %get-tuple-element.112), channel_id=1, source_target_pairs={{0,24},{8,0},{16,8},{24,16},{1,25},{9,1},{17,9},{25,17},{2,26},{10... | collective-permute-start | bytes 1966088 | tf_op jit(solution)/shard_map/ppermute | solution.py:72
  708.3 16.7 %collective-permute-start.55 = (bf16[160,2048]{1,0:T(8,128)(2,1)S(1)}, bf16[160,2048]{1,0:T(8,128)(2,1)S(1)}, u32[]{:S(2)}, u32[]{:S(2)}) collective-permute-start(bf16[160,2048]{1,0:T(8,128)(2,1)S(1)} %get-tuple-element.85), channel_id=1, source_target_pairs={{0,4},{4,0},{1,5},{5,1},{2,6},{6,2},{3,7},{7,3},{8,12},{12,8},{9,1... | collective-permute-start | bytes 1966088 | tf_op jit(solution)/shard_map/ppermute | solution.py:67
  725.1 29.9 %collective-permute-start.56 = (bf16[320,2048]{1,0:T(8,128)(2,1)S(1)}, bf16[320,2048]{1,0:T(8,128)(2,1)S(1)}, u32[]{:S(2)}, u32[]{:S(2)}) collective-permute-start(bf16[320,2048]{1,0:T(8,128)(2,1)S(1)} %pad_maximum_fusion.14), channel_id=1, source_target_pairs={{0,2},{1,3},{2,0},{3,1},{4,6},{5,7},{6,4},{7,5},{8,10},{9,11},{10,... | collective-permute-start | bytes 3932168 | tf_op jit(solution)/shard_map/ppermute | solution.py:67
  804.4 231.2 %reduce-scatter.5.cloned.1.call-start = ((), (), s32[]{:S(2)}) async-start(), calls=%async_computation.5 | async-start | bytes 10813440 | tf_op jit(solution)/shard_map/reduce_scatter | solution.py:225
  836.7 24.0 %collective-permute-start.58 = (bf16[640,2048]{1,0:T(8,128)(2,1)S(1)}, bf16[640,2048]{1,0:T(8,128)(2,1)}, u32[]{:S(2)}, u32[]{:S(2)}) collective-permute-start(bf16[640,2048]{1,0:T(8,128)(2,1)S(1)} %slice.696), channel_id=1, source_target_pairs={{0,1},{1,0},{2,3},{3,2},{4,5},{5,4},{6,7},{7,6},{8,9},{9,8},{10,11... | collective-permute-start | bytes 7864328 | tf_op jit(solution)/shard_map/ppermute | solution.py:67
  843.2 20.8 %collective-permute-start.70 = (bf16[704,2048]{1,0:T(8,128)(2,1)}, bf16[704,2048]{1,0:T(8,128)(2,1)S(1)}, u32[]{:S(2)}, u32[]{:S(2)}) collective-permute-start(bf16[704,2048]{1,0:T(8,128)(2,1)} %convolution_convert_fusion.3), channel_id=1, source_target_pairs={{0,1},{1,0},{2,3},{3,2},{4,5},{5,4},{6,7},{7,6},{8,9},{9,8},{10,11... | collective-permute-start | bytes 8650760 | tf_op jit(solution)/shard_map/ppermute | solution.py:67
  848.1 23.6 %collective-permute-start.68 = (bf16[704,2048]{1,0:T(8,128)(2,1)}, bf16[704,2048]{1,0:T(8,128)(2,1)S(1)}, u32[]{:S(2)}, u32[]{:S(2)}) collective-permute-start(bf16[704,2048]{1,0:T(8,128)(2,1)} %convolution_convert_fusion.4), channel_id=1, source_target_pairs={{0,1},{1,0},{2,3},{3,2},{4,5},{5,4},{6,7},{7,6},{8,9},{9,8},{10,11... | collective-permute-start | bytes 8650760 | tf_op jit(solution)/shard_map/ppermute | solution.py:67
  854.0 43.4 %collective-permute-start.72 = (bf16[704,2048]{1,0:T(8,128)(2,1)}, bf16[704,2048]{1,0:T(8,128)(2,1)}, u32[]{:S(2)}, u32[]{:S(2)}) collective-permute-start(bf16[704,2048]{1,0:T(8,128)(2,1)} %convolution_convert_fusion.2), channel_id=1, source_target_pairs={{0,1},{1,0},{2,3},{3,2},{4,5},{5,4},{6,7},{7,6},{8,9},{9,8},{10,11... | collective-permute-start | bytes 8650760 | tf_op jit(solution)/shard_map/ppermute | solution.py:67
  863.9 31.6 %collective-permute-start.59 = (bf16[320,2048]{1,0:T(8,128)(2,1)S(1)}, bf16[320,2048]{1,0:T(8,128)(2,1)S(1)}, u32[]{:S(2)}, u32[]{:S(2)}) collective-permute-start(bf16[320,2048]{1,0:T(8,128)(2,1)S(1)} %slice.703), channel_id=1, source_target_pairs={{0,2},{1,3},{2,0},{3,1},{4,6},{5,7},{6,4},{7,5},{8,10},{9,11},{10,... | collective-permute-start | bytes 3932168 | tf_op jit(solution)/shard_map/ppermute | solution.py:67
  869.9 56.7 %collective-permute-start.71 = (bf16[352,2048]{1,0:T(8,128)(2,1)}, bf16[352,2048]{1,0:T(8,128)(2,1)}, u32[]{:S(2)}, u32[]{:S(2)}) collective-permute-start(bf16[352,2048]{1,0:T(8,128)(2,1)} %slice.701), channel_id=1, source_target_pairs={{0,2},{1,3},{2,0},{3,1},{4,6},{5,7},{6,4},{7,5},{8,10},{9,11},{10,... | collective-permute-start | bytes 4325384 | tf_op jit(solution)/shard_map/ppermute | solution.py:67
  876.6 80.9 %collective-permute-start.69 = (bf16[352,2048]{1,0:T(8,128)(2,1)}, bf16[352,2048]{1,0:T(8,128)(2,1)}, u32[]{:S(2)}, u32[]{:S(2)}) collective-permute-start(bf16[352,2048]{1,0:T(8,128)(2,1)} %slice.702), channel_id=1, source_target_pairs={{0,2},{1,3},{2,0},{3,1},{4,6},{5,7},{6,4},{7,5},{8,10},{9,11},{10,... | collective-permute-start | bytes 4325384 | tf_op jit(solution)/shard_map/ppermute | solution.py:67
  896.1 16.0 %collective-permute-start.60 = (bf16[160,2048]{1,0:T(8,128)(2,1)S(1)}, bf16[160,2048]{1,0:T(8,128)(2,1)S(1)}, u32[]{:S(2)}, u32[]{:S(2)}) collective-permute-start(bf16[160,2048]{1,0:T(8,128)(2,1)S(1)} %slice.707), channel_id=1, source_target_pairs={{0,4},{4,0},{1,5},{5,1},{2,6},{6,2},{3,7},{7,3},{8,12},{12,8},{9,1... | collective-permute-start | bytes 1966088 | tf_op jit(solution)/shard_map/ppermute | solution.py:67
  906.0 86.0 %collective-permute-start.73 = (bf16[352,2048]{1,0:T(8,128)(2,1)}, bf16[352,2048]{1,0:T(8,128)(2,1)}, u32[]{:S(2)}, u32[]{:S(2)}) collective-permute-start(bf16[352,2048]{1,0:T(8,128)(2,1)} %slice.700), channel_id=1, source_target_pairs={{0,2},{1,3},{2,0},{3,1},{4,6},{5,7},{6,4},{7,5},{8,10},{9,11},{10,... | collective-permute-start | bytes 4325384 | tf_op jit(solution)/shard_map/ppermute | solution.py:67
  931.0 59.5 %collective-permute-start.62 = (f32[14,2048]{1,0:T(8,128)S(1)}, f32[14,2048]{1,0:T(8,128)S(1)}, u32[]{:S(2)}, u32[]{:S(2)}) collective-permute-start(f32[14,2048]{1,0:T(8,128)S(1)} %add.343), channel_id=1, source_target_pairs={{0,2},{1,3},{2,0},{3,1},{4,6},{5,7},{6,4},{7,5},{8,10},{9,11},{10,... | collective-permute-start | bytes 344072 | tf_op jit(solution)/shard_map/ppermute | solution.py:67
  1037.9 26.6 %collective-permute-start.67 = (bf16[2112,256]{1,0:T(8,128)(2,1)}, bf16[2112,256]{1,0:T(8,128)(2,1)}, u32[]{:S(2)}, u32[]{:S(2)}) collective-permute-start(bf16[2112,256]{1,0:T(8,128)(2,1)} %constant_dynamic-slice_fusion.2), channel_id=1, source_target_pairs={{0,4},{4,0},{1,5},{5,1},{2,6},{6,2},{3,7},{7,3},{8,12},{12,8},{9,1... | collective-permute-start | bytes 3244040 | tf_op jit(solution)/shard_map/ppermute | solution.py:67
  (144 other events, 2165.5 us)
Sparse Core Ops, SparseCore 0:
  35.5 94.9 all-gather.2
  183.7 199.9 all-gather.4
  804.5 74.0 reduce-scatter.2
  881.0 154.6 reduce-scatter.4

commit v2 on v1

v2 whole, which is shorter than its diff:
```python
import functools

import jax
import jax.numpy as jnp
from jax import lax
from jax.experimental import pallas as pl
from jax.experimental.pallas import tpu as pltpu
from jax.sharding import PartitionSpec as P

HD = 128
TOP = 4
LANES = 128

NO_COST = pl.CostEstimate(flops=0, bytes_accessed=0, transcendentals=0)

epsilon = 1e-06
rope_base = 1000000.0

RING, PAIR, SHARD = "ring", "pair", "shard"

BF, F32 = jnp.bfloat16, jnp.float32

ATTN_STEPS, ATTN_BACK_STEPS = 4, 2


def rope_tables(positions, head_size):
    exponent = jnp.arange(0, head_size, 2, dtype=F32) / head_size
    frequency = rope_base ** (-exponent)
    angles = positions.astype(F32)[..., None] * frequency
    cosine, sine = jnp.cos(angles), jnp.sin(angles)
    return (
        jnp.concatenate([cosine, cosine], axis=-1),
        jnp.concatenate([-sine, sine], axis=-1),
    )


def seq_positions(lengths, length_total):
    seq_ends = jnp.cumsum(lengths)
    starts = seq_ends - lengths
    places = jnp.arange(length_total, dtype=jnp.int32)
    member = (places[:, None] >= starts[None, :]) & (places[:, None] < seq_ends[None, :])
    return places - jnp.sum(jnp.where(member, starts[None, :], 0), axis=1)


def norm_back(grad_normed, values_in, inverse, gain_wide, upstream_rows):
    normed = grad_normed * gain_wide
    return (
        upstream_rows
        + inverse * normed
        - values_in * inverse**3 * jnp.mean(normed * values_in, axis=1, keepdims=True)
    )


def dot(left, right, contract):
    return lax.dot_general(
        left, right, (((contract[0],), (contract[1],)), ((), ())), preferred_element_type=F32
    )


def two_parts(values_in):
    high = values_in.astype(BF)
    return high, (values_in - high.astype(F32)).astype(BF)


def swap_halves(values_in):
    return pltpu.roll(values_in, HD // 2, 1)


def causal_probs(query, key, start, scale):
    raw = dot(query, key, (1, 1)) * scale
    row = lax.broadcasted_iota(jnp.int32, raw.shape, 0)
    column = lax.broadcasted_iota(jnp.int32, raw.shape, 1)
    masked = jnp.where((column <= row) & (column >= start), raw, -1e30)
    powers = jnp.exp(masked - jnp.max(masked, axis=-1, keepdims=True))
    return powers / jnp.sum(powers, axis=-1, keepdims=True)


def in_halves(kept_ref, given_ref, made):
    steps = pl.num_programs(0)

    @pl.when(pl.program_id(0) < steps // 2)
    def _():
        kept_ref[...] = made

    @pl.when(pl.program_id(0) >= steps // 2)
    def _():
        given_ref[...] = made


def half_blocks(steps, rows_each, width):
    half = steps // 2
    return [
        pl.BlockSpec((rows_each, width), lambda i: (jnp.minimum(i, half - 1), 0)),
        pl.BlockSpec((rows_each, width), lambda i: (jnp.maximum(i - half, 0), 0)),
    ]


def attention_forward_body(
    rows, heads, scale, h_ref, w_ref, bias_ref, cos_ref, sin_ref, start_ref, kept_ref, given_ref, qkv_ref, att_ref
):
    width = heads * HD
    qkv = dot(h_ref[...], w_ref[: 3 * width], (1, 1)) + bias_ref[...]
    for block in range(h_ref.shape[0] // rows):
        here = slice(block * rows, (block + 1) * rows)
        cosine, sine, start = cos_ref[here], sin_ref[here], start_ref[here]
        for head in range(heads):
            at = [slice(i * width + head * HD, i * width + (head + 1) * HD) for i in range(3)]
            query, key, value = (qkv[here, span] for span in at)
            query = (query * cosine + swap_halves(query) * sine).astype(BF)
            key = (key * cosine + swap_halves(key) * sine).astype(BF)
            value = value.astype(BF)
            for span, kept in zip(at, (query, key, value), strict=True):
                qkv_ref[here, span] = kept
            probs = causal_probs(query, key, start, scale).astype(BF)
            att_ref[here, at[0]] = dot(probs, value, (1, 0)).astype(BF)
    in_halves(kept_ref, given_ref, dot(att_ref[...], w_ref[3 * width :], (1, 0)).astype(BF))


def attention_backward_body(
    rows,
    heads,
    scale,
    grad_ref,
    h_ref,
    w_ref,
    qkv_ref,
    att_ref,
    cos_ref,
    sin_ref,
    start_ref,
    kept_ref,
    given_ref,
    pack_ref,
    bias_ref,
    grad_qkv_ref,
    total_ref,
):
    width = heads * HD
    step = pl.program_id(0)
    grad_att = dot(grad_ref[...], w_ref[3 * width :], (1, 1)).astype(BF)
    for block in range(grad_ref.shape[0] // rows):
        here = slice(block * rows, (block + 1) * rows)
        cosine, sine, start = cos_ref[here], sin_ref[here], start_ref[here]
        for head in range(heads):
            at = [slice(i * width + head * HD, i * width + (head + 1) * HD) for i in range(3)]
            query, key, value = (qkv_ref[here, span] for span in at)
            grad_out = grad_att[here, at[0]]
            probs = causal_probs(query, key, start, scale)
            grad_probs = dot(grad_out, value, (1, 1))
            grad_value = dot(probs.astype(BF), grad_out, (0, 0))
            delta = jnp.sum(probs * grad_probs, axis=-1, keepdims=True)
            grad_scores = (probs * (grad_probs - delta) * scale).astype(BF)
            grad_query = dot(grad_scores, key, (1, 0))
            grad_key = dot(grad_scores, query, (0, 0))
            grad_query = grad_query * cosine - swap_halves(grad_query) * sine
            grad_key = grad_key * cosine - swap_halves(grad_key) * sine
            for span, made in zip(at, (grad_query, grad_key, grad_value), strict=True):
                grad_qkv_ref[here, span] = made.astype(BF)
    grad_qkv = grad_qkv_ref[...]
    in_halves(kept_ref, given_ref, dot(grad_qkv, w_ref[: 3 * width], (1, 0)).astype(BF))
    bias_share = jnp.sum(grad_qkv.astype(F32), axis=0, keepdims=True)
    qkv_share = dot(grad_qkv, h_ref[...], (0, 0))
    out_share = dot(att_ref[...], grad_ref[...], (0, 0))

    @pl.when(step == 0)
    def _():
        bias_ref[...] = bias_share
        total_ref[: 3 * width] = qkv_share
        total_ref[3 * width :] = out_share

    @pl.when(step > 0)
    def _():
        bias_ref[...] += bias_share
        total_ref[: 3 * width] += qkv_share
        total_ref[3 * width :] += out_share

    @pl.when(step == pl.num_programs(0) - 1)
    def _():
        pack_ref[...] = total_ref[...].astype(BF)


def anywhere():
    return pl.BlockSpec(memory_space=pl.ANY)


def waiting(body, count):
    def run(*refs):
        body(*refs[count:])

    return run


def once_block(*shape):
    return pl.BlockSpec(shape, lambda *i: (0,) * len(shape), pipeline_mode=pl.Buffered(1))


def step_block(rows_each, *rest):
    return pl.BlockSpec((rows_each,) + rest, lambda i: (i,) + (0,) * len(rest))


def whole_block(*shape):
    return pl.BlockSpec(shape, lambda i: (0,) * len(shape))


def attention_forward(h_one, weights, bias, cosine, sine, start, rows, heads, steps, waits=()):
    total, model = h_one.shape
    each, width = total // steps, heads * HD
    return pl.pallas_call(
        waiting(functools.partial(attention_forward_body, rows, heads, HD ** (-0.5)), len(waits)),
        grid=(steps,),
        in_specs=[anywhere()] * len(waits)
        + [
            step_block(each, model),
            whole_block(4 * width, model),
            whole_block(1, 3 * width),
            step_block(each, HD),
            step_block(each, HD),
            step_block(each, 1),
        ],
        out_specs=half_blocks(steps, each, model) + [step_block(each, 3 * width), step_block(each, width)],
        out_shape=[
            jax.ShapeDtypeStruct((total // 2, model), BF),
            jax.ShapeDtypeStruct((total // 2, model), BF),
            jax.ShapeDtypeStruct((total, 3 * width), BF),
            jax.ShapeDtypeStruct((total, width), BF),
        ],
        compiler_params=pltpu.CompilerParams(vmem_limit_bytes=40 << 20),
        cost_estimate=NO_COST,
    )(*waits, h_one, weights, bias, cosine, sine, start)


def attention_backward(grad, h_one, weights, qkv, att, cosine, sine, start, rows, heads, steps, waits=()):
    total, model = h_one.shape
    each, width = total // steps, heads * HD
    return pl.pallas_call(
        waiting(functools.partial(attention_backward_body, rows, heads, HD ** (-0.5)), len(waits)),
        grid=(steps,),
        in_specs=[anywhere()] * len(waits)
        + [
            step_block(each, model),
            step_block(each, model),
            whole_block(4 * width, model),
            step_block(each, 3 * width),
            step_block(each, width),
            step_block(each, HD),
            step_block(each, HD),
            step_block(each, 1),
        ],
        out_specs=half_blocks(steps, each, model) + [whole_block(4 * width, model), whole_block(1, 3 * width)],
        out_shape=[
            jax.ShapeDtypeStruct((total // 2, model), BF),
            jax.ShapeDtypeStruct((total // 2, model), BF),
            jax.ShapeDtypeStruct((4 * width, model), BF),
            jax.ShapeDtypeStruct((1, 3 * width), F32),
        ],
        scratch_shapes=[
            pltpu.VMEM((each, 3 * width), BF),
            pltpu.VMEM((4 * width, model), F32),
        ],
        compiler_params=pltpu.CompilerParams(vmem_limit_bytes=56 << 20),
        cost_estimate=NO_COST,
    )(*waits, grad, h_one, weights, qkv, att, cosine, sine, start)


def gated(gate, up):
    logistic = jax.nn.sigmoid(gate)
    silu = gate * logistic
    return silu, silu * up, logistic * (1.0 + gate * (1.0 - logistic))


def routed_body(
    experts,
    rows_ref,
    up_ref,
    own_ref,
    router_ref,
    gate_w_ref,
    up_w_ref,
    down_w_ref,
    *rest,
):
    units_refs, rest = rest[:6], rest[6:]
    grad_rows_ref, grad_in_ref, high_ref, low_ref, row_gate_ref, total_ref, grads_ref, probs_ref, share_ref = rest
    part = pl.program_id(0)
    rows_in = rows_ref[...]
    each = rows_in.shape[0]
    here = pl.ds(pl.multiple_of(pl.program_id(1) * each, each), each)

    @pl.when(part == 0)
    def _():
        logits = dot(rows_in, router_ref[...], (1, 0))
        lane = lax.broadcasted_iota(jnp.int32, logits.shape, 1)
        logits = jnp.where(lane < experts, logits, -1e30)
        powers = jnp.exp(logits - jnp.max(logits, axis=1, keepdims=True))
        probs = powers / jnp.sum(powers, axis=1, keepdims=True)
        probs_ref[here] = probs
        gate = jnp.sum(probs * own_ref[...], axis=1, keepdims=True)
        row_gate_ref[...] = gate
        grad_rows = (gate * up_ref[...].astype(F32)).astype(BF)
        grad_rows_ref[...] = grad_rows
        grads_ref[here] = grad_rows

    gate_e = dot(rows_in, gate_w_ref[...], (1, 1))
    up_e = dot(rows_in, up_w_ref[...], (1, 1))
    silu, hidden, slope = gated(gate_e, up_e)
    hidden = hidden.astype(BF)
    grad_hidden = dot(grads_ref[here], down_w_ref[...], (1, 1))
    grad_gate = (grad_hidden * up_e * slope).astype(BF)
    grad_up = (grad_hidden * silu).astype(BF)
    for i in range(2):

        @pl.when(part == i)
        def _():
            for ref, made in zip(units_refs[3 * i :], (grad_gate, grad_up, hidden), strict=False):
                ref[...] = made

    share = jnp.sum(hidden.astype(F32) * grad_hidden, axis=1, keepdims=True)
    made = dot(grad_gate, gate_w_ref[...], (1, 0)) + dot(grad_up, up_w_ref[...], (1, 0))

    @pl.when(part == 0)
    def _():
        share_ref[here] = share
        total_ref[here] = made

    @pl.when(part > 0)
    def _():
        high, low = two_parts((share_ref[here] + share) * (own_ref[...] - probs_ref[here]))
        high_ref[...] = high
        low_ref[...] = low
        from_router = dot(high, router_ref[...], (1, 1)) + dot(low, router_ref[...], (1, 1))
        grad_in_ref[...] = (total_ref[here] + made + from_router).astype(BF)


def routed_expert(rows_in, up_rows, own, router, gate_w, up_w, down_w, experts, waits=()):
    total, model = rows_in.shape
    units = gate_w.shape[0]
    steps, parts = 2, 2
    each, part_units = total // steps, units // parts
    weight = pl.BlockSpec((part_units, model), lambda j, i: (j, 0))

    def by_rows(width, part=None):
        if part is None:
            return pl.BlockSpec((each, width), lambda j, i: (i, 0))
        if part == 0:
            return pl.BlockSpec((each, width), lambda j, i: (jnp.where(j == 0, i, steps - 1), 0))
        return pl.BlockSpec((each, width), lambda j, i: (jnp.where(j == 0, 0, i), 0))

    return pl.pallas_call(
        waiting(functools.partial(routed_body, experts), len(waits)),
        grid=(parts, steps),
        in_specs=[anywhere()] * len(waits)
        + [by_rows(model), by_rows(model), once_block(1, LANES), once_block(model, LANES)]
        + [weight] * 3,
        out_specs=[by_rows(part_units, 0)] * 3
        + [by_rows(part_units, 1)] * 3
        + [by_rows(model, 0), by_rows(model, 1)]
        + [by_rows(LANES, 1)] * 2
        + [by_rows(1, 0)],
        out_shape=[jax.ShapeDtypeStruct((total, part_units), BF)] * 6
        + [jax.ShapeDtypeStruct((total, model), BF)] * 2
        + [jax.ShapeDtypeStruct((total, LANES), BF)] * 2
        + [jax.ShapeDtypeStruct((total, 1), F32)],
        scratch_shapes=[
            pltpu.VMEM((total, model), F32),
            pltpu.VMEM((total, model), BF),
            pltpu.VMEM((total, LANES), F32),
            pltpu.VMEM((total, 1), F32),
        ],
        compiler_params=pltpu.CompilerParams(vmem_limit_bytes=60 << 20),
        cost_estimate=NO_COST,
    )(*waits, rows_in, up_rows, own, router, gate_w, up_w, down_w)


def routed_out_body(first_ref, second_ref, down_w_ref, row_gate_ref, out_ref):
    units = first_ref.shape[1]
    out = dot(first_ref[...], down_w_ref[:units], (1, 0))
    out += dot(second_ref[...], down_w_ref[units:], (1, 0))
    out_ref[...] = (row_gate_ref[...] * out.astype(BF).astype(F32)).astype(BF)


def routed_out(first, second, down_w, row_gate, waits=()):
    steps = 4
    total, model = first.shape[0], down_w.shape[1]
    each = model // steps
    return pl.pallas_call(
        waiting(routed_out_body, len(waits)),
        grid=(steps,),
        in_specs=[anywhere()] * len(waits)
        + [
            once_block(*first.shape),
            once_block(*second.shape),
            pl.BlockSpec((down_w.shape[0], each), lambda i: (0, i)),
            once_block(*row_gate.shape),
        ],
        out_specs=pl.BlockSpec((total, each), lambda i: (0, i)),
        out_shape=jax.ShapeDtypeStruct((total, model), BF),
        compiler_params=pltpu.CompilerParams(vmem_limit_bytes=40 << 20),
        cost_estimate=NO_COST,
    )(*waits, first, second, down_w, row_gate)


def shared_body(
    h_ref,
    up_ref,
    gate_up_w_ref,
    down_w_ref,
    mix_w_ref,
    kept_ref,
    given_ref,
    hidden_ref,
    grad_gate_ref,
    grad_up_ref,
    grad_out_ref,
    grad_mix_ref,
    mix_ref,
):
    units = down_w_ref.shape[0]
    h_in, mix_w = h_ref[...], mix_w_ref[...]
    mix = jax.nn.sigmoid(jnp.sum(h_in.astype(F32) * mix_w, axis=1, keepdims=True))
    mix_ref[...] = mix
    gate_s = dot(h_in, gate_up_w_ref[:units], (1, 1))
    up_s = dot(h_in, gate_up_w_ref[units:], (1, 1))
    silu, hidden, slope = gated(gate_s, up_s)
    hidden = hidden.astype(BF)
    hidden_ref[...] = hidden
    grad_out = (mix * up_ref[...].astype(F32)).astype(BF)
    grad_out_ref[...] = grad_out
    grad_hidden = dot(grad_out, down_w_ref[...], (1, 1))
    grad_gate = (grad_hidden * up_s * slope).astype(BF)
    grad_up = (grad_hidden * silu).astype(BF)
    grad_gate_ref[...] = grad_gate
    grad_up_ref[...] = grad_up
    grad_mix = jnp.sum(hidden.astype(F32) * grad_hidden, axis=1, keepdims=True) * (1.0 - mix)
    grad_mix_ref[...] = grad_mix
    made = dot(grad_gate, gate_up_w_ref[:units], (1, 0)) + dot(grad_up, gate_up_w_ref[units:], (1, 0))
    in_halves(kept_ref, given_ref, (made + grad_mix * mix_w).astype(BF))


def shared_expert(h_team, up_team, gate_up_w, down_w, mix_w, waits=()):
    total, model = h_team.shape
    units = down_w.shape[0]
    steps = 4
    each = total // steps
    return pl.pallas_call(
        waiting(shared_body, len(waits)),
        grid=(steps,),
        in_specs=[anywhere()] * len(waits)
        + [
            step_block(each, model),
            step_block(each, model),
            once_block(2 * units, model),
            once_block(units, model),
            once_block(1, model),
        ],
        out_specs=half_blocks(steps, each, model)
        + [step_block(each, units)] * 3
        + [step_block(each, model)]
        + [step_block(each, 1)] * 2,
        out_shape=[jax.ShapeDtypeStruct((total // 2, model), BF)] * 2
        + [jax.ShapeDtypeStruct((total, units), BF)] * 3
        + [jax.ShapeDtypeStruct((total, model), BF)]
        + [jax.ShapeDtypeStruct((total, 1), F32)] * 2,
        compiler_params=pltpu.CompilerParams(vmem_limit_bytes=56 << 20),
        cost_estimate=NO_COST,
    )(*waits, h_team, up_team, gate_up_w, down_w, mix_w)


def shared_out_body(hidden_ref, down_w_ref, mix_ref, kept_ref, given_ref):
    made = mix_ref[...] * dot(hidden_ref[...], down_w_ref[...], (1, 0))
    in_halves(kept_ref, given_ref, made.astype(BF))


def shared_out(hidden, down_w, mix, waits=()):
    total, units = hidden.shape
    model = down_w.shape[1]
    steps = 4
    each = total // steps
    return pl.pallas_call(
        waiting(shared_out_body, len(waits)),
        grid=(steps,),
        in_specs=[anywhere()] * len(waits)
        + [step_block(each, units), once_block(units, model), step_block(each, 1)],
        out_specs=half_blocks(steps, each, model),
        out_shape=[jax.ShapeDtypeStruct((total // 2, model), BF)] * 2,
        compiler_params=pltpu.CompilerParams(vmem_limit_bytes=40 << 20),
        cost_estimate=NO_COST,
    )(*waits, hidden, down_w, mix)


def nothing_body(*refs):
    del refs


def after(values_in, *others):
    return pl.pallas_call(
        nothing_body,
        in_specs=[anywhere()] * (1 + len(others)),
        out_specs=anywhere(),
        out_shape=jax.ShapeDtypeStruct(values_in.shape, values_in.dtype),
        input_output_aliases={0: 0},
        cost_estimate=NO_COST,
    )(values_in, *others)


def flip(values_in, axis, bit):
    size = lax.axis_size(axis)
    return lax.ppermute(values_in, axis, [(i, i ^ bit) for i in range(size)])


def shift(values_in, step):
    size = lax.axis_size(RING)
    return lax.ppermute(values_in, RING, [(i, (i + step) % size) for i in range(size)])


def shard_bits():
    bits, bit = [], lax.axis_size(SHARD) // 2
    while bit:
        bits.append(bit)
        bit //= 2
    return bits


def team_bits():
    bits = [(SHARD, bit) for bit in shard_bits()]
    return bits[:-1] + [(PAIR, 1)] + bits[-1:]


def team_order():
    order = [(0, 0)]
    for axis, bit in team_bits():
        order += [(p ^ bit, s) if axis == PAIR else (p, s ^ bit) for p, s in order]
    return order


def add_got(kept, given, axis, bit):
    return kept.astype(F32) + flip(given.astype(BF), axis, bit).astype(F32)


def halve(values_in, axis, bit):
    half = values_in.shape[0] // 2
    return add_got(values_in[:half], values_in[half:], axis, bit)


def team_sum(kept, given, held=None):
    bits = list(reversed(team_bits()))
    stages = [add_got(kept, given, *bits[0])]
    for i, (axis, bit) in enumerate(bits[1:]):
        ready = (held or {}).get(i, lambda: ())()
        stages.append(halve(after(stages[-1], *ready) if ready else stages[-1], axis, bit))
    return stages


def ring_gather(block):
    size = lax.axis_size(RING)
    ups, downs = [block], []
    up = down = block
    for k in range(1, size // 2 + 1):
        up = shift(up, 1)
        if k <= (size - 1) // 2:
            down = shift(down, -1)
            downs.append(down)
        ups.append(up)
        if k == 1 and downs:
            up = after(up, downs[0])
    return ups + downs


class RingSum:
    def __init__(self, blocks):
        size = lax.axis_size(RING)
        self.hops = size // 2
        self.back = list(blocks[1 : self.hops + 1])
        self.ahead = list(blocks[self.hops + 1 :])
        self.back_got = self.ahead_got = 0.0

    def running(self):
        back = [(self.back[-1].astype(F32) + self.back_got).astype(BF)]
        if len(self.back) == self.hops or not self.ahead:
            return back
        return back + [(self.ahead[-1].astype(F32) + self.ahead_got).astype(BF)]

    def hop(self, *ready):
        got = []
        for name, step, running in zip(("back", "ahead"), (-1, 1), self.running(), strict=False):
            getattr(self, name).pop()
            got.append(shift(after(running, *ready) if ready else running, step))
            setattr(self, name + "_got", got[-1].astype(F32))
        return got

    def total(self):
        while self.back or self.ahead:
            self.hop()
        return self.back_got + self.ahead_got


def ring_total(blocks):
    size = lax.axis_size(RING)
    total = blocks[0].astype(F32)
    if size > 4:
        others = RingSum(blocks).total()
        return total + others, (others,)
    offsets = [-k for k in range(1, size // 2 + 1)] + list(range(1, (size + 1) // 2))
    got = [shift(block, k) for k, block in zip(offsets, blocks[1:], strict=True)]
    return total + sum(one.astype(F32) for one in got), got


def pair_sum(own, other):
    return own.astype(F32) + flip(other.astype(BF), PAIR, 1).astype(F32)


def all_sum(values_in):
    for axis in (SHARD, PAIR, RING):
        bit = 1
        while bit < lax.axis_size(axis):
            values_in = values_in + flip(values_in, axis, bit)
            bit *= 2
    return values_in


def local(
    tokens,
    norm_attn,
    w_query,
    b_query,
    w_key,
    b_key,
    w_value,
    b_value,
    w_output,
    norm_ffn,
    w_router,
    shared_mix,
    shared_gate,
    shared_up,
    shared_down,
    expert_gate,
    expert_up,
    expert_down,
    routes,
    seq_lengths,
    cotangent,
):
    n_shard = lax.axis_size(SHARD)
    ring_at, pair_at, shard_at = (lax.axis_index(a) for a in (RING, PAIR, SHARD))
    expert_at = ring_at * 2 + pair_at
    group_rows, model = tokens.shape
    rows = group_rows // n_shard
    experts = w_router.shape[1]
    capacity = rows * TOP * 5 // (4 * experts)
    slot_rows = experts * capacity
    order = team_order()
    team = len(order)

    def block_of(values_in, flipped):
        return lax.dynamic_slice_in_dim(values_in, (shard_at ^ flipped) * rows, rows, 0)

    def halves(values_in):
        return values_in.reshape(2, values_in.shape[0] // 2, values_in.shape[1])

    def pair_units(parts):
        pack = jnp.concatenate([halves(part) for part in parts], axis=1)
        mine = lax.dynamic_index_in_dim(pack, pair_at, 0, keepdims=False)
        theirs = lax.dynamic_index_in_dim(pack, 1 - pair_at, 0, keepdims=False)
        got = flip(theirs, PAIR, 1)
        return jnp.where(
            pair_at == 0,
            jnp.concatenate([mine, got], axis=1),
            jnp.concatenate([got, mine], axis=1),
        )

    def gather_units(block):
        return lax.all_gather(block, RING, axis=1, tiled=True)

    def scatter_units(pack):
        return lax.psum_scatter(pack, RING, scatter_dimension=1, tiled=True)

    def unpair_units(summed, parts):
        width = summed.shape[1] // 2
        mine = lax.dynamic_slice_in_dim(summed, pair_at * width, width, 1)
        theirs = lax.dynamic_slice_in_dim(summed, (1 - pair_at) * width, width, 1)
        got = flip(theirs, PAIR, 1)
        first, second = jnp.where(pair_at == 0, mine, got), jnp.where(pair_at == 0, got, mine)
        n = summed.shape[0] // parts
        return [
            jnp.concatenate([first[i * n : (i + 1) * n], second[i * n : (i + 1) * n]], axis=0).astype(
                F32
            )
            for i in range(parts)
        ]

    attn_block = pair_units([w_query.T, w_key.T, w_value.T, w_output])
    attn_w = gather_units(attn_block)
    width_here = attn_w.shape[0] // 4
    heads_here = width_here // HD
    gate_up_block = pair_units([shared_gate.T, shared_up.T])
    down_block = pair_units([shared_down])

    shared_gate_up = gather_units(gate_up_block)
    shared_down_w = gather_units(down_block)

    def far_rows(block, hold=lambda i, joined: joined):
        far = [block]
        for i, bit in enumerate(shard_bits()):
            got = flip(hold(i, jnp.concatenate(far, axis=0)), SHARD, bit)
            far += [got[i * rows : (i + 1) * rows] for i in range(len(far))]
        return dict(zip([s for p, s in order if p == 1], far, strict=True))

    def team_rows(near, far):
        return jnp.concatenate([far[s] if p else near[s] for p, s in order], axis=0)

    near = {s: block_of(tokens, s) for p, s in order if p == 0}
    def shard_gather(parts):
        for bit in shard_bits()[1:]:
            parts = parts + [flip(one, SHARD, bit) for one in parts]
        return jnp.concatenate(parts, axis=0)

    first_bit = shard_bits()[0]
    far = far_rows(flip(near[0], PAIR, 1))
    gate_part = after(expert_gate[0].T, far[first_bit])
    gate_parts = [gate_part, flip(gate_part, SHARD, first_bit)]
    up_part = after(expert_up[0].T, gate_parts[1])
    up_parts = [up_part, flip(up_part, SHARD, first_bit)]
    gate_w, up_w = shard_gather(gate_parts), shard_gather(up_parts)
    tokens_team = team_rows(near, far)
    resid_in = near[0].astype(F32)

    ring_size = experts // 2
    slots = ring_size * capacity
    routes_in = jnp.concatenate(ring_gather(routes.T), axis=1)
    places = jnp.arange(ring_size * rows, dtype=jnp.int32)
    ahead = (jnp.arange(ring_size, dtype=jnp.int32) - ring_at + ring_size) % ring_size
    listed = jnp.where(
        ahead == 0, 0, jnp.where(ahead >= ring_size // 2, ring_size - ahead, ring_size // 2 + ahead)
    )

    def taking_of(expert):
        chosen = jnp.any(routes_in == expert, axis=0)
        slot = jnp.sum(
            jnp.where((places[None, :] < places[:, None]) & chosen[None, :], 1, 0), axis=1
        )
        slot = jnp.where(chosen, slot, -1)
        in_ring = jnp.take(slot.reshape(ring_size, rows), listed, axis=0).reshape(-1)
        ids = jnp.arange(slots, dtype=jnp.int32)[:, None]
        return (slot[None, :] == ids).astype(BF), (in_ring[None, :] == ids).astype(BF)

    take_own, take_own_up = taking_of(expert_at)
    take_other, take_other_up = taking_of(expert_at + 1 - 2 * pair_at)

    up_near = {s: block_of(cotangent, s) for p, s in order if p == 0}
    upstream = up_near[0].astype(F32)
    up_ring = lax.all_gather(after(up_near[0], attn_block), RING, axis=0, tiled=True)
    up_far = flip(up_near[0], PAIR, 1)
    up_own = dot(take_own_up, up_ring, (1, 0)).astype(BF)
    up_other = flip(dot(take_other_up, up_ring, (1, 0)).astype(BF), PAIR, 1)
    def team_gather(own, other, *ready):
        first = shard_bits()[0]
        both = jnp.concatenate([own, other], axis=0)
        got = flip(after(both, *ready) if ready else both, SHARD, first)
        rows_here = jnp.concatenate([own, got[:rows], other, got[rows:]], axis=0)
        return jnp.concatenate([rows_here, flip(rows_here, SHARD, shard_bits()[1])], axis=0)

    def shard_sums(kept, given):
        last, first = shard_bits()[-1], shard_bits()[0]
        summed = add_got(kept, given, SHARD, last)
        split = summed.reshape(2, 2, rows, model)
        sent = split[:, 1].astype(BF)
        done = add_got(split[:, 0], sent, SHARD, first)
        return sent, done.reshape(2 * rows, model)

    far_lengths = flip(seq_lengths, PAIR, 1)
    lengths = jnp.stack(
        [
            lax.dynamic_index_in_dim(far_lengths if p else seq_lengths, shard_at ^ s, 0, False)
            for p, s in order
        ]
    )
    positions = jax.vmap(lambda row: seq_positions(row, rows))(lengths)
    cosine, sine = (table.reshape(team * rows, HD) for table in rope_tables(positions, HD))
    start = (jnp.arange(rows, dtype=jnp.int32)[None, :] - positions).reshape(team * rows, 1)
    resid_team = tokens_team.astype(F32)
    gain_one = norm_attn.astype(F32)
    inv_one_team = lax.rsqrt(jnp.mean(resid_team * resid_team, axis=1, keepdims=True) + epsilon)
    h_one = (resid_team * inv_one_team * gain_one).astype(BF)
    head_start = (shard_at * 2 + pair_at) * width_here
    qkv_b = jnp.concatenate(
        [lax.dynamic_slice_in_dim(b, head_start, width_here, 0) for b in (b_query, b_key, b_value)]
    ).astype(F32)[None]
    attn_kept, attn_given, qkv, attended = attention_forward(
        h_one,
        attn_w,
        qkv_b,
        cosine,
        sine,
        start,
        rows,
        heads_here,
        ATTN_STEPS,
        (gate_parts[1], up_far, gate_up_block, down_block, take_own, take_other, take_own_up, take_other_up),
    )
    attn_out = team_sum(attn_kept, attn_given, {1: lambda: (up_parts[1],)})[-1]
    down_part = after(expert_down[0], attn_out)
    down_parts = [down_part, flip(down_part, SHARD, first_bit)]
    down_w = shard_gather(down_parts)

    up_far = far_rows(after(up_far, attn_out))
    up_team = team_rows(up_near, up_far)
    up_rows = jnp.concatenate([up_own, up_other], axis=0)

    x_two = resid_in + attn_out
    gain_two = norm_ffn.astype(F32)
    inv_two = lax.rsqrt(jnp.mean(x_two * x_two, axis=1, keepdims=True) + epsilon)
    h_two = (x_two * inv_two * gain_two).astype(BF)

    h_ring = ring_gather(h_two)
    h_team = team_gather(h_two, flip(h_two, PAIR, 1), h_ring[1], h_ring[-1])
    h_ring = after(jnp.concatenate(h_ring, axis=0), up_other, down_parts[1])
    rows_other = flip(dot(take_other, h_ring, (1, 0)).astype(BF), PAIR, 1)
    rows_in = jnp.concatenate([dot(take_own, h_ring, (1, 0)).astype(BF), rows_other], axis=0)

    own_expert = (jnp.arange(LANES, dtype=jnp.int32) == expert_at).astype(F32)[None]
    router_wide = jnp.pad(w_router, ((0, 0), (0, LANES - experts)))
    *units, grad_rows, grad_inputs, high, low, row_gate = routed_expert(
        rows_in, up_rows, own_expert, router_wide, gate_w, up_w, down_w, experts
    )
    kept_units, given_units = units[:3], units[3:]

    def returned(values_in, *ready):
        got = flip(values_in[slots:], PAIR, 1)
        own = after(values_in[:slots], *ready)
        made = (dot(take_own, own, (0, 0)) + dot(take_other, got, (0, 0))).astype(BF)
        return [made[i * rows : (i + 1) * rows] for i in range(ring_size)]

    def expert_products(units, across):
        return dot(units, across, (0, 0)).astype(BF)

    across = (rows_in, rows_in, grad_rows)

    mix_w = shared_mix.astype(F32)[None]
    (
        share_kept,
        share_given,
        hidden_s,
        grad_gate_s,
        grad_up_s,
        grad_out_s,
        grad_mix,
        mix_team,
    ) = shared_expert(
        h_team, up_team, shared_gate_up, shared_down_w, mix_w, (grad_inputs,)
    )
    grad_returned = returned(grad_inputs, share_given)

    def from_team(shared_rows):
        return pair_sum(shared_rows[:rows], shared_rows[rows:])

    share_stages = shard_sums(share_kept, share_given)
    grad_ring, ring_got = ring_total(grad_returned)
    grad_h_two = grad_ring + from_team(share_stages[-1])
    grad_x_two = norm_back(grad_h_two, x_two, inv_two, gain_two, upstream)
    grad_norm_ffn = jnp.sum(grad_h_two * x_two * inv_two, axis=0)

    grad_gate_s, grad_up_s, grad_out_s = (
        after(one, share_stages[0], *grad_returned[1:]) for one in (grad_gate_s, grad_up_s, grad_out_s)
    )
    shared_grad_pack = jnp.concatenate(
        [
            dot(grad_gate_s, h_team, (0, 0)).astype(BF),
            dot(grad_up_s, h_team, (0, 0)).astype(BF),
            dot(hidden_s, grad_out_s, (0, 0)).astype(BF),
        ],
        axis=0,
    )
    shared_grad_pack = after(shared_grad_pack, *ring_got, share_stages[-1])
    shared_summed = scatter_units(shared_grad_pack)
    mix_parts = jnp.concatenate(two_parts(grad_mix), axis=1)
    grad_mix_w = jnp.sum(dot(mix_parts, h_team, (0, 0)), axis=0)

    last_shard = shard_bits()[-1]
    ready = (shared_grad_pack,)
    expert_sums, given_grads = [], []
    for i in range(3):
        given_grads.append(expert_products(after(given_units[i], *ready), across[i]))
        kept = expert_products(after(kept_units[i], given_grads[-1]), across[i])
        expert_sums.append(add_got(kept, given_grads[-1], SHARD, last_shard))
        ready = (expert_sums[-1],)
        if i == 0:
            out_made = routed_out(kept_units[2], given_units[2], down_w, row_gate, ready)
            ready = (out_made,)
    out_kept, out_given = shared_out(hidden_s, shared_down_w, mix_team, ready)
    grad_router = (dot(high, rows_in, (0, 0)) + dot(low, rows_in, (0, 0)))[:experts]
    first, second, third = expert_sums
    grad_attn = grad_x_two.astype(BF)
    grad_other = flip(grad_attn, PAIR, 1)
    out_returned = returned(after(out_made, grad_other), grad_other)
    out_ring = RingSum(out_returned)
    out_ring.hop()
    grad_attn = team_gather(grad_attn, grad_other)
    units_half = first.shape[0] // 2
    sent = [one[units_half:].astype(BF) for one in (first, second, third)]
    sent = [after(one, grad_attn) for one in sent]
    grad_kept, grad_given, attn_grad_pack, grad_qkv_b = attention_backward(
        grad_attn, h_one, attn_w, qkv, attended, cosine, sine, start, rows, heads_here, ATTN_BACK_STEPS, (out_given, *sent, *out_returned[1:])
    )
    attn_grad_pack = after(attn_grad_pack, shared_summed)
    attn_summed = scatter_units(attn_grad_pack)
    grad_given = after(grad_given, attn_grad_pack)
    first, second, third = (
        add_got(after(one[:units_half], grad_kept), other, SHARD, first_bit)
        for one, other in zip((first, second, third), sent, strict=True)
    )
    grad_h_one = team_sum(
        grad_kept, grad_given, {0: lambda: (first, second, third)}
    )[-1]
    inv_one = lax.rsqrt(jnp.mean(resid_in * resid_in, axis=1, keepdims=True) + epsilon)
    grad_norm_attn = jnp.sum(grad_h_one * resid_in * inv_one, axis=0)
    grad_tokens = norm_back(grad_h_one, resid_in, inv_one, gain_one, grad_x_two)

    out_s = shard_sums(out_kept, after(out_given, attn_grad_pack))[-1]
    out_routed = out_returned[0].astype(F32) + out_ring.total()
    block_out = (x_two + out_routed + from_team(out_s)).astype(BF)

    grad_expert_gate, grad_expert_up, grad_expert_down = first, second, third
    grad_shared_gate, grad_shared_up, grad_shared_down = unpair_units(shared_summed, 3)
    grad_query_w, grad_key_w, grad_value_w, grad_output_w = unpair_units(attn_summed, 4)
    grad_qkv_b = lax.dynamic_update_slice_in_dim(
        jnp.zeros((3, b_query.shape[0]), F32), grad_qkv_b.reshape(3, width_here), head_start, 1
    )
    small = all_sum(
        jnp.concatenate(
            [
                grad_qkv_b,
                jnp.stack([grad_norm_attn, grad_norm_ffn, grad_mix_w]),
                grad_router,
            ],
            axis=0,
        )
    )
    return (
        block_out,
        grad_tokens,
        small[3],
        grad_query_w.T,
        small[0],
        grad_key_w.T,
        small[1],
        grad_value_w.T,
        small[2],
        grad_output_w,
        small[4],
        small[6:].T,
        small[5],
        grad_shared_gate.T,
        grad_shared_up.T,
        grad_shared_down,
        grad_expert_gate.T[None],
        grad_expert_up.T[None],
        grad_expert_down[None],
    )


def solution(mesh):
    experts, shards = mesh.shape["expert"], mesh.shape["shard"]
    grid = jax.sharding.Mesh(
        mesh.devices.reshape(experts // 2, 2, shards), (RING, PAIR, SHARD)
    )
    expert = (RING, PAIR)
    every = (RING, PAIR, SHARD)
    return jax.shard_map(
        local,
        mesh=grid,
        in_specs=(
            P(expert, None),
            P(),
            P(expert, SHARD),
            P(),
            P(expert, SHARD),
            P(),
            P(expert, SHARD),
            P(),
            P(SHARD, expert),
            P(),
            P(),
            P(),
            P(expert, SHARD),
            P(expert, SHARD),
            P(SHARD, expert),
            P(expert, None, SHARD),
            P(expert, None, SHARD),
            P(expert, SHARD, None),
            P(every, None),
            P(expert, None),
            P(expert, None),
        ),
        out_specs=(
            P(every, None),
            P(every, None),
            P(),
            P(expert, SHARD),
            P(),
            P(expert, SHARD),
            P(),
            P(expert, SHARD),
            P(),
            P(SHARD, expert),
            P(),
            P(),
            P(),
            P(expert, SHARD),
            P(expert, SHARD),
            P(SHARD, expert),
            P(expert, None, SHARD),
            P(expert, None, SHARD),
            P(expert, SHARD, None),
        ),
        check_vma=False,
    )
```

time: 1090 us -> 924 us (0.85)
  Pallas kernels: 0 us -> 147 us
  waiting for transfers between devices: 431 us -> 294 us
  matrix products: 215 us -> 88.6 us
  starting transfers between devices: 154 us -> 76.7 us
  other arithmetic: 97.4 us -> 141 us
  local copies, waits for them, and re-layouts: 164 us -> 153 us
    pallas_call x0 -> x39, Pallas kernels: none -> 147 us  [the longest x1 46.9 us: routed_expert(): pl.pallas_call(waiting(functools.partial(routed_body, experts), len(waits...]
    dot_general x30 -> x20, matrix products: 185 us -> 88.6 us  [dot(): lax.dot_general(left, right, (((contract[0],), (contract[1],)), ((), ()))...]
    ppermute x15 -> x12, starting transfers between devices: 103 us -> 27.6 us  [shift(): lax.ppermute(values_in, RING, [(i, (i + step) % size) for i in range(size)])]
    all_gather x2 -> x3, waiting for transfers between devices: 51.7 us -> 0.01 us  [gather_units(): return lax.all_gather(block, RING, axis=1, tiled=True)]
    ppermute x59 -> x54, waiting for transfers between devices: 280 us -> 238 us  [flip(): return lax.ppermute(values_in, axis, [(i, i ^ bit) for i in range(size)])]
    ppermute x15 -> x12, waiting for transfers between devices: 91.9 us -> 55.1 us  [shift(): lax.ppermute(values_in, RING, [(i, (i + step) % size) for i in range(size)])]
    gather x4 -> x2, local copies, waits for them, and re-layouts: 35.7 us -> 1.12 us  [taking_of(): jnp.take(slot.reshape(ring_size, rows), listed, axis=0).reshape(-1)]
    concatenate x11 -> x14, other arithmetic: 20.1 us -> 46.9 us  [the longest x3 20.7 us: shard_gather(): return jnp.concatenate(parts, axis=0)]
  transfers between devices with their start and end apart: 78 -> 72, of which waited for: 34 -> 29; matrix products, arithmetic and copies ran while one was open for 33% -> 36% of each run, Pallas kernels for 0% -> 16%
where the time goes in v2:
time: 924 us; the launch traced here: 916 us
  waiting for transfers between devices  294 us (32%)
  local copies, waits for them, and re-layouts  153 us (17%)
  Pallas kernels  147 us (16%)
  other arithmetic  141 us (15%)
  matrix products  88.6 us (10%)
  starting transfers between devices  76.7 us (8%)
  between operations  15.8 us (2%)
    ppermute x54, waiting for transfers between devices, flip(): return lax.ppermute(values_in, axis, [(i, i ^ bit) for i in range(size)])  238 us
    dot_general x20, matrix products, dot(): lax.dot_general(left, right, (((contract[0],), (contract[1],)), ((), ()))...  88.6 us
    unnamed x288, local copies, waits for them, and re-layouts  85.7 us
    ppermute x12, waiting for transfers between devices, shift(): lax.ppermute(values_in, RING, [(i, (i + step) % size) for i in range(size)])  55.1 us
    ppermute x54, starting transfers between devices, flip(): return lax.ppermute(values_in, axis, [(i, i ^ bit) for i in range(size)])  48.4 us
    pallas_call x1, Pallas kernels, routed_expert(): pl.pallas_call(waiting(functools.partial(routed_body, experts), len(waits...  46.9 us
    add x13, other arithmetic, add_got(): return kept.astype(F32) + flip(given.astype(BF), axis, bit).astype(F32)  42.4 us
    pallas_call x1, Pallas kernels, attention_backward(): pl.pallas_call(waiting(functools.partial(attention_backward_body, rows, h...  35.2 us
  transfers between devices with their start and end apart: 72, of which 29 were waited for; matrix products, arithmetic and copies ran while one was open for 36% of the time, Pallas kernels for 16%

profile of v2, /device:TPU:0, one launch (start us, length us, event | category | flops | bytes accessed | tf_op | source)
XLA Modules:
  0.0 915.7 jit_solution(6401038062994237453)
XLA Ops:
  15.9 11.9 %collective-permute-done.10 = bf16[1024,256]{1,0:T(8,128)(2,1)S(1)} collective-permute-done((bf16[1024,256]{1,0:T(8,128)(2,1)S(1)}, bf16[1024,256]{1,0:T(8,128)(2,1)S(1)}, u32[]{:S(2)}, u32[]{:S(2)}) %collective-permute-start.10) | collective-permute-done | bytes 524320 | tf_op jit(solution)/shard_map/ppermute | solution.py:507
  54.8 3.6 fusion.44
  72.5 6.4 collective-permute-done.1.refs_1_
  81.4 6.2 collective-permute-done.5
  103.9 3.7 fusion
  108.0 3.5 fusion.2.refs_8_
  111.5 13.8 %collective-permute-done.2.refs_0_.refs_1_ = bf16[352,2048]{1,0:T(8,128)(2,1)S(1)} collective-permute-done((bf16[352,2048]{1,0:T(8,128)(2,1)}, bf16[352,2048]{1,0:T(8,128)(2,1)S(1)}, u32[]{:S(2)}, u32[]{:S(2)}) %collective-permute-start.2) | collective-permute-done | bytes 1441824 | tf_op jit(solution)/shard_map/ppermute | solution.py:507
  134.4 17.7 %shard_map.350 = (bf16[640,2048]{1,0:T(8,128)(2,1)S(1)}, bf16[640,2048]{1,0:T(8,128)(2,1)}, bf16[1280,768]{1,0:T(8,128)(2,1)S(1)}, bf16[1280,256]{1,0:T(8,128)(2,1)S(1)}) custom-call(bf16[352,2048]{1,0:T(8,128)(2,1)S(1)} %collective-permute-done.2.refs_0_.refs_1_, bf16[160,2048]{1,0:T(8,128)(2,1)S(1)} %collective-permute-done.3.refs_1_.refs_0_, ...), custom_call_target="tpu_custom_call" | custom-call | tf_op jit(solution)/shard_map/pallas_call | solution.py:208
  160.9 3.6 convert_add_fusion.6
  174.1 15.9 %collective-permute-done.14.refs_1_ = bf16[352,2048]{1,0:T(8,128)(2,1)} collective-permute-done((bf16[352,2048]{1,0:T(8,128)(2,1)}, bf16[352,2048]{1,0:T(8,128)(2,1)}, u32[]{:S(2)}, u32[]{:S(2)}) %collective-permute-start.14) | collective-permute-done | bytes 1441824 | tf_op jit(solution)/shard_map/ppermute | solution.py:507
  190.0 10.0 %pad_maximum_fusion.1.refs_4_ = bf16[1408,2048]{1,0:T(8,128)(2,1)} fusion(bf16[352,2048]{1,0:T(8,128)(2,1)} %collective-permute-done.23, bf16[352,2048]{1,0:T(8,128)(2,1)} %collective-permute-done.22, bf16[352,2048]{1,0:T(8,128)(2,1)S(1)} %copy-done.4, bf16[352,2048]{1,0:T(8,128)(2,1)S(1)} %copy-done.46), kind=kLoop, calls=%fused_computation.8 | loop fusion | flops 23068672 | bytes 11534336 | tf_op jit(solution)/shard_map/concatenate | solution.py:715
  200.0 4.1 slice_add_fusion.1.refs_0_
  206.9 4.5 convolution_convert_fusion.12
  215.6 7.1 collective-permute-done.15
  226.5 3.8 collective-permute-start.17
  230.3 5.4 pad_maximum_fusion.2.refs_5_
  237.2 26.4 %collective-permute-done.28 = bf16[160,2048]{1,0:T(8,128)(2,1)S(1)} collective-permute-done((bf16[160,2048]{1,0:T(8,128)(2,1)S(1)}, bf16[160,2048]{1,0:T(8,128)(2,1)S(1)}, u32[]{:S(2)}, u32[]{:S(2)}) %collective-permute-start.28) | collective-permute-done | bytes 655392 | tf_op jit(solution)/shard_map/ppermute | solution.py:507
  265.4 18.5 %collective-permute-done.17.refs_1_.refs_2_ = bf16[160,2048]{1,0:T(8,128)(2,1)} collective-permute-done((bf16[160,2048]{1,0:T(8,128)(2,1)S(1)}, bf16[160,2048]{1,0:T(8,128)(2,1)}, u32[]{:S(2)}, u32[]{:S(2)}) %collective-permute-start.17) | collective-permute-done | bytes 655392 | tf_op jit(solution)/shard_map/ppermute | solution.py:512
  285.4 4.1 pad_maximum_fusion.7.refs_1_
  303.5 21.5 %collective-permute-done.29 = bf16[320,2048]{1,0:T(8,128)(2,1)} collective-permute-done((bf16[320,2048]{1,0:T(8,128)(2,1)}, bf16[320,2048]{1,0:T(8,128)(2,1)}, u32[]{:S(2)}, u32[]{:S(2)}) %collective-permute-start.29) | collective-permute-done | bytes 1310752 | tf_op jit(solution)/shard_map/ppermute | solution.py:507
  327.4 4.0 fusion.6
  332.1 3.3 convolution_convert_fusion.10
  341.5 5.3 pad_maximum_fusion.3.refs_6_.refs_3_
  346.8 27.0 %collective-permute-done.21 = bf16[400,2048]{1,0:T(8,128)(2,1)S(1)} collective-permute-done((bf16[400,2048]{1,0:T(8,128)(2,1)S(1)}, bf16[400,2048]{1,0:T(8,128)(2,1)S(1)}, u32[]{:S(2)}, u32[]{:S(2)}) %collective-permute-start.21) | collective-permute-done | bytes 1638432 | tf_op jit(solution)/shard_map/ppermute | solution.py:507
  376.9 46.9 %shard_map.357 = (bf16[800,704]{1,0:T(8,128)(2,1)}, bf16[800,704]{1,0:T(8,128)(2,1)}, bf16[800,704]{1,0:T(8,128)(2,1)}, bf16[800,704]{1,0:T(8,128)(2,1)}, bf16[8...) custom-call(bf16[800,2048]{1,0:T(8,128)(2,1)} %pad_maximum_fusion.6., ...), custom_call_target="tpu_custom_call" | custom-call | tf_op jit(solution)/shard_map/pallas_call | solution.py:348
  423.7 3.4 fusion.55
  431.1 3.6 constant_dynamic-update-slice_fusion.4.refs_1_
  434.7 33.4 %shard_map.360 = (bf16[640,2048]{1,0:T(8,128)(2,1)}, bf16[640,2048]{1,0:T(8,128)(2,1)}, bf16[1280,704]{1,0:T(8,128)(2,1)}, bf16[1280,704]{1,0:T(8,128)(2,1)}, bf...) custom-call(bf16[800,2048]{1,0:T(8,128)(2,1)} %get-tuple-element.53.refs_0_, ...), custom_call_target="tpu_custom_call" | custom-call | tf_op jit(solution)/shard_map/pallas_call | solution.py:444
  474.3 12.4 %collective-permute-start.35 = (bf16[160,2048]{1,0:T(8,128)(2,1)}, bf16[160,2048]{1,0:T(8,128)(2,1)}, u32[]{:S(2)}, u32[]{:S(2)}) collective-permute-start(bf16[160,2048]{1,0:T(8,128)(2,1)} %get-tuple-element.186.refs_2_), channel_id=1, source_target_pairs={{0,24},{8,0},{16,8},{24,16},{1,25},{9,1},{17,9},{25,17},{2,26},{10... | collective-permute-start | bytes 1966088 | tf_op jit(solution)/shard_map/ppermute | solution.py:512
  496.1 8.6 convolution_convert_fusion.8
  504.7 8.6 convolution_convert_fusion.7
  514.8 6.6 convolution_convert_fusion.6
  521.5 4.5 pad_maximum_fusion.refs_0_
  526.0 4.1 fusion.8
  530.0 14.0 %collective-permute-done.36.refs_2_ = bf16[160,2048]{1,0:T(8,128)(2,1)} collective-permute-done((bf16[160,2048]{1,0:T(8,128)(2,1)}, bf16[160,2048]{1,0:T(8,128)(2,1)}, u32[]{:S(2)}, u32[]{:S(2)}) %collective-permute-start.36) | collective-permute-done | bytes 655392 | tf_op jit(solution)/shard_map/ppermute | solution.py:512
  549.2 7.2 convolution_convert_fusion.5.refs_1_
  563.2 3.4 multiply_reduce_fusion
  574.2 5.0 convolution_convert_fusion.4
  579.2 6.1 collective-permute-done.41.refs_1_
  590.9 8.7 shard_map.368.refs_0_.refs_1_
  601.4 7.1 convolution_convert_fusion.3.refs_1_
  610.5 5.1 collective-permute-done.48
  619.3 4.0 fusion.54
  626.7 4.7 convolution_convert_fusion.2
  631.4 5.4 convert_add_fusion.1.refs_1_
  638.7 5.9 convolution_convert_fusion.1.refs_1_
  645.8 16.1 %collective-permute-done.42 = bf16[400,2048]{1,0:T(8,128)(2,1)} collective-permute-done((bf16[400,2048]{1,0:T(8,128)(2,1)}, bf16[400,2048]{1,0:T(8,128)(2,1)}, u32[]{:S(2)}, u32[]{:S(2)}) %collective-permute-start.42) | collective-permute-done | bytes 1638432 | tf_op jit(solution)/shard_map/ppermute | solution.py:507
  668.3 3.5 constant_dynamic-update-slice_fusion.13.refs_1_.refs_7_
  676.4 3.7 convolution_reduce_fusion
  686.9 20.9 %collective-permute-done.43 = bf16[160,2048]{1,0:T(8,128)(2,1)S(1)} collective-permute-done((bf16[160,2048]{1,0:T(8,128)(2,1)S(1)}, bf16[160,2048]{1,0:T(8,128)(2,1)S(1)}, u32[]{:S(2)}, u32[]{:S(2)}) %collective-permute-start.43) | collective-permute-done | bytes 655392 | tf_op jit(solution)/shard_map/ppermute | solution.py:512
  712.4 3.9 slice.301.refs_0_
  716.3 5.1 convert_add_fusion.refs_0_
  728.7 5.3 shard_map.375
  737.0 35.2 %shard_map.379 = (bf16[640,2048]{1,0:T(8,128)(2,1)}, bf16[640,2048]{1,0:T(8,128)(2,1)}, bf16[1024,2048]{1,0:T(8,128)(2,1)}, f32[1,768]{1,0:T(1,128)}) custom-call(bf16[640,2048]{1,0:T(8,128)(2,1)} %copy-done.10, bf16[352,2048]{1,0:T(8,128)(2,1)} %shard_map.376.refs_1_, bf16[352,2048]{1,0:T(8,128)(2,1)} %shard_map.377.refs_2_, ...), custom_call_target="tpu_custom_call" | custom-call | tf_op jit(solution)/shard_map/pallas_call | solution.py:235
  784.5 3.7 slice.302.refs_0_
  789.1 4.5 convert_add_fusion.7.refs_3_
  793.5 12.2 %collective-permute-done.65 = bf16[2112,256]{1,0:T(8,128)(2,1)} collective-permute-done((bf16[2112,256]{1,0:T(8,128)(2,1)}, bf16[2112,256]{1,0:T(8,128)(2,1)}, u32[]{:S(2)}, u32[]{:S(2)}) %collective-permute-start.65) | collective-permute-done | bytes 1081376 | tf_op jit(solution)/shard_map/ppermute | solution.py:507
  807.4 5.0 convert_add_fusion.3.refs_0_
  822.7 21.4 %collective-permute-done.57 = bf16[320,2048]{1,0:T(8,128)(2,1)S(1)} collective-permute-done((bf16[320,2048]{1,0:T(8,128)(2,1)S(1)}, bf16[320,2048]{1,0:T(8,128)(2,1)S(1)}, u32[]{:S(2)}, u32[]{:S(2)}) %collective-permute-start.57) | collective-permute-done | bytes 1310752 | tf_op jit(solution)/shard_map/ppermute | solution.py:507
  845.4 5.3 collective-permute-done.51
  852.8 9.6 %collective-permute-done.58 = bf16[160,2048]{1,0:T(8,128)(2,1)S(1)} collective-permute-done((bf16[160,2048]{1,0:T(8,128)(2,1)S(1)}, bf16[160,2048]{1,0:T(8,128)(2,1)S(1)}, u32[]{:S(2)}, u32[]{:S(2)}) %collective-permute-start.58) | collective-permute-done | bytes 655392 | tf_op jit(solution)/shard_map/ppermute | solution.py:507
  873.5 3.9 fusion.21
  886.0 4.3 collective-permute-done.63
  893.4 10.0 %collective-permute-done.64 = bf16[1024,256]{1,0:T(8,128)(2,1)S(1)} collective-permute-done((bf16[1024,256]{1,0:T(8,128)(2,1)S(1)}, bf16[1024,256]{1,0:T(8,128)(2,1)S(1)}, u32[]{:S(2)}, u32[]{:S(2)}) %collective-permute-start.64) | collective-permute-done | bytes 524320 | tf_op jit(solution)/shard_map/ppermute | solution.py:507
  (583 shorter events, 286.4 us)
Async XLA Ops:
  7.2 118.1 %all-gather.5.cloned.1.call-start = ((), (), s32[]{:S(2)}) async-start(), calls=%async_computation.2 | async-start | bytes 5242880 | tf_op jit(solution)/shard_map/all_gather | solution.py:672
  12.9 15.0 %collective-permute-start.10 = (bf16[1024,256]{1,0:T(8,128)(2,1)S(1)}, bf16[1024,256]{1,0:T(8,128)(2,1)S(1)}, u32[]{:S(2)}, u32[]{:S(2)}) collective-permute-start(bf16[1024,256]{1,0:T(8,128)(2,1)S(1)} %get-tuple-element.204), channel_id=1, source_target_pairs={{0,4},{4,0},{1,5},{5,1},{2,6},{6,2},{3,7},{7,3},{8,12},{12,8},{9,1... | collective-permute-start | bytes 1572872 | tf_op jit(solution)/shard_map/ppermute | solution.py:507
  29.1 177.9 %all-gather.7.cloned.1.call-start = ((), (), s32[]{:S(2)}) async-start(), calls=%async_computation.3 | async-start | bytes 3276800 | tf_op jit(solution)/shard_map/all_gather | solution.py:751
  29.1 29.3 %collective-permute-start.6 = (s32[4,160]{1,0:T(4,128)S(1)}, s32[4,160]{1,0:T(4,128)S(1)}, u32[]{:S(2)}, u32[]{:S(2)}) collective-permute-start(s32[4,160]{1,0:T(4,128)S(1)} %bitcast.157), channel_id=1, source_target_pairs={{0,8},{8,16},{16,24},{24,0},{1,9},{9,17},{17,25},{25,1},{2,10},{10... | collective-permute-start | bytes 7688 | tf_op jit(solution)/shard_map/ppermute | solution.py:512
  31.0 28.4 %collective-permute-start.7 = (s32[4,160]{1,0:T(4,128)S(1)}, s32[4,160]{1,0:T(4,128)S(1)}, u32[]{:S(2)}, u32[]{:S(2)}) collective-permute-start(s32[4,160]{1,0:T(4,128)S(1)} %bitcast.158), channel_id=1, source_target_pairs={{0,24},{8,0},{16,8},{24,16},{1,25},{9,1},{17,9},{25,17},{2,26},{10... | collective-permute-start | bytes 7688 | tf_op jit(solution)/shard_map/ppermute | solution.py:512
  34.9 32.8 %collective-permute-start = (bf16[160,2048]{1,0:T(8,128)(2,1)S(1)}, bf16[160,2048]{1,0:T(8,128)(2,1)}, u32[]{:S(2)}, u32[]{:S(2)}) collective-permute-start(bf16[160,2048]{1,0:T(8,128)(2,1)S(1)} %get-tuple-element.163), channel_id=1, source_target_pairs={{0,4},{4,0},{1,5},{5,1},{2,6},{6,2},{3,7},{7,3},{8,12},{12,8},{9,1... | collective-permute-start | bytes 1966088 | tf_op jit(solution)/shard_map/ppermute | solution.py:507
  36.6 16.1 %collective-permute-start.11 = (s32[4,8]{1,0:T(4,128)S(1)}, s32[4,8]{1,0:T(4,128)S(1)}, u32[]{:S(2)}, u32[]{:S(2)}) collective-permute-start(s32[4,8]{1,0:T(4,128)S(1)} %copy-done.121), channel_id=1, source_target_pairs={{0,4},{4,0},{1,5},{5,1},{2,6},{6,2},{3,7},{7,3},{8,12},{12,8},{9,1... | collective-permute-start | bytes 392 | tf_op jit(solution)/shard_map/ppermute | solution.py:507
  39.3 72.2 %collective-permute-start.3 = (bf16[160,2048]{1,0:T(8,128)(2,1)}, bf16[160,2048]{1,0:T(8,128)(2,1)S(1)}, u32[]{:S(2)}, u32[]{:S(2)}) collective-permute-start(bf16[160,2048]{1,0:T(8,128)(2,1)} %get-tuple-element.169), channel_id=1, source_target_pairs={{0,4},{4,0},{1,5},{5,1},{2,6},{6,2},{3,7},{7,3},{8,12},{12,8},{9,1... | collective-permute-start | bytes 1966088 | tf_op jit(solution)/shard_map/ppermute | solution.py:507
  47.3 387.4 %all-gather.11.cloned.1.call-start = ((), (), s32[]{:S(2)}) async-start(), calls=%async_computation.5 | async-start | bytes 3604480 | tf_op jit(solution)/shard_map/all_gather | solution.py:672
  52.7 39.4 %collective-permute-start.4 = (bf16[1408,256]{1,0:T(8,128)(2,1)}, bf16[1408,256]{1,0:T(8,128)(2,1)}, u32[]{:S(2)}, u32[]{:S(2)}) collective-permute-start(bf16[1408,256]{1,0:T(8,128)(2,1)} %get-tuple-element.190), channel_id=1, source_target_pairs={{0,4},{4,0},{1,5},{5,1},{2,6},{6,2},{3,7},{7,3},{8,12},{12,8},{9,1... | collective-permute-start | bytes 2162696 | tf_op jit(solution)/shard_map/ppermute | solution.py:507
  58.4 29.2 %collective-permute-start.5 = (bf16[704,256]{1,0:T(8,128)(2,1)}, bf16[704,256]{1,0:T(8,128)(2,1)}, u32[]{:S(2)}, u32[]{:S(2)}) collective-permute-start(bf16[704,256]{1,0:T(8,128)(2,1)} %get-tuple-element.206), channel_id=1, source_target_pairs={{0,4},{4,0},{1,5},{5,1},{2,6},{6,2},{3,7},{7,3},{8,12},{12,8},{9,1... | collective-permute-start | bytes 1081352 | tf_op jit(solution)/shard_map/ppermute | solution.py:507
  81.4 19.9 %collective-permute-start.9 = (bf16[320,2048]{1,0:T(8,128)(2,1)}, bf16[320,2048]{1,0:T(8,128)(2,1)}, u32[]{:S(2)}, u32[]{:S(2)}) collective-permute-start(bf16[320,2048]{1,0:T(8,128)(2,1)} %pad_maximum_fusion.9), channel_id=1, source_target_pairs={{0,1},{1,0},{2,3},{3,2},{4,5},{5,4},{6,7},{7,6},{8,9},{9,8},{10,11... | collective-permute-start | bytes 3932168 | tf_op jit(solution)/shard_map/ppermute | solution.py:507
  89.9 344.9 %all-gather.9.cloned.1.call-start = ((), (), s32[]{:S(2)}) async-start(), calls=%async_computation.4 | async-start | bytes 7208960 | tf_op jit(solution)/shard_map/all_gather | solution.py:672
  93.8 31.5 %collective-permute-start.2 = (bf16[352,2048]{1,0:T(8,128)(2,1)}, bf16[352,2048]{1,0:T(8,128)(2,1)S(1)}, u32[]{:S(2)}, u32[]{:S(2)}) collective-permute-start(bf16[352,2048]{1,0:T(8,128)(2,1)} %shard_map.348), channel_id=1, source_target_pairs={{0,2},{1,3},{2,0},{3,1},{4,6},{5,7},{6,4},{7,5},{8,10},{9,11},{10,... | collective-permute-start | bytes 4325384 | tf_op jit(solution)/shard_map/ppermute | solution.py:507
  155.7 34.3 %collective-permute-start.14 = (bf16[352,2048]{1,0:T(8,128)(2,1)}, bf16[352,2048]{1,0:T(8,128)(2,1)}, u32[]{:S(2)}, u32[]{:S(2)}) collective-permute-start(bf16[352,2048]{1,0:T(8,128)(2,1)} %shard_map.351), channel_id=1, source_target_pairs={{0,2},{1,3},{2,0},{3,1},{4,6},{5,7},{6,4},{7,5},{8,10},{9,11},{10,... | collective-permute-start | bytes 4325384 | tf_op jit(solution)/shard_map/ppermute | solution.py:507
  157.1 32.9 %collective-permute-start.22 = (bf16[352,2048]{1,0:T(8,128)(2,1)S(1)}, bf16[352,2048]{1,0:T(8,128)(2,1)}, u32[]{:S(2)}, u32[]{:S(2)}) collective-permute-start(bf16[352,2048]{1,0:T(8,128)(2,1)S(1)} %copy-done.46), channel_id=1, source_target_pairs={{0,1},{1,0},{2,3},{3,2},{4,5},{5,4},{6,7},{7,6},{8,9},{9,8},{10,11... | collective-permute-start | bytes 4325384 | tf_op jit(solution)/shard_map/ppermute | solution.py:507
  157.5 32.5 %collective-permute-start.23 = (bf16[352,2048]{1,0:T(8,128)(2,1)S(1)}, bf16[352,2048]{1,0:T(8,128)(2,1)}, u32[]{:S(2)}, u32[]{:S(2)}) collective-permute-start(bf16[352,2048]{1,0:T(8,128)(2,1)S(1)} %copy-done.4), channel_id=1, source_target_pairs={{0,1},{1,0},{2,3},{3,2},{4,5},{5,4},{6,7},{7,6},{8,9},{9,8},{10,11... | collective-permute-start | bytes 4325384 | tf_op jit(solution)/shard_map/ppermute | solution.py:507
  168.1 31.9 %collective-permute-start.13 = (bf16[320,2048]{1,0:T(8,128)(2,1)}, bf16[320,2048]{1,0:T(8,128)(2,1)}, u32[]{:S(2)}, u32[]{:S(2)}) collective-permute-start(bf16[320,2048]{1,0:T(8,128)(2,1)} %slice.379), channel_id=1, source_target_pairs={{0,4},{4,0},{1,5},{5,1},{2,6},{6,2},{3,7},{7,3},{8,12},{12,8},{9,1... | collective-permute-start | bytes 3932168 | tf_op jit(solution)/shard_map/ppermute | solution.py:507
  173.8 598.5 %reduce-scatter.3.cloned.1.call-start = ((), (), s32[]{:S(2)}) async-start(), calls=%async_computation.6 | async-start | bytes 10813440 | tf_op jit(solution)/shard_map/reduce_scatter | solution.py:675
  174.0 52.4 %collective-permute-start.24 = (bf16[352,2048]{1,0:T(8,128)(2,1)}, bf16[352,2048]{1,0:T(8,128)(2,1)}, u32[]{:S(2)}, u32[]{:S(2)}) collective-permute-start(bf16[352,2048]{1,0:T(8,128)(2,1)} %shard_map.351), channel_id=1, source_target_pairs={{0,1},{1,0},{2,3},{3,2},{4,5},{5,4},{6,7},{7,6},{8,9},{9,8},{10,11... | collective-permute-start | bytes 4325384 | tf_op jit(solution)/shard_map/ppermute | solution.py:507
  190.0 40.3 %collective-permute-start.25 = (bf16[352,2048]{1,0:T(8,128)(2,1)}, bf16[352,2048]{1,0:T(8,128)(2,1)}, u32[]{:S(2)}, u32[]{:S(2)}) collective-permute-start(bf16[352,2048]{1,0:T(8,128)(2,1)} %collective-permute-done.14.refs_1_), channel_id=1, source_target_pairs={{0,1},{1,0},{2,3},{3,2},{4,5},{5,4},{6,7},{7,6},{8,9},{9,8},{10,11... | collective-permute-start | bytes 4325384 | tf_op jit(solution)/shard_map/ppermute | solution.py:507
  205.5 17.2 %collective-permute-start.15 = (bf16[160,2048]{1,0:T(8,128)(2,1)S(1)}, bf16[160,2048]{1,0:T(8,128)(2,1)S(1)}, u32[]{:S(2)}, u32[]{:S(2)}) collective-permute-start(bf16[160,2048]{1,0:T(8,128)(2,1)S(1)} %slice.381), channel_id=1, source_target_pairs={{0,2},{1,3},{2,0},{3,1},{4,6},{5,7},{6,4},{7,5},{8,10},{9,11},{10,... | collective-permute-start | bytes 1966088 | tf_op jit(solution)/shard_map/ppermute | solution.py:507
  211.5 74.0 %collective-permute-start.19 = (bf16[400,2048]{1,0:T(8,128)(2,1)}, bf16[400,2048]{1,0:T(8,128)(2,1)}, u32[]{:S(2)}, u32[]{:S(2)}) collective-permute-start(bf16[400,2048]{1,0:T(8,128)(2,1)} %convolution_convert_fusion.12), channel_id=1, source_target_pairs={{0,4},{4,0},{1,5},{5,1},{2,6},{6,2},{3,7},{7,3},{8,12},{12,8},{9,1... | collective-permute-start | bytes 4915208 | tf_op jit(solution)/shard_map/ppermute | solution.py:507
  225.1 38.5 %collective-permute-start.28 = (bf16[160,2048]{1,0:T(8,128)(2,1)S(1)}, bf16[160,2048]{1,0:T(8,128)(2,1)S(1)}, u32[]{:S(2)}, u32[]{:S(2)}) collective-permute-start(bf16[160,2048]{1,0:T(8,128)(2,1)S(1)} %get-tuple-element.171), channel_id=1, source_target_pairs={{0,4},{4,0},{1,5},{5,1},{2,6},{6,2},{3,7},{7,3},{8,12},{12,8},{9,1... | collective-permute-start | bytes 1966088 | tf_op jit(solution)/shard_map/ppermute | solution.py:507
  226.5 39.0 %collective-permute-start.16 = (bf16[160,2048]{1,0:T(8,128)(2,1)S(1)}, bf16[160,2048]{1,0:T(8,128)(2,1)S(1)}, u32[]{:S(2)}, u32[]{:S(2)}) collective-permute-start(bf16[160,2048]{1,0:T(8,128)(2,1)S(1)} %get-tuple-element.171), channel_id=1, source_target_pairs={{0,8},{8,16},{16,24},{24,0},{1,9},{9,17},{17,25},{25,1},{2,10},{10... | collective-permute-start | bytes 1966088 | tf_op jit(solution)/shard_map/ppermute | solution.py:512
  226.5 57.4 %collective-permute-start.17 = (bf16[160,2048]{1,0:T(8,128)(2,1)S(1)}, bf16[160,2048]{1,0:T(8,128)(2,1)}, u32[]{:S(2)}, u32[]{:S(2)}) collective-permute-start(bf16[160,2048]{1,0:T(8,128)(2,1)S(1)} %get-tuple-element.171), channel_id=1, source_target_pairs={{0,24},{8,0},{16,8},{24,16},{1,25},{9,1},{17,9},{25,17},{2,26},{10... | collective-permute-start | bytes 1966088 | tf_op jit(solution)/shard_map/ppermute | solution.py:512
  235.7 54.8 %collective-permute-start.31 = (bf16[160,2048]{1,0:T(8,128)(2,1)}, bf16[160,2048]{1,0:T(8,128)(2,1)}, u32[]{:S(2)}, u32[]{:S(2)}) collective-permute-start(bf16[160,2048]{1,0:T(8,128)(2,1)} %shard_map.359), channel_id=1, source_target_pairs={{0,2},{1,3},{2,0},{3,1},{4,6},{5,7},{6,4},{7,5},{8,10},{9,11},{10,... | collective-permute-start | bytes 1966088 | tf_op jit(solution)/shard_map/ppermute | solution.py:507
  263.6 39.9 %collective-permute-start.20 = (bf16[352,2048]{1,0:T(8,128)(2,1)}, bf16[352,2048]{1,0:T(8,128)(2,1)}, u32[]{:S(2)}, u32[]{:S(2)}) collective-permute-start(bf16[352,2048]{1,0:T(8,128)(2,1)} %shard_map.355), channel_id=1, source_target_pairs={{0,2},{1,3},{2,0},{3,1},{4,6},{5,7},{6,4},{7,5},{8,10},{9,11},{10,... | collective-permute-start | bytes 4325384 | tf_op jit(solution)/shard_map/ppermute | solution.py:507
  283.9 41.1 %collective-permute-start.29 = (bf16[320,2048]{1,0:T(8,128)(2,1)}, bf16[320,2048]{1,0:T(8,128)(2,1)}, u32[]{:S(2)}, u32[]{:S(2)}) collective-permute-start(bf16[320,2048]{1,0:T(8,128)(2,1)} %shard_map.358), channel_id=1, source_target_pairs={{0,2},{1,3},{2,0},{3,1},{4,6},{5,7},{6,4},{7,5},{8,10},{9,11},{10,... | collective-permute-start | bytes 3932168 | tf_op jit(solution)/shard_map/ppermute | solution.py:507
  289.6 51.9 %collective-permute-start.26 = (bf16[352,2048]{1,0:T(8,128)(2,1)S(1)}, bf16[352,2048]{1,0:T(8,128)(2,1)}, u32[]{:S(2)}, u32[]{:S(2)}) collective-permute-start(bf16[352,2048]{1,0:T(8,128)(2,1)S(1)} %copy-done.47), channel_id=1, source_target_pairs={{0,1},{1,0},{2,3},{3,2},{4,5},{5,4},{6,7},{7,6},{8,9},{9,8},{10,11... | collective-permute-start | bytes 4325384 | tf_op jit(solution)/shard_map/ppermute | solution.py:507
  292.8 135.8 %collective-permute-start.32 = (bf16[320,2048]{1,0:T(8,128)(2,1)}, bf16[320,2048]{1,0:T(8,128)(2,1)}, u32[]{:S(2)}, u32[]{:S(2)}) collective-permute-start(bf16[320,2048]{1,0:T(8,128)(2,1)} %pad_maximum_fusion.11), channel_id=1, source_target_pairs={{0,1},{1,0},{2,3},{3,2},{4,5},{5,4},{6,7},{7,6},{8,9},{9,8},{10,11... | collective-permute-start | bytes 3932168 | tf_op jit(solution)/shard_map/ppermute | solution.py:507
  294.1 33.3 %collective-permute-start.18 = (bf16[160,2048]{1,0:T(8,128)(2,1)}, bf16[160,2048]{1,0:T(8,128)(2,1)S(1)}, u32[]{:S(2)}, u32[]{:S(2)}) collective-permute-start(bf16[160,2048]{1,0:T(8,128)(2,1)} %shard_map.353), channel_id=1, source_target_pairs={{0,8},{8,16},{16,24},{24,0},{1,9},{9,17},{17,25},{25,1},{2,10},{10... | collective-permute-start | bytes 1966088 | tf_op jit(solution)/shard_map/ppermute | solution.py:512
  303.5 37.9 %collective-permute-start.27 = (bf16[352,2048]{1,0:T(8,128)(2,1)}, bf16[352,2048]{1,0:T(8,128)(2,1)}, u32[]{:S(2)}, u32[]{:S(2)}) collective-permute-start(bf16[352,2048]{1,0:T(8,128)(2,1)} %collective-permute-done.20.refs_2_), channel_id=1, source_target_pairs={{0,1},{1,0},{2,3},{3,2},{4,5},{5,4},{6,7},{7,6},{8,9},{9,8},{10,11... | collective-permute-start | bytes 4325384 | tf_op jit(solution)/shard_map/ppermute | solution.py:507
  331.4 99.7 %collective-permute-start.30 = (bf16[640,2048]{1,0:T(8,128)(2,1)}, bf16[640,2048]{1,0:T(8,128)(2,1)}, u32[]{:S(2)}, u32[]{:S(2)}) collective-permute-start(bf16[640,2048]{1,0:T(8,128)(2,1)} %get-tuple-element.207), channel_id=1, source_target_pairs={{0,1},{1,0},{2,3},{3,2},{4,5},{5,4},{6,7},{7,6},{8,9},{9,8},{10,11... | collective-permute-start | bytes 7864328 | tf_op jit(solution)/shard_map/ppermute | solution.py:507
  335.5 38.3 %collective-permute-start.21 = (bf16[400,2048]{1,0:T(8,128)(2,1)S(1)}, bf16[400,2048]{1,0:T(8,128)(2,1)S(1)}, u32[]{:S(2)}, u32[]{:S(2)}) collective-permute-start(bf16[400,2048]{1,0:T(8,128)(2,1)S(1)} %convolution_convert_fusion.10), channel_id=1, source_target_pairs={{0,4},{4,0},{1,5},{5,1},{2,6},{6,2},{3,7},{7,3},{8,12},{12,8},{9,1... | collective-permute-start | bytes 4915208 | tf_op jit(solution)/shard_map/ppermute | solution.py:507
  427.1 41.1 %collective-permute-start.34 = (bf16[400,2048]{1,0:T(8,128)(2,1)S(1)}, bf16[400,2048]{1,0:T(8,128)(2,1)}, u32[]{:S(2)}, u32[]{:S(2)}) collective-permute-start(bf16[400,2048]{1,0:T(8,128)(2,1)S(1)} %get-tuple-element.178), channel_id=1, source_target_pairs={{0,4},{4,0},{1,5},{5,1},{2,6},{6,2},{3,7},{7,3},{8,12},{12,8},{9,1... | collective-permute-start | bytes 4915208 | tf_op jit(solution)/shard_map/ppermute | solution.py:507
  468.1 20.3 %collective-permute-start.33 = (bf16[640,2048]{1,0:T(8,128)(2,1)}, bf16[640,2048]{1,0:T(8,128)(2,1)}, u32[]{:S(2)}, u32[]{:S(2)}) collective-permute-start(bf16[640,2048]{1,0:T(8,128)(2,1)} %get-tuple-element.56.refs_1_), channel_id=1, source_target_pairs={{0,1},{1,0},{2,3},{3,2},{4,5},{5,4},{6,7},{7,6},{8,9},{9,8},{10,11... | collective-permute-start | bytes 7864328 | tf_op jit(solution)/shard_map/ppermute | solution.py:507
  474.3 55.8 %collective-permute-start.35 = (bf16[160,2048]{1,0:T(8,128)(2,1)}, bf16[160,2048]{1,0:T(8,128)(2,1)}, u32[]{:S(2)}, u32[]{:S(2)}) collective-permute-start(bf16[160,2048]{1,0:T(8,128)(2,1)} %get-tuple-element.186.refs_2_), channel_id=1, source_target_pairs={{0,24},{8,0},{16,8},{24,16},{1,25},{9,1},{17,9},{25,17},{2,26},{10... | collective-permute-start | bytes 1966088 | tf_op jit(solution)/shard_map/ppermute | solution.py:512
  486.7 57.4 %collective-permute-start.36 = (bf16[160,2048]{1,0:T(8,128)(2,1)}, bf16[160,2048]{1,0:T(8,128)(2,1)}, u32[]{:S(2)}, u32[]{:S(2)}) collective-permute-start(bf16[160,2048]{1,0:T(8,128)(2,1)} %get-tuple-element.185.refs_3_), channel_id=1, source_target_pairs={{0,16},{8,24},{16,0},{24,8},{1,17},{9,25},{17,1},{25,9},{2,18},{10... | collective-permute-start | bytes 1966088 | tf_op jit(solution)/shard_map/ppermute | solution.py:512
  486.7 57.4 %collective-permute-start.37 = (bf16[160,2048]{1,0:T(8,128)(2,1)}, bf16[160,2048]{1,0:T(8,128)(2,1)}, u32[]{:S(2)}, u32[]{:S(2)}) collective-permute-start(bf16[160,2048]{1,0:T(8,128)(2,1)} %get-tuple-element.184.refs_4_), channel_id=1, source_target_pairs={{0,8},{8,16},{16,24},{24,0},{1,9},{9,17},{17,25},{25,1},{2,10},{10... | collective-permute-start | bytes 1966088 | tf_op jit(solution)/shard_map/ppermute | solution.py:512
  494.7 31.3 %collective-permute-start.38 = (bf16[2,160,2048]{2,1,0:T(8,128)(2,1)}, bf16[2,160,2048]{2,1,0:T(8,128)(2,1)}, u32[]{:S(2)}, u32[]{:S(2)}) collective-permute-start(bf16[2,160,2048]{2,1,0:T(8,128)(2,1)} %fusion.17.refs_1_), channel_id=1, source_target_pairs={{0,2},{1,3},{2,0},{3,1},{4,6},{5,7},{6,4},{7,5},{8,10},{9,11},{10,... | collective-permute-start | bytes 3932168 | tf_op jit(solution)/shard_map/ppermute | solution.py:507
  544.1 346.2 %reduce-scatter.5.cloned.1.call-start = ((), (), s32[]{:S(2)}) async-start(), calls=%async_computation.7 | async-start | bytes 5242880 | tf_op jit(solution)/shard_map/reduce_scatter | solution.py:675
  546.4 16.8 %collective-permute-start.40 = (bf16[160,2048]{1,0:T(8,128)(2,1)}, bf16[160,2048]{1,0:T(8,128)(2,1)}, u32[]{:S(2)}, u32[]{:S(2)}) collective-permute-start(bf16[160,2048]{1,0:T(8,128)(2,1)} %fusion.34), channel_id=1, source_target_pairs={{0,4},{4,0},{1,5},{5,1},{2,6},{6,2},{3,7},{7,3},{8,12},{12,8},{9,1... | collective-permute-start | bytes 1966088 | tf_op jit(solution)/shard_map/ppermute | solution.py:507
  556.4 31.5 %collective-permute-start.39 = (bf16[704,2048]{1,0:T(8,128)(2,1)}, bf16[704,2048]{1,0:T(8,128)(2,1)}, u32[]{:S(2)}, u32[]{:S(2)}) collective-permute-start(bf16[704,2048]{1,0:T(8,128)(2,1)} %convolution_convert_fusion.5.refs_1_), channel_id=1, source_target_pairs={{0,1},{1,0},{2,3},{3,2},{4,5},{5,4},{6,7},{7,6},{8,9},{9,8},{10,11... | collective-permute-start | bytes 8650760 | tf_op jit(solution)/shard_map/ppermute | solution.py:507
  569.6 15.7 %collective-permute-start.41 = (bf16[160,2048]{1,0:T(8,128)(2,1)S(1)}, bf16[160,2048]{1,0:T(8,128)(2,1)S(1)}, u32[]{:S(2)}, u32[]{:S(2)}) collective-permute-start(bf16[160,2048]{1,0:T(8,128)(2,1)S(1)} %get-tuple-element.165), channel_id=1, source_target_pairs={{0,4},{4,0},{1,5},{5,1},{2,6},{6,2},{3,7},{7,3},{8,12},{12,8},{9,1... | collective-permute-start | bytes 1966088 | tf_op jit(solution)/shard_map/ppermute | solution.py:507
  586.5 29.1 %collective-permute-start.48 = (bf16[320,2048]{1,0:T(8,128)(2,1)}, bf16[320,2048]{1,0:T(8,128)(2,1)S(1)}, u32[]{:S(2)}, u32[]{:S(2)}) collective-permute-start(bf16[320,2048]{1,0:T(8,128)(2,1)} %pad_maximum_fusion.12), channel_id=1, source_target_pairs={{0,2},{1,3},{2,0},{3,1},{4,6},{5,7},{6,4},{7,5},{8,10},{9,11},{10,... | collective-permute-start | bytes 3932168 | tf_op jit(solution)/shard_map/ppermute | solution.py:507
  608.5 22.9 %collective-permute-start.46 = (bf16[704,2048]{1,0:T(8,128)(2,1)}, bf16[704,2048]{1,0:T(8,128)(2,1)}, u32[]{:S(2)}, u32[]{:S(2)}) collective-permute-start(bf16[704,2048]{1,0:T(8,128)(2,1)} %convolution_convert_fusion.3.refs_1_), channel_id=1, source_target_pairs={{0,1},{1,0},{2,3},{3,2},{4,5},{5,4},{6,7},{7,6},{8,9},{9,8},{10,11... | collective-permute-start | bytes 8650760 | tf_op jit(solution)/shard_map/ppermute | solution.py:507
  618.4 49.9 %collective-permute-start.49 = (bf16[640,2048]{1,0:T(8,128)(2,1)}, bf16[640,2048]{1,0:T(8,128)(2,1)}, u32[]{:S(2)}, u32[]{:S(2)}) collective-permute-start(bf16[640,2048]{1,0:T(8,128)(2,1)} %pad_maximum_fusion.8), channel_id=1, source_target_pairs={{0,1},{1,0},{2,3},{3,2},{4,5},{5,4},{6,7},{7,6},{8,9},{9,8},{10,11... | collective-permute-start | bytes 7864328 | tf_op jit(solution)/shard_map/ppermute | solution.py:507
  623.3 38.5 %collective-permute-start.42 = (bf16[400,2048]{1,0:T(8,128)(2,1)}, bf16[400,2048]{1,0:T(8,128)(2,1)}, u32[]{:S(2)}, u32[]{:S(2)}) collective-permute-start(bf16[400,2048]{1,0:T(8,128)(2,1)} %get-tuple-element.176), channel_id=1, source_target_pairs={{0,4},{4,0},{1,5},{5,1},{2,6},{6,2},{3,7},{7,3},{8,12},{12,8},{9,1... | collective-permute-start | bytes 4915208 | tf_op jit(solution)/shard_map/ppermute | solution.py:507
  644.6 71.7 %collective-permute-start.47 = (bf16[704,2048]{1,0:T(8,128)(2,1)}, bf16[704,2048]{1,0:T(8,128)(2,1)}, u32[]{:S(2)}, u32[]{:S(2)}) collective-permute-start(bf16[704,2048]{1,0:T(8,128)(2,1)} %convolution_convert_fusion.1.refs_1_), channel_id=1, source_target_pairs={{0,1},{1,0},{2,3},{3,2},{4,5},{5,4},{6,7},{7,6},{8,9},{9,8},{10,11... | collective-permute-start | bytes 8650760 | tf_op jit(solution)/shard_map/ppermute | solution.py:507
  667.9 40.0 %collective-permute-start.43 = (bf16[160,2048]{1,0:T(8,128)(2,1)S(1)}, bf16[160,2048]{1,0:T(8,128)(2,1)S(1)}, u32[]{:S(2)}, u32[]{:S(2)}) collective-permute-start(bf16[160,2048]{1,0:T(8,128)(2,1)S(1)} %get-tuple-element.182.refs_5_), channel_id=1, source_target_pairs={{0,24},{8,0},{16,8},{24,16},{1,25},{9,1},{17,9},{25,17},{2,26},{10... | collective-permute-start | bytes 1966088 | tf_op jit(solution)/shard_map/ppermute | solution.py:512
  675.0 97.4 %collective-permute-start.55 = (bf16[352,2048]{1,0:T(8,128)(2,1)}, bf16[352,2048]{1,0:T(8,128)(2,1)}, u32[]{:S(2)}, u32[]{:S(2)}) collective-permute-start(bf16[352,2048]{1,0:T(8,128)(2,1)} %shard_map.377.refs_2_), channel_id=1, source_target_pairs={{0,2},{1,3},{2,0},{3,1},{4,6},{5,7},{6,4},{7,5},{8,10},{9,11},{10,... | collective-permute-start | bytes 4325384 | tf_op jit(solution)/shard_map/ppermute | solution.py:507
  685.0 188.6 %collective-permute-start.45 = (bf16[160,2048]{1,0:T(8,128)(2,1)}, bf16[160,2048]{1,0:T(8,128)(2,1)}, u32[]{:S(2)}, u32[]{:S(2)}) collective-permute-start(bf16[160,2048]{1,0:T(8,128)(2,1)} %get-tuple-element.181.refs_6_), channel_id=1, source_target_pairs={{0,8},{8,16},{16,24},{24,0},{1,9},{9,17},{17,25},{25,1},{2,10},{10... | collective-permute-start | bytes 1966088 | tf_op jit(solution)/shard_map/ppermute | solution.py:512
  710.0 71.2 %collective-permute-start.54 = (bf16[352,2048]{1,0:T(8,128)(2,1)}, bf16[352,2048]{1,0:T(8,128)(2,1)}, u32[]{:S(2)}, u32[]{:S(2)}) collective-permute-start(bf16[352,2048]{1,0:T(8,128)(2,1)} %shard_map.376.refs_1_), channel_id=1, source_target_pairs={{0,2},{1,3},{2,0},{3,1},{4,6},{5,7},{6,4},{7,5},{8,10},{9,11},{10,... | collective-permute-start | bytes 4325384 | tf_op jit(solution)/shard_map/ppermute | solution.py:507
  725.2 63.8 %collective-permute-start.56 = (bf16[352,2048]{1,0:T(8,128)(2,1)}, bf16[352,2048]{1,0:T(8,128)(2,1)}, u32[]{:S(2)}, u32[]{:S(2)}) collective-permute-start(bf16[352,2048]{1,0:T(8,128)(2,1)} %shard_map.378.refs_3_), channel_id=1, source_target_pairs={{0,2},{1,3},{2,0},{3,1},{4,6},{5,7},{6,4},{7,5},{8,10},{9,11},{10,... | collective-permute-start | bytes 4325384 | tf_op jit(solution)/shard_map/ppermute | solution.py:507
  772.3 35.2 %collective-permute-start.53 = (bf16[640,2048]{1,0:T(8,128)(2,1)}, bf16[640,2048]{1,0:T(8,128)(2,1)}, u32[]{:S(2)}, u32[]{:S(2)}) collective-permute-start(bf16[640,2048]{1,0:T(8,128)(2,1)} %shard_map.382), channel_id=1, source_target_pairs={{0,1},{1,0},{2,3},{3,2},{4,5},{5,4},{6,7},{7,6},{8,9},{9,8},{10,11... | collective-permute-start | bytes 7864328 | tf_op jit(solution)/shard_map/ppermute | solution.py:507
  779.9 25.9 %collective-permute-start.65 = (bf16[2112,256]{1,0:T(8,128)(2,1)}, bf16[2112,256]{1,0:T(8,128)(2,1)}, u32[]{:S(2)}, u32[]{:S(2)}) collective-permute-start(bf16[2112,256]{1,0:T(8,128)(2,1)} %constant_dynamic-slice_fusion), channel_id=1, source_target_pairs={{0,4},{4,0},{1,5},{5,1},{2,6},{6,2},{3,7},{7,3},{8,12},{12,8},{9,1... | collective-permute-start | bytes 3244040 | tf_op jit(solution)/shard_map/ppermute | solution.py:507
  781.2 34.7 %collective-permute-start.50 = (bf16[640,2048]{1,0:T(8,128)(2,1)}, bf16[640,2048]{1,0:T(8,128)(2,1)}, u32[]{:S(2)}, u32[]{:S(2)}) collective-permute-start(bf16[640,2048]{1,0:T(8,128)(2,1)} %shard_map.381), channel_id=1, source_target_pairs={{0,1},{1,0},{2,3},{3,2},{4,5},{5,4},{6,7},{7,6},{8,9},{9,8},{10,11... | collective-permute-start | bytes 7864328 | tf_op jit(solution)/shard_map/ppermute | solution.py:507
  789.0 84.5 %collective-permute-start.44 = (bf16[160,2048]{1,0:T(8,128)(2,1)}, bf16[160,2048]{1,0:T(8,128)(2,1)}, u32[]{:S(2)}, u32[]{:S(2)}) collective-permute-start(bf16[160,2048]{1,0:T(8,128)(2,1)} %add_convert_fusion.2), channel_id=1, source_target_pairs={{0,24},{8,0},{16,8},{24,16},{1,25},{9,1},{17,9},{25,17},{2,26},{10... | collective-permute-start | bytes 1966088 | tf_op jit(solution)/shard_map/ppermute | solution.py:512
  814.5 29.6 %collective-permute-start.57 = (bf16[320,2048]{1,0:T(8,128)(2,1)S(1)}, bf16[320,2048]{1,0:T(8,128)(2,1)S(1)}, u32[]{:S(2)}, u32[]{:S(2)}) collective-permute-start(bf16[320,2048]{1,0:T(8,128)(2,1)S(1)} %slice.378), channel_id=1, source_target_pairs={{0,4},{4,0},{1,5},{5,1},{2,6},{6,2},{3,7},{7,3},{8,12},{12,8},{9,1... | collective-permute-start | bytes 3932168 | tf_op jit(solution)/shard_map/ppermute | solution.py:507
  818.9 31.8 %collective-permute-start.51 = (bf16[2,160,2048]{2,1,0:T(8,128)(2,1)S(1)}, bf16[2,160,2048]{2,1,0:T(8,128)(2,1)S(1)}, u32[]{:S(2)}, u32[]{:S(2)}) collective-permute-start(bf16[2,160,2048]{2,1,0:T(8,128)(2,1)S(1)} %fusion.18), channel_id=1, source_target_pairs={{0,2},{1,3},{2,0},{3,1},{4,6},{5,7},{6,4},{7,5},{8,10},{9,11},{10,... | collective-permute-start | bytes 3932168 | tf_op jit(solution)/shard_map/ppermute | solution.py:507
  844.6 17.7 %collective-permute-start.58 = (bf16[160,2048]{1,0:T(8,128)(2,1)S(1)}, bf16[160,2048]{1,0:T(8,128)(2,1)S(1)}, u32[]{:S(2)}, u32[]{:S(2)}) collective-permute-start(bf16[160,2048]{1,0:T(8,128)(2,1)S(1)} %slice.380), channel_id=1, source_target_pairs={{0,2},{1,3},{2,0},{3,1},{4,6},{5,7},{6,4},{7,5},{8,10},{9,11},{10,... | collective-permute-start | bytes 1966088 | tf_op jit(solution)/shard_map/ppermute | solution.py:507
  852.1 21.4 %collective-permute-start.52 = (bf16[160,2048]{1,0:T(8,128)(2,1)}, bf16[160,2048]{1,0:T(8,128)(2,1)}, u32[]{:S(2)}, u32[]{:S(2)}) collective-permute-start(bf16[160,2048]{1,0:T(8,128)(2,1)} %fusion.35), channel_id=1, source_target_pairs={{0,4},{4,0},{1,5},{5,1},{2,6},{6,2},{3,7},{7,3},{8,12},{12,8},{9,1... | collective-permute-start | bytes 1966088 | tf_op jit(solution)/shard_map/ppermute | solution.py:507
  891.4 12.1 %collective-permute-start.64 = (bf16[1024,256]{1,0:T(8,128)(2,1)S(1)}, bf16[1024,256]{1,0:T(8,128)(2,1)S(1)}, u32[]{:S(2)}, u32[]{:S(2)}) collective-permute-start(bf16[1024,256]{1,0:T(8,128)(2,1)S(1)} %constant_dynamic-slice_fusion.1), channel_id=1, source_target_pairs={{0,4},{4,0},{1,5},{5,1},{2,6},{6,2},{3,7},{7,3},{8,12},{12,8},{9,1... | collective-permute-start | bytes 1572872 | tf_op jit(solution)/shard_map/ppermute | solution.py:507
  (137 other events, 1576.7 us)
Sparse Core Ops, SparseCore 0:
  29.2 82.3 all-gather.4
  113.7 53.2 all-gather.6
  168.6 57.8 all-gather.10
  228.0 136.2 all-gather.8
  544.2 167.5 reduce-scatter.2
  777.5 90.1 reduce-scatter.4

commit v3 on v2

v3 whole, which is shorter than its diff:
```python
import functools

import jax
import jax.numpy as jnp
from jax import lax
from jax.experimental import pallas as pl
from jax.experimental.pallas import tpu as pltpu
from jax.sharding import PartitionSpec as P

HD = 128
TOP = 4
LANES = 128


def taking(microseconds):
    return pl.CostEstimate(flops=int(microseconds * 1.15e9), bytes_accessed=0, transcendentals=0)

epsilon = 1e-06
rope_base = 1000000.0

RING, PAIR, SHARD = "ring", "pair", "shard"

BF, F32 = jnp.bfloat16, jnp.float32

ATTN_STEPS, ATTN_BACK_STEPS = 4, 2


def rope_tables(positions, head_size):
    exponent = jnp.arange(0, head_size, 2, dtype=F32) / head_size
    frequency = rope_base ** (-exponent)
    angles = positions.astype(F32)[..., None] * frequency
    cosine, sine = jnp.cos(angles), jnp.sin(angles)
    return jnp.concatenate([cosine, cosine, -sine, sine], axis=-1)


def seq_positions(lengths, length_total):
    seq_ends = jnp.cumsum(lengths)
    starts = seq_ends - lengths
    places = jnp.arange(length_total, dtype=jnp.int32)
    member = (places[:, None] >= starts[None, :]) & (places[:, None] < seq_ends[None, :])
    return places - jnp.sum(jnp.where(member, starts[None, :], 0), axis=1)


def norm_back(grad_normed, values_in, inverse, gain_wide, upstream_rows):
    normed = grad_normed * gain_wide
    return (
        upstream_rows
        + inverse * normed
        - values_in * inverse**3 * jnp.mean(normed * values_in, axis=1, keepdims=True)
    )


def dot(left, right, contract):
    return lax.dot_general(
        left, right, (((contract[0],), (contract[1],)), ((), ())), preferred_element_type=F32
    )


def two_parts(values_in):
    high = values_in.astype(BF)
    return high, (values_in - high.astype(F32)).astype(BF)


def from_table(table):
    return table[:, :HD], table[:, HD : 2 * HD], table[:, 2 * HD : 2 * HD + 1]


def swap_halves(values_in):
    return pltpu.roll(values_in, HD // 2, 1)


def causal_probs(query, key, start, scale):
    raw = dot(query, key, (1, 1)) * scale
    row = lax.broadcasted_iota(jnp.int32, raw.shape, 0)
    column = lax.broadcasted_iota(jnp.int32, raw.shape, 1)
    masked = jnp.where((column <= row) & (column.astype(F32) >= start), raw, -1e30)
    powers = jnp.exp(masked - jnp.max(masked, axis=-1, keepdims=True))
    return powers / jnp.sum(powers, axis=-1, keepdims=True)


def in_halves(kept_ref, given_ref, made):
    steps = pl.num_programs(0)

    @pl.when(pl.program_id(0) < steps // 2)
    def _():
        kept_ref[...] = made

    @pl.when(pl.program_id(0) >= steps // 2)
    def _():
        given_ref[...] = made


def half_blocks(steps, rows_each, width):
    half = steps // 2
    return [
        pl.BlockSpec((rows_each, width), lambda i: (jnp.minimum(i, half - 1), 0)),
        pl.BlockSpec((rows_each, width), lambda i: (jnp.maximum(i - half, 0), 0)),
    ]


def attention_forward_body(
    rows, heads, scale, h_ref, w_ref, bias_ref, table_ref, kept_ref, given_ref, qkv_ref, att_ref
):
    width = heads * HD
    qkv = dot(h_ref[...], w_ref[: 3 * width], (1, 1)) + bias_ref[...]
    for block in range(h_ref.shape[0] // rows):
        here = slice(block * rows, (block + 1) * rows)
        cosine, sine, start = from_table(table_ref[here])
        for head in range(heads):
            at = [slice(i * width + head * HD, i * width + (head + 1) * HD) for i in range(3)]
            query, key, value = (qkv[here, span] for span in at)
            query = (query * cosine + swap_halves(query) * sine).astype(BF)
            key = (key * cosine + swap_halves(key) * sine).astype(BF)
            value = value.astype(BF)
            for span, kept in zip(at, (query, key, value), strict=True):
                qkv_ref[here, span] = kept
            probs = causal_probs(query, key, start, scale).astype(BF)
            att_ref[here, at[0]] = dot(probs, value, (1, 0)).astype(BF)
    in_halves(kept_ref, given_ref, dot(att_ref[...], w_ref[3 * width :], (1, 0)).astype(BF))


def attention_backward_body(
    rows,
    heads,
    scale,
    first_ref,
    second_ref,
    h_ref,
    w_ref,
    qkv_ref,
    att_ref,
    table_ref,
    kept_ref,
    given_ref,
    pack_ref,
    bias_ref,
    grad_qkv_ref,
    total_ref,
):
    width = heads * HD
    step = pl.program_id(0)
    columns = first_ref.shape[1]
    grad_att = dot(first_ref[...], w_ref[3 * width :, :columns], (1, 1))
    grad_att += dot(second_ref[...], w_ref[3 * width :, columns:], (1, 1))
    grad_att = grad_att.astype(BF)
    for block in range(first_ref.shape[0] // rows):
        here = slice(block * rows, (block + 1) * rows)
        cosine, sine, start = from_table(table_ref[here])
        for head in range(heads):
            at = [slice(i * width + head * HD, i * width + (head + 1) * HD) for i in range(3)]
            query, key, value = (qkv_ref[here, span] for span in at)
            grad_out = grad_att[here, at[0]]
            probs = causal_probs(query, key, start, scale)
            grad_probs = dot(grad_out, value, (1, 1))
            grad_value = dot(probs.astype(BF), grad_out, (0, 0))
            delta = jnp.sum(probs * grad_probs, axis=-1, keepdims=True)
            grad_scores = (probs * (grad_probs - delta) * scale).astype(BF)
            grad_query = dot(grad_scores, key, (1, 0))
            grad_key = dot(grad_scores, query, (0, 0))
            grad_query = grad_query * cosine - swap_halves(grad_query) * sine
            grad_key = grad_key * cosine - swap_halves(grad_key) * sine
            for span, made in zip(at, (grad_query, grad_key, grad_value), strict=True):
                grad_qkv_ref[here, span] = made.astype(BF)
    grad_qkv = grad_qkv_ref[...]
    in_halves(kept_ref, given_ref, dot(grad_qkv, w_ref[: 3 * width], (1, 0)).astype(BF))
    bias_share = jnp.sum(grad_qkv.astype(F32), axis=0, keepdims=True)
    qkv_share = dot(grad_qkv, h_ref[...], (0, 0))
    out_first = dot(att_ref[...], first_ref[...], (0, 0))
    out_second = dot(att_ref[...], second_ref[...], (0, 0))

    @pl.when(step == 0)
    def _():
        bias_ref[...] = bias_share
        total_ref[: 3 * width] = qkv_share
        total_ref[3 * width :, :columns] = out_first
        total_ref[3 * width :, columns:] = out_second

    @pl.when(step > 0)
    def _():
        bias_ref[...] += bias_share
        total_ref[: 3 * width] += qkv_share
        total_ref[3 * width :, :columns] += out_first
        total_ref[3 * width :, columns:] += out_second

    @pl.when(step == pl.num_programs(0) - 1)
    def _():
        pack_ref[...] = total_ref[...].astype(BF)


def in_hbm(shape, dtype):
    return pltpu.HBM(shape, dtype)


def anywhere():
    return pl.BlockSpec(memory_space=pl.ANY)


def waiting(body, count):
    def run(*refs):
        body(*refs[count:])

    return run


def once_block(*shape):
    return pl.BlockSpec(shape, lambda *i: (0,) * len(shape), pipeline_mode=pl.Buffered(1))


def step_block(rows_each, *rest):
    return pl.BlockSpec((rows_each,) + rest, lambda i: (i,) + (0,) * len(rest))


def whole_block(*shape):
    return pl.BlockSpec(shape, lambda i: (0,) * len(shape))


def attention_forward(h_one, weights, bias, table, rows, heads, steps, waits=()):
    total, model = h_one.shape
    each, width = total // steps, heads * HD
    return pl.pallas_call(
        waiting(functools.partial(attention_forward_body, rows, heads, HD ** (-0.5)), len(waits)),
        grid=(steps,),
        in_specs=[anywhere()] * len(waits)
        + [
            step_block(each, model),
            whole_block(4 * width, model),
            whole_block(1, 3 * width),
            step_block(each, table.shape[1]),
        ],
        out_specs=half_blocks(steps, each, model) + [step_block(each, 3 * width), step_block(each, width)],
        out_shape=[
            in_hbm((total // 2, model), BF),
            in_hbm((total // 2, model), BF),
            in_hbm((total, 3 * width), BF),
            in_hbm((total, width), BF),
        ],
        compiler_params=pltpu.CompilerParams(vmem_limit_bytes=60 << 20),
        cost_estimate=taking(0),
    )(*waits, h_one, weights, bias, table)


def attention_backward(grads, h_one, weights, qkv, att, table, rows, heads, steps, waits=()):
    total, model = h_one.shape
    each, width = total // steps, heads * HD
    return pl.pallas_call(
        waiting(functools.partial(attention_backward_body, rows, heads, HD ** (-0.5)), len(waits)),
        grid=(steps,),
        in_specs=[anywhere()] * len(waits)
        + [
            step_block(each, model // 2),
            step_block(each, model // 2),
            step_block(each, model),
            whole_block(4 * width, model),
            step_block(each, 3 * width),
            step_block(each, width),
            step_block(each, table.shape[1]),
        ],
        out_specs=half_blocks(steps, each, model) + [whole_block(4 * width, model), whole_block(1, 3 * width)],
        out_shape=[
            in_hbm((total // 2, model), BF),
            in_hbm((total // 2, model), BF),
            in_hbm((4 * width, model), BF),
            in_hbm((1, 3 * width), F32),
        ],
        scratch_shapes=[
            pltpu.VMEM((each, 3 * width), BF),
            pltpu.VMEM((4 * width, model), F32),
        ],
        compiler_params=pltpu.CompilerParams(vmem_limit_bytes=60 << 20),
        cost_estimate=taking(35),
    )(*waits, *grads, h_one, weights, qkv, att, table)


def gated(gate, up):
    logistic = jax.nn.sigmoid(gate)
    silu = gate * logistic
    return silu, silu * up, logistic * (1.0 + gate * (1.0 - logistic))


def routed_body(experts, pieces, rows_ref, up_ref, own_ref, router_ref, *rest):
    weights, rest = rest[: 3 * pieces], rest[3 * pieces :]
    units_refs, rest = rest[:6], rest[6:]
    grad_rows_ref, grad_own_ref, grad_other_ref, high_ref, low_ref, row_gate_ref = rest[:6]
    total_ref, probs_ref, share_ref, all_ref, sem_ref = rest[6:]
    step, part = pl.program_id(0), pl.program_id(1)
    piece = weights[0].shape[0]
    half = pieces // 2
    copies = [
        [
            [
                pltpu.make_async_copy(
                    weights[kind * pieces + which * half + i],
                    all_ref.at[which, kind, pl.ds(i * piece, piece)],
                    sem_ref.at[kind * pieces + which * half + i],
                )
                for i in range(half)
            ]
            for kind in range(3)
        ]
        for which in range(2)
    ]

    @pl.when((step == 0) & (part == 0))
    def _():
        for one in sum(copies[0] + copies[1], []):
            one.start()

    def arrived(kind):
        for which in range(2):

            @pl.when((step == 0) & (part == which))
            def _():
                for one in copies[which][kind]:
                    one.wait()

        return all_ref[part, kind]

    rows_in = rows_ref[...]

    @pl.when(part == 0)
    def _():
        logits = dot(rows_in, router_ref[...], (1, 0))
        lane = lax.broadcasted_iota(jnp.int32, logits.shape, 1)
        logits = jnp.where(lane < experts, logits, -1e30)
        powers = jnp.exp(logits - jnp.max(logits, axis=1, keepdims=True))
        probs = powers / jnp.sum(powers, axis=1, keepdims=True)
        probs_ref[...] = probs

    gate = jnp.sum(probs_ref[...] * own_ref[...], axis=1, keepdims=True)
    grad_rows = (gate * up_ref[...].astype(F32)).astype(BF)

    @pl.when(part == 0)
    def _():
        row_gate_ref[...] = gate
        grad_rows_ref[...] = grad_rows

    gate_w = arrived(0)
    gate_e = dot(rows_in, gate_w, (1, 1))
    up_w = arrived(1)
    up_e = dot(rows_in, up_w, (1, 1))
    silu, hidden, slope = gated(gate_e, up_e)
    hidden = hidden.astype(BF)
    grad_hidden = dot(grad_rows, arrived(2), (1, 1))
    grad_gate = (grad_hidden * up_e * slope).astype(BF)
    grad_up = (grad_hidden * silu).astype(BF)
    for i in range(2):

        @pl.when(part == i)
        def _():
            for ref, made in zip(units_refs[3 * i :], (grad_gate, grad_up, hidden), strict=False):
                ref[...] = made

    share = jnp.sum(hidden.astype(F32) * grad_hidden, axis=1, keepdims=True)
    made = dot(grad_gate, gate_w, (1, 0)) + dot(grad_up, up_w, (1, 0))

    @pl.when(part == 0)
    def _():
        share_ref[...] = share
        total_ref[...] = made

    @pl.when(part > 0)
    def _():
        high, low = two_parts((share_ref[...] + share) * (own_ref[...] - probs_ref[...]))
        high_ref[...] = high
        low_ref[...] = low
        from_router = dot(high, router_ref[...], (1, 1)) + dot(low, router_ref[...], (1, 1))
        grad_in = (total_ref[...] + made + from_router).astype(BF)
        for i, ref in enumerate((grad_own_ref, grad_other_ref)):

            @pl.when(step == i)
            def _():
                ref[...] = grad_in


def routed_expert(rows_in, up_rows, own, router, weights, experts, waits=()):
    total, model = rows_in.shape
    pieces = len(weights[0])
    units = pieces * weights[0][0].shape[0]
    steps, parts = 2, 2
    each, part_units = total // steps, units // parts

    def by_rows(width):
        return pl.BlockSpec((each, width), lambda i, j: (i, 0))

    return pl.pallas_call(
        waiting(functools.partial(routed_body, experts, pieces), len(waits)),
        grid=(steps, parts),
        in_specs=[anywhere()] * len(waits)
        + [by_rows(model), by_rows(model), once_block(1, LANES), once_block(model, LANES)]
        + [anywhere()] * (3 * pieces),
        out_specs=[by_rows(part_units)] * 6
        + [by_rows(model)]
        + [once_block(each, model)] * 2
        + [by_rows(LANES)] * 2
        + [by_rows(1)],
        out_shape=[in_hbm((total, part_units), BF)] * 6
        + [in_hbm((total, model), BF)]
        + [in_hbm((each, model), BF)] * 2
        + [in_hbm((total, LANES), BF)] * 2
        + [in_hbm((total, 1), F32)],
        scratch_shapes=[
            pltpu.VMEM((each, model), F32),
            pltpu.VMEM((each, LANES), F32),
            pltpu.VMEM((each, 1), F32),
            pltpu.VMEM((parts, 3, part_units, model), BF),
            pltpu.SemaphoreType.DMA((3 * pieces,)),
        ],
        compiler_params=pltpu.CompilerParams(vmem_limit_bytes=60 << 20),
        cost_estimate=taking(20),
    )(*waits, rows_in, up_rows, own, router, *(one for kind in weights for one in kind))


def routed_out_body(pieces, first_ref, second_ref, row_gate_ref, *rest):
    weights, (own_ref, other_ref, down_ref) = rest[:pieces], rest[pieces:]
    piece = weights[0].shape[0]
    for i, ref in enumerate(weights):
        down_ref[i * piece : (i + 1) * piece] = ref[...]
    units = first_ref.shape[1]
    out = dot(first_ref[...], down_ref[:units], (1, 0))
    out += dot(second_ref[...], down_ref[units:], (1, 0))
    out = (row_gate_ref[...] * out.astype(BF).astype(F32)).astype(BF)
    own_ref[...] = out[: own_ref.shape[0]]
    other_ref[...] = out[own_ref.shape[0] :]


def routed_out(first, second, weights, row_gate, waits=()):
    steps = 4
    total, (piece, model) = first.shape[0], weights[0].shape
    each = model // steps
    return pl.pallas_call(
        waiting(functools.partial(routed_out_body, len(weights)), len(waits)),
        grid=(steps,),
        in_specs=[anywhere()] * len(waits)
        + [once_block(*first.shape), once_block(*second.shape), once_block(*row_gate.shape)]
        + [pl.BlockSpec((piece, each), lambda i: (0, i))] * len(weights),
        out_specs=[pl.BlockSpec((total // 2, each), lambda i: (0, i))] * 2,
        out_shape=[in_hbm((total // 2, model), BF)] * 2,
        scratch_shapes=[pltpu.VMEM((piece * len(weights), each), BF)],
        compiler_params=pltpu.CompilerParams(vmem_limit_bytes=60 << 20),
        cost_estimate=taking(7),
    )(*waits, first, second, row_gate, *weights)


def products_body(picks, stacked, units_refs_count, across_count, *refs):
    done_ref, refs = refs[-1], refs[:-1]
    done_ref[...] = jnp.zeros_like(done_ref)
    units_refs, refs = refs[:units_refs_count], refs[units_refs_count:]
    across_refs, out_refs = refs[:across_count], refs[across_count:]
    for i, (ref, pick) in enumerate(zip(units_refs, picks, strict=True)):
        made = dot(ref[...], across_refs[pick][...], (0, 0)).astype(BF)
        if stacked:
            rows = made.shape[0]
            out_refs[0][i * rows : (i + 1) * rows] = made
        else:
            out_refs[i][...] = made


def products(units, across, picks, stacked, waits=()):
    steps = 4
    rows, model = across[0].shape
    each, count = model // steps, units[0].shape[1]
    heights = [count * len(units)] if stacked else [count] * len(units)
    *made, done = pl.pallas_call(
        waiting(
            functools.partial(products_body, picks, stacked, len(units), len(across)), len(waits)
        ),
        grid=(steps,),
        in_specs=[anywhere()] * len(waits)
        + [once_block(rows, count)] * len(units)
        + [pl.BlockSpec((rows, each), lambda i: (0, i))] * len(across),
        out_specs=[pl.BlockSpec((height, each), lambda i: (0, i)) for height in heights]
        + [whole_block(8, LANES)],
        out_shape=[in_hbm((height, model), BF) for height in heights]
        + [in_hbm((8, LANES), F32)],
        compiler_params=pltpu.CompilerParams(vmem_limit_bytes=60 << 20),
        cost_estimate=taking(0.0045 * rows * len(units)),
    )(*waits, *units, *across)
    return made[0] if stacked else made, done


def shared_body(
    h_ref,
    up_ref,
    gate_up_w_ref,
    down_w_ref,
    mix_w_ref,
    kept_ref,
    given_ref,
    hidden_ref,
    grad_gate_ref,
    grad_up_ref,
    grad_out_ref,
    grad_mix_ref,
    mix_ref,
):
    units = down_w_ref.shape[0]
    h_in, mix_w = h_ref[...], mix_w_ref[...]
    mix = jax.nn.sigmoid(jnp.sum(h_in.astype(F32) * mix_w, axis=1, keepdims=True))
    mix_ref[...] = mix
    gate_s = dot(h_in, gate_up_w_ref[:units], (1, 1))
    up_s = dot(h_in, gate_up_w_ref[units:], (1, 1))
    silu, hidden, slope = gated(gate_s, up_s)
    hidden = hidden.astype(BF)
    hidden_ref[...] = hidden
    grad_out = (mix * up_ref[...].astype(F32)).astype(BF)
    grad_out_ref[...] = grad_out
    grad_hidden = dot(grad_out, down_w_ref[...], (1, 1))
    grad_gate = (grad_hidden * up_s * slope).astype(BF)
    grad_up = (grad_hidden * silu).astype(BF)
    grad_gate_ref[...] = grad_gate
    grad_up_ref[...] = grad_up
    grad_mix = jnp.sum(hidden.astype(F32) * grad_hidden, axis=1, keepdims=True) * (1.0 - mix)
    grad_mix_ref[...] = grad_mix
    made = dot(grad_gate, gate_up_w_ref[:units], (1, 0)) + dot(grad_up, gate_up_w_ref[units:], (1, 0))
    in_halves(kept_ref, given_ref, (made + grad_mix * mix_w).astype(BF))


def shared_expert(h_team, up_team, gate_up_w, down_w, mix_w, waits=()):
    total, model = h_team.shape
    units = down_w.shape[0]
    steps = 4
    each = total // steps
    return pl.pallas_call(
        waiting(shared_body, len(waits)),
        grid=(steps,),
        in_specs=[anywhere()] * len(waits)
        + [
            step_block(each, model),
            step_block(each, model),
            once_block(2 * units, model),
            once_block(units, model),
            once_block(1, model),
        ],
        out_specs=half_blocks(steps, each, model)
        + [step_block(each, units)] * 3
        + [step_block(each, model)]
        + [step_block(each, 1)] * 2,
        out_shape=[in_hbm((total // 2, model), BF)] * 2
        + [in_hbm((total, units), BF)] * 3
        + [in_hbm((total, model), BF)]
        + [in_hbm((total, 1), F32)] * 2,
        compiler_params=pltpu.CompilerParams(vmem_limit_bytes=60 << 20),
        cost_estimate=taking(34),
    )(*waits, h_team, up_team, gate_up_w, down_w, mix_w)


def shared_out_body(hidden_ref, down_w_ref, mix_ref, kept_ref, given_ref):
    made = mix_ref[...] * dot(hidden_ref[...], down_w_ref[...], (1, 0))
    in_halves(kept_ref, given_ref, made.astype(BF))


def shared_out(hidden, down_w, mix, waits=()):
    total, units = hidden.shape
    model = down_w.shape[1]
    steps = 4
    each = total // steps
    return pl.pallas_call(
        waiting(shared_out_body, len(waits)),
        grid=(steps,),
        in_specs=[anywhere()] * len(waits)
        + [step_block(each, units), once_block(units, model), step_block(each, 1)],
        out_specs=half_blocks(steps, each, model),
        out_shape=[in_hbm((total // 2, model), BF)] * 2,
        compiler_params=pltpu.CompilerParams(vmem_limit_bytes=60 << 20),
        cost_estimate=taking(6),
    )(*waits, hidden, down_w, mix)


def nothing_body(*refs):
    del refs


def after(values_in, *others):
    return pl.pallas_call(
        nothing_body,
        in_specs=[anywhere()] * (1 + len(others)),
        out_specs=anywhere(),
        out_shape=jax.ShapeDtypeStruct(values_in.shape, values_in.dtype),
        input_output_aliases={0: 0},
        cost_estimate=taking(0),
    )(values_in, *others)


def flip(values_in, axis, bit):
    size = lax.axis_size(axis)
    return lax.ppermute(values_in, axis, [(i, i ^ bit) for i in range(size)])


def shift(values_in, step):
    size = lax.axis_size(RING)
    return lax.ppermute(values_in, RING, [(i, (i + step) % size) for i in range(size)])


def shard_bits():
    bits, bit = [], lax.axis_size(SHARD) // 2
    while bit:
        bits.append(bit)
        bit //= 2
    return bits


def team_bits():
    bits = [(SHARD, bit) for bit in shard_bits()]
    return bits[:-1] + [(PAIR, 1)] + bits[-1:]


def team_order():
    order = [(0, 0)]
    for axis, bit in team_bits():
        order += [(p ^ bit, s) if axis == PAIR else (p, s ^ bit) for p, s in order]
    return order


def low_sum(parts):
    return sum(part.astype(F32) for part in parts).astype(BF)


def team_sum(kept, given, held):
    (_, last), _, (_, first) = reversed(team_bits())

    def arrive(got, stage):
        return after(got, *held[stage]) if stage in held else got

    parts = [kept, arrive(flip(given, SHARD, last), 0)]
    rows, columns = kept.shape[0] // 4, kept.shape[1] // 2
    sums = []
    for i, ways in enumerate((((PAIR, 1), (SHARD, first)), ((SHARD, first), (PAIR, 1)))):
        here = [part[:, i * columns : (i + 1) * columns].reshape(2, 2, rows, columns) for part in parts]
        if i:
            here = [part.swapaxes(0, 1) for part in here]
        for stage, way in enumerate(ways):
            got = flip(low_sum(part[1] for part in here), *way)
            here = [part[0] for part in here] + [arrive(got, stage + 1)]
        sums.append(sum(part.astype(F32) for part in here))
    return jnp.concatenate(sums, axis=1)


def ring_gather(block, *ready):
    size = lax.axis_size(RING)
    ups, downs = [block], []
    up = down = block
    for k in range(1, size // 2 + 1):
        up = shift(up, 1)
        if k <= (size - 1) // 2:
            down = shift(down, -1)
            downs.append(down)
        ups.append(up)
        if k == 1 and downs:
            up = after(up, downs[0], *ready)
    return ups + downs


class RingSum:
    def __init__(self, blocks):
        size = lax.axis_size(RING)
        self.hops = size // 2
        self.back = list(blocks[1 : self.hops + 1])
        self.ahead = list(blocks[self.hops + 1 :])
        self.back_got, self.ahead_got = [], []

    def hold(self, *ready):
        self.back_got = [after(one, *ready) for one in self.back_got]
        self.ahead_got = [after(one, *ready) for one in self.ahead_got]

    def hop(self, *ready):
        if ready:
            self.hold(*ready)
        both = len(self.back) < self.hops and self.ahead
        sent = [low_sum([self.back.pop()] + self.back_got)]
        if both:
            sent.append(low_sum([self.ahead.pop()] + self.ahead_got))
            self.ahead_got = [shift(sent[1], 1)]
        self.back_got = [shift(sent[0], -1)]
        return sent

    def total(self):
        while self.back or self.ahead:
            self.hop()
        return sum(one.astype(F32) for one in self.back_got + self.ahead_got)


def all_sum(values_in):
    for axis in (SHARD, PAIR, RING):
        bit = 1
        while bit < lax.axis_size(axis):
            values_in = values_in + flip(values_in, axis, bit)
            bit *= 2
    return values_in


def local(
    tokens,
    norm_attn,
    w_query,
    b_query,
    w_key,
    b_key,
    w_value,
    b_value,
    w_output,
    norm_ffn,
    w_router,
    shared_mix,
    shared_gate,
    shared_up,
    shared_down,
    expert_gate,
    expert_up,
    expert_down,
    routes,
    seq_lengths,
    cotangent,
):
    n_shard = lax.axis_size(SHARD)
    ring_at, pair_at, shard_at = (lax.axis_index(a) for a in (RING, PAIR, SHARD))
    expert_at = ring_at * 2 + pair_at
    group_rows, model = tokens.shape
    rows = group_rows // n_shard
    experts = w_router.shape[1]
    capacity = rows * TOP * 5 // (4 * experts)
    slot_rows = experts * capacity
    order = team_order()
    team = len(order)

    def block_of(values_in, flipped):
        return lax.dynamic_slice_in_dim(values_in, (shard_at ^ flipped) * rows, rows, 0)

    def halves(values_in):
        return values_in.reshape(2, values_in.shape[0] // 2, values_in.shape[1])

    def pair_units(parts, *ready):
        pack = jnp.concatenate([halves(part) for part in parts], axis=1)
        mine = lax.dynamic_index_in_dim(pack, pair_at, 0, keepdims=False)
        theirs = lax.dynamic_index_in_dim(pack, 1 - pair_at, 0, keepdims=False)
        got = flip(theirs, PAIR, 1)
        got = after(got, *ready) if ready else got
        return jnp.where(
            pair_at == 0,
            jnp.concatenate([mine, got], axis=1),
            jnp.concatenate([got, mine], axis=1),
        )

    def gather_units(block):
        return lax.all_gather(block, RING, axis=1, tiled=True)

    def scatter_units(pack):
        return lax.psum_scatter(pack, RING, scatter_dimension=1, tiled=True)

    def unpair_units(summed, parts):
        width = summed.shape[1] // 2
        mine = lax.dynamic_slice_in_dim(summed, pair_at * width, width, 1)
        theirs = lax.dynamic_slice_in_dim(summed, (1 - pair_at) * width, width, 1)
        got = flip(theirs, PAIR, 1)
        first, second = jnp.where(pair_at == 0, mine, got), jnp.where(pair_at == 0, got, mine)
        n = summed.shape[0] // parts
        return [
            jnp.concatenate([first[i * n : (i + 1) * n], second[i * n : (i + 1) * n]], axis=0).astype(
                F32
            )
            for i in range(parts)
        ]

    attn_block = pair_units([w_query.T, w_key.T, w_value.T, w_output])
    attn_w = gather_units(attn_block)
    width_here = attn_w.shape[0] // 4
    heads_here = width_here // HD
    def far_rows(block, hold=lambda i, joined: joined):
        far = [block]
        for i, bit in enumerate(shard_bits()):
            got = flip(hold(i, jnp.concatenate(far, axis=0)), SHARD, bit)
            far += [got[i * rows : (i + 1) * rows] for i in range(len(far))]
        return dict(zip([s for p, s in order if p == 1], far, strict=True))

    def team_rows(near, far):
        return jnp.concatenate([far[s] if p else near[s] for p, s in order], axis=0)

    near = {s: block_of(tokens, s) for p, s in order if p == 0}
    def shard_pieces(part):
        first_got = flip(part, SHARD, first_bit)
        parts = [part, first_got]
        return parts + [flip(one, SHARD, shard_bits()[1]) for one in parts], first_got

    first_bit = shard_bits()[0]
    far = far_rows(flip(near[0], PAIR, 1))

    gate_up_block = pair_units([shared_gate.T, shared_up.T], far[shard_bits()[1]])
    down_block = pair_units([shared_down], far[shard_bits()[1]])
    shared_gate_up = gather_units(gate_up_block)
    shared_down_w = gather_units(down_block)

    tokens_team = team_rows(near, far)
    resid_in = near[0].astype(F32)

    ring_size = experts // 2
    back = ring_size // 2
    nearer = [i for i in range(ring_size) if i != back]

    def whole_tiles(count):
        return -(-count // 16) * 16

    slots_near, slots_back = whole_tiles(capacity * (ring_size - 1)), whole_tiles(capacity)
    slots = slots_near + slots_back
    routes_in = jnp.concatenate(ring_gather(routes.T), axis=1)
    places = jnp.arange(ring_size * rows, dtype=jnp.int32)
    ahead = (jnp.arange(ring_size, dtype=jnp.int32) - ring_at + ring_size) % ring_size
    listed = jnp.where(
        ahead == 0, 0, jnp.where(ahead >= ring_size // 2, ring_size - ahead, ring_size // 2 + ahead)
    )

    def one_hot(slot, count):
        return (slot[None, :] == jnp.arange(count, dtype=jnp.int32)[:, None]).astype(BF)

    def taking_of(expert):
        chosen = jnp.any(routes_in == expert, axis=0)
        furthest = places // rows == back
        same = furthest[None, :] == furthest[:, None]
        earlier = (places[None, :] < places[:, None]) & same & chosen[None, :]
        slot = jnp.sum(earlier.astype(jnp.int32), axis=1) + jnp.where(furthest, slots_near, 0)
        slot = jnp.where(chosen, slot, -1)
        blocks = slot.reshape(ring_size, rows)
        in_ring = jnp.take(blocks, listed, axis=0).reshape(-1)
        near_slot = jnp.concatenate([blocks[i] for i in nearer])
        return (
            one_hot(slot, slots),
            one_hot(near_slot, slots_near),
            one_hot(blocks[back] - slots_near, slots_back),
            one_hot(in_ring, slots),
        )

    take_own, take_own_near, take_own_back, take_own_up = taking_of(expert_at)
    take_other, take_other_near, take_other_back, take_other_up = taking_of(
        expert_at + 1 - 2 * pair_at
    )

    up_near = {s: block_of(cotangent, s) for p, s in order if p == 0}
    upstream = up_near[0].astype(F32)
    up_ring = lax.all_gather(after(up_near[0], attn_block), RING, axis=0, tiled=True)
    up_far = far_rows(flip(up_near[0], PAIR, 1))
    up_team = team_rows(up_near, up_far)
    up_own = dot(take_own_up, up_ring, (1, 0)).astype(BF)
    up_other = flip(dot(take_other_up, up_ring, (1, 0)).astype(BF), PAIR, 1)
    def team_gather(own, other, ready, held, late):
        both = after(jnp.concatenate([own, other], axis=0), *ready)
        got = after(flip(both, SHARD, first_bit), *held)
        rows_here = jnp.concatenate([own, got[:rows], other, got[rows:]], axis=0)
        rows_here = after(rows_here, *late)
        return jnp.concatenate([rows_here, flip(rows_here, SHARD, shard_bits()[1])], axis=0)

    def team_spread(own, late):
        columns = own.shape[1] // 2
        one, two = own[:, :columns], own[:, columns:]
        across = flip(one, PAIR, 1)
        beside = flip(two, SHARD, first_bit)
        one_got = flip(jnp.concatenate([one, across], axis=0), SHARD, first_bit)
        two_got = flip(jnp.concatenate([two, beside], axis=0), PAIR, 1)
        one = [one, one_got[:rows], across, one_got[rows:]]
        two = [two, beside, two_got[:rows], two_got[rows:]]
        last = shard_bits()[1]
        halves_here = [jnp.concatenate(one, axis=0), jnp.concatenate(two, axis=0)]
        halves_here[1] = after(halves_here[1], *late)
        return [jnp.concatenate([half, flip(half, SHARD, last)], axis=0) for half in halves_here]

    def shard_sends(kept, given, *ready):
        got = flip(given, SHARD, shard_bits()[1])
        parts = [kept, after(got, *ready) if ready else got]
        parts = [part.reshape(2, 2, rows, model) for part in parts]
        sent = low_sum(part[:, 1] for part in parts)
        return sent, [part[:, 0] for part in parts]

    def shard_done(parts, got):
        return sum(part.astype(F32) for part in parts + [got]).reshape(2 * rows, model)

    far_lengths = flip(seq_lengths, PAIR, 1)
    lengths = jnp.stack(
        [
            lax.dynamic_index_in_dim(far_lengths if p else seq_lengths, shard_at ^ s, 0, False)
            for p, s in order
        ]
    )
    positions = jax.vmap(lambda row: seq_positions(row, rows))(lengths)
    start = (jnp.arange(rows, dtype=jnp.int32)[None, :] - positions).astype(F32)
    start = jnp.broadcast_to(start[..., None], (team, rows, LANES))
    table = jnp.concatenate([rope_tables(positions, HD), start], axis=-1).reshape(team * rows, -1)
    resid_team = tokens_team.astype(F32)
    gain_one = norm_attn.astype(F32)
    inv_one_team = lax.rsqrt(jnp.mean(resid_team * resid_team, axis=1, keepdims=True) + epsilon)
    h_one = (resid_team * inv_one_team * gain_one).astype(BF)
    head_start = (shard_at * 2 + pair_at) * width_here
    qkv_b = jnp.concatenate(
        [lax.dynamic_slice_in_dim(b, head_start, width_here, 0) for b in (b_query, b_key, b_value)]
    ).astype(F32)[None]
    attn_kept, attn_given, qkv, attended = attention_forward(
        h_one,
        attn_w,
        qkv_b,
        table,
        rows,
        heads_here,
        ATTN_STEPS,
        (up_far[shard_bits()[1]], gate_up_block, down_block, routes_in),
    )
    attn_out = team_sum(attn_kept, attn_given, {})

    gate_pieces, gate_got = shard_pieces(after(expert_gate[0].T, attn_out))
    up_pieces, up_got = shard_pieces(after(expert_up[0].T, attn_out))
    down_pieces, down_got = shard_pieces(after(expert_down[0], attn_out))

    up_rows = jnp.concatenate([up_own, up_other], axis=0)

    x_two = resid_in + attn_out
    gain_two = norm_ffn.astype(F32)
    inv_two = lax.rsqrt(jnp.mean(x_two * x_two, axis=1, keepdims=True) + epsilon)
    h_two = (x_two * inv_two * gain_two).astype(BF)

    h_ring = ring_gather(h_two)
    h_back = h_ring[back]
    h_near = jnp.concatenate([h_ring[i] for i in nearer], axis=0)
    near_got = flip(dot(take_other_near, h_near, (1, 0)).astype(BF), PAIR, 1)
    h_team = team_gather(
        h_two,
        after(flip(h_two, PAIR, 1), h_ring[1], h_ring[-1]),
        (gate_got, up_got, up_other, up_team),
        (near_got, down_got, h_back, up_rows),
        (shared_down_w,),
    )
    back_sent = dot(take_other_back, h_back, (1, 0)).astype(BF)
    back_got = after(flip(back_sent, PAIR, 1), h_team)
    rows_other = [near_got, back_got]
    rows_own = [
        dot(take_own_near, h_near, (1, 0)).astype(BF),
        dot(take_own_back, h_back, (1, 0)).astype(BF),
    ]
    rows_in = jnp.concatenate(rows_own + rows_other, axis=0)

    own_expert = (jnp.arange(LANES, dtype=jnp.int32) == expert_at).astype(F32)[None]
    router_wide = jnp.pad(w_router, ((0, 0), (0, LANES - experts)))
    *units, grad_rows, grad_in_own, grad_in_other, high, low, row_gate = routed_expert(
        rows_in,
        up_rows,
        own_expert,
        router_wide,
        (gate_pieces, up_pieces, down_pieces),
        experts,
    )
    kept_units, given_units = units[:3], units[3:]

    def returned(own, got):
        made = (dot(take_own, own, (0, 0)) + dot(take_other, got, (0, 0))).astype(BF)
        return [made[i * rows : (i + 1) * rows] for i in range(ring_size)]

    grad_got = flip(grad_in_other, PAIR, 1)
    out_own, out_other = routed_out(
        kept_units[2], given_units[2], down_pieces, row_gate, (grad_in_other, shared_gate_up)
    )

    mix_w = shared_mix.astype(F32)[None]
    (
        share_kept,
        share_given,
        hidden_s,
        grad_gate_s,
        grad_up_s,
        grad_out_s,
        grad_mix,
        mix_team,
    ) = shared_expert(
        h_team, up_team, shared_gate_up, shared_down_w, mix_w, (out_other,)
    )
    grad_returned = returned(after(grad_in_own, share_given), grad_got)

    def from_team(shared_rows):
        return shared_rows[:rows] + flip(shared_rows[rows:].astype(BF), PAIR, 1).astype(F32)

    share_sent, share_parts = shard_sends(share_kept, share_given, *grad_returned[1:2])
    share_got = flip(share_sent, SHARD, first_bit)
    grad_ring = RingSum(grad_returned)
    grad_ring.hop()

    shared_grad_pack, done = products(
        [grad_gate_s, grad_up_s, hidden_s],
        [h_team, grad_out_s],
        (0, 0, 1),
        True,
        (share_sent, *grad_returned[1:]),
    )
    next_sent = grad_ring.hop(done)
    given_grads, done = products(
        given_units, [rows_in, grad_rows], (0, 0, 1), False, (done, *next_sent)
    )
    grad_share = from_team(shard_done(share_parts, after(share_got, done)))
    kept_grads, done = products(kept_units, [rows_in, grad_rows], (0, 0, 1), False, (done,))
    grad_ring.hold(done)
    grad_h_two = grad_share + grad_returned[0].astype(F32) + grad_ring.total()
    grad_x_two = norm_back(grad_h_two, x_two, inv_two, gain_two, upstream)
    grad_norm_ffn = jnp.sum(grad_h_two * x_two * inv_two, axis=0)
    shared_summed = scatter_units(shared_grad_pack)
    mix_parts = jnp.concatenate(two_parts(grad_mix), axis=1)
    grad_mix_w = jnp.sum(dot(mix_parts, h_team, (0, 0)), axis=0)

    last_shard = shard_bits()[-1]
    ready = (shared_grad_pack,)
    grad_router = (dot(high, rows_in, (0, 0)) + dot(low, rows_in, (0, 0)))[:experts]
    grad_attn = grad_x_two.astype(BF)
    units_half = kept_grads[0].shape[0] // 2
    expert_parts = [
        [kept, flip(given, SHARD, last_shard)]
        for kept, given in zip(kept_grads, given_grads, strict=True)
    ]
    sent = [low_sum(part[units_half:] for part in parts) for parts in expert_parts]
    grad_attn = team_spread(grad_attn, sent)
    first_got, second_got, third_got = (
        flip(after(one, *grad_attn), SHARD, first_bit) for one in sent
    )
    out_got = flip(after(out_other, *grad_attn), PAIR, 1)
    grad_kept, grad_given, attn_grad_pack, grad_qkv_b = attention_backward(
        grad_attn, h_one, attn_w, qkv, attended, table, rows, heads_here, ATTN_BACK_STEPS, (out_own,)
    )
    attn_grad_pack = after(attn_grad_pack, shared_summed)
    attn_summed = scatter_units(attn_grad_pack)
    out_kept, out_given = shared_out(hidden_s, shared_down_w, mix_team, (grad_kept,))
    out_sent, out_parts = shard_sends(out_kept, out_given)
    out_shard_got = flip(out_sent, SHARD, first_bit)
    first_got, second_got = (after(one, grad_kept) for one in (first_got, second_got))
    third_got, out_got, out_shard_got = (
        after(one, attn_grad_pack) for one in (third_got, out_got, out_shard_got)
    )
    out_returned = returned(out_own, out_got)
    out_ring = RingSum(out_returned)
    out_ring.hop()
    grad_h_one = team_sum(
        grad_kept,
        grad_given,
        {0: (attn_grad_pack, first_got, second_got), 2: (third_got, *out_returned[1:])},
    )
    grad_expert_gate, grad_expert_up, grad_expert_down = (
        sum(part[:units_half].astype(F32) for part in parts) + got.astype(F32)
        for parts, got in zip(expert_parts, (first_got, second_got, third_got), strict=True)
    )
    inv_one = lax.rsqrt(jnp.mean(resid_in * resid_in, axis=1, keepdims=True) + epsilon)
    grad_norm_attn = jnp.sum(grad_h_one * resid_in * inv_one, axis=0)
    grad_tokens = norm_back(grad_h_one, resid_in, inv_one, gain_one, grad_x_two)

    out_s = shard_done(out_parts, out_shard_got)
    out_routed = out_returned[0].astype(F32) + out_ring.total()
    block_out = (x_two + out_routed + from_team(out_s)).astype(BF)

    grad_shared_gate, grad_shared_up, grad_shared_down = unpair_units(shared_summed, 3)
    grad_query_w, grad_key_w, grad_value_w, grad_output_w = unpair_units(attn_summed, 4)
    grad_qkv_b = lax.dynamic_update_slice_in_dim(
        jnp.zeros((3, b_query.shape[0]), F32), grad_qkv_b.reshape(3, width_here), head_start, 1
    )
    small = all_sum(
        jnp.concatenate(
            [
                grad_qkv_b,
                jnp.stack([grad_norm_attn, grad_norm_ffn, grad_mix_w]),
                grad_router,
            ],
            axis=0,
        )
    )
    return (
        block_out,
        grad_tokens,
        small[3],
        grad_query_w.T,
        small[0],
        grad_key_w.T,
        small[1],
        grad_value_w.T,
        small[2],
        grad_output_w,
        small[4],
        small[6:].T,
        small[5],
        grad_shared_gate.T,
        grad_shared_up.T,
        grad_shared_down,
        grad_expert_gate.T[None],
        grad_expert_up.T[None],
        grad_expert_down[None],
    )


def solution(mesh):
    experts, shards = mesh.shape["expert"], mesh.shape["shard"]
    grid = jax.sharding.Mesh(
        mesh.devices.reshape(experts // 2, 2, shards), (RING, PAIR, SHARD)
    )
    expert = (RING, PAIR)
    every = (RING, PAIR, SHARD)
    return jax.shard_map(
        local,
        mesh=grid,
        in_specs=(
            P(expert, None),
            P(),
            P(expert, SHARD),
            P(),
            P(expert, SHARD),
            P(),
            P(expert, SHARD),
            P(),
            P(SHARD, expert),
            P(),
            P(),
            P(),
            P(expert, SHARD),
            P(expert, SHARD),
            P(SHARD, expert),
            P(expert, None, SHARD),
            P(expert, None, SHARD),
            P(expert, SHARD, None),
            P(every, None),
            P(expert, None),
            P(expert, None),
        ),
        out_specs=(
            P(every, None),
            P(every, None),
            P(),
            P(expert, SHARD),
            P(),
            P(expert, SHARD),
            P(),
            P(expert, SHARD),
            P(),
            P(SHARD, expert),
            P(),
            P(),
            P(),
            P(expert, SHARD),
            P(expert, SHARD),
            P(SHARD, expert),
            P(expert, None, SHARD),
            P(expert, None, SHARD),
            P(expert, SHARD, None),
        ),
        check_vma=False,
    )
```

time: 924 us -> 815 us (0.88)
  local copies, waits for them, and re-layouts: 153 us -> 90.3 us
  Pallas kernels: 147 us -> 203 us
  matrix products: 88.6 us -> 33.2 us
  waiting for transfers between devices: 294 us -> 260 us
  other arithmetic: 141 us -> 125 us
    ppermute x54 -> x62, waiting for transfers between devices: 238 us -> 148 us  [flip(): return lax.ppermute(values_in, axis, [(i, i ^ bit) for i in range(size)])]
    dot_general x20 -> x13, matrix products: 88.6 us -> 33.2 us  [dot(): lax.dot_general(left, right, (((contract[0],), (contract[1],)), ((), ()))...]
    ppermute x12, waiting for transfers between devices: 55.1 us -> 106 us  [shift(): lax.ppermute(values_in, RING, [(i, (i + step) % size) for i in range(size)])]
    pallas_call x2 -> x5, Pallas kernels: 55.5 us -> 107 us  [the longest x1 53.1 us: routed_expert(): pl.pallas_call(waiting(functools.partial(routed_body, experts, pieces), l...]
    unnamed x288 -> x221, local copies, waits for them, and re-layouts: 85.7 us -> 53.7 us
    add x13 -> x6, other arithmetic: 42.4 us -> 10.7 us  [the longest x4 6.05 us: team_sum(): sums.append(sum((part.astype(F32) for part in here)))]
    convert_element_type x5 -> x18, other arithmetic: 5.2 us -> 32.8 us  [the longest x15 31.2 us: low_sum(): return sum((part.astype(F32) for part in parts)).astype(BF)]
    slice x12 -> x10, local copies, waits for them, and re-layouts: 29.2 us -> 5.24 us  [the longest x4 3.23 us: team_sum(): part[:, i * columns:(i + 1) * columns].reshape(2, 2, rows, columns)]
  transfers between devices with their start and end apart: 72 -> 80, of which waited for: 29 -> 27; matrix products, arithmetic and copies ran while one was open for 36% -> 27% of each run, Pallas kernels for 16% -> 25%
where the time goes in v3:
time: 815 us; the launch traced here: 804 us
  waiting for transfers between devices  260 us (32%)
  Pallas kernels  203 us (25%)
  other arithmetic  125 us (15%)
  local copies, waits for them, and re-layouts  90.3 us (11%)
  starting transfers between devices  77 us (9%)
  matrix products  33.2 us (4%)
  between operations  15.8 us (2%)
    ppermute x62, waiting for transfers between devices, flip(): return lax.ppermute(values_in, axis, [(i, i ^ bit) for i in range(size)])  148 us
    ppermute x12, waiting for transfers between devices, shift(): lax.ppermute(values_in, RING, [(i, (i + step) % size) for i in range(size)])  106 us
    unnamed x221, local copies, waits for them, and re-layouts  53.7 us
    pallas_call x1, Pallas kernels, routed_expert(): pl.pallas_call(waiting(functools.partial(routed_body, experts, pieces), l...  53.1 us
    ppermute x62, starting transfers between devices, flip(): return lax.ppermute(values_in, axis, [(i, i ^ bit) for i in range(size)])  47.9 us
    pallas_call x3, Pallas kernels, products(): pl.pallas_call(waiting(functools.partial(products_body, picks, stacked, l...  44.1 us
    pallas_call x1, Pallas kernels, attention_backward(): pl.pallas_call(waiting(functools.partial(attention_backward_body, rows, h...  34.8 us
    pallas_call x1, Pallas kernels, shared_expert(): pl.pallas_call(waiting(shared_body, len(waits)), grid=(steps,), in_specs=...  33.8 us
  transfers between devices with their start and end apart: 80, of which 27 were waited for; matrix products, arithmetic and copies ran while one was open for 27% of the time, Pallas kernels for 25%

profile of v3, /device:TPU:0, one launch (start us, length us, event | category | flops | bytes accessed | tf_op | source)
XLA Modules:
  0.0 804.4 jit_solution(4939177192284759162)
XLA Ops:
  7.2 2.7 copy.255
  13.8 3.0 collective-permute-start.11
  16.9 11.9 %collective-permute-done.11 = bf16[1024,256]{1,0:T(8,128)(2,1)S(1)} collective-permute-done((bf16[1024,256]{1,0:T(8,128)(2,1)S(1)}, bf16[1024,256]{1,0:T(8,128)(2,1)S(1)}, u32[]{:S(2)}, u32[]{:S(2)}) %collective-permute-start.11) | collective-permute-done | bytes 524320 | tf_op jit(solution)/shard_map/ppermute | solution.py:586
  56.8 12.6 %collective-permute-done = bf16[160,2048]{1,0:T(8,128)(2,1)} collective-permute-done((bf16[160,2048]{1,0:T(8,128)(2,1)S(1)}, bf16[160,2048]{1,0:T(8,128)(2,1)}, u32[]{:S(2)}, u32[]{:S(2)}) %collective-permute-start) | collective-permute-done | bytes 655392 | tf_op jit(solution)/shard_map/ppermute | solution.py:586
  70.9 3.7 multiply_sine_fusion
  75.8 4.4 concatenate.158.refs_7_
  83.8 3.8 collective-permute-done.10
  100.0 3.6 fusion
  103.7 2.8 maximum_select_fusion.refs_1_
  107.5 6.0 fusion.2.refs_4_.refs_3_
  113.5 18.6 %shard_map.351 = (bf16[640,2048]{1,0:T(8,128)(2,1)}, bf16[640,2048]{1,0:T(8,128)(2,1)}, bf16[1280,768]{1,0:T(8,128)(2,1)}, bf16[1280,256]{1,0:T(8,128)(2,1)}) custom-call(bf16[160,2048]{1,0:T(8,128)(2,1)} %slice.511.refs_0_, bf16[1408,512]{1,0:T(8,128)(2,1)} %maximum_select_fusion.refs_1_, bf16[704,512]{1,0:T(8,128)(2,1)} %maximum_select_fusion.2.refs_2_, ...), custom_call_target="tpu_custom_call" | custom-call | tf_op jit(solution)/shard_map/pallas_call | solution.py:220
  143.0 14.0 %collective-permute-done.14 = bf16[2,160,1024]{2,1,0:T(8,128)(2,1)S(1)} collective-permute-done((bf16[2,160,1024]{2,1,0:T(8,128)(2,1)S(1)}, bf16[2,160,1024]{2,1,0:T(8,128)(2,1)S(1)}, u32[]{:S(2)}, u32[]{:S(2)}) %collective-permute-start.14) | collective-permute-done | bytes 655392 | tf_op jit(solution)/shard_map/ppermute | solution.py:586
  162.0 5.5 all-gather.7.cloned.1.call-done
  167.5 4.4 convolution_convert_fusion.1
  184.0 15.6 %collective-permute-start.19 = (bf16[160,2048]{1,0:T(8,128)(2,1)S(1)}, bf16[160,2048]{1,0:T(8,128)(2,1)}, u32[]{:S(2)}, u32[]{:S(2)}) collective-permute-start(bf16[160,2048]{1,0:T(8,128)(2,1)S(1)} %multiply_convert_fusion), channel_id=1, source_target_pairs={{0,24},{8,0},{16,8},{24,16},{1,25},{9,1},{17,9},{25,17},{2,26},{10... | collective-permute-start | bytes 1966088 | tf_op jit(solution)/shard_map/ppermute | solution.py:591
  199.6 12.8 %collective-permute-done.18.refs_0_.refs_1_ = bf16[160,2048]{1,0:T(8,128)(2,1)} collective-permute-done((bf16[160,2048]{1,0:T(8,128)(2,1)S(1)}, bf16[160,2048]{1,0:T(8,128)(2,1)}, u32[]{:S(2)}, u32[]{:S(2)}) %collective-permute-start.18) | collective-permute-done | bytes 655392 | tf_op jit(solution)/shard_map/ppermute | solution.py:591
  219.6 28.4 %collective-permute-done.19.refs_1_.refs_2_ = bf16[160,2048]{1,0:T(8,128)(2,1)} collective-permute-done((bf16[160,2048]{1,0:T(8,128)(2,1)S(1)}, bf16[160,2048]{1,0:T(8,128)(2,1)}, u32[]{:S(2)}, u32[]{:S(2)}) %collective-permute-start.19) | collective-permute-done | bytes 655392 | tf_op jit(solution)/shard_map/ppermute | solution.py:591
  254.3 3.1 convolution_convert_fusion.2
  258.8 3.1 convolution_convert_fusion.3
  262.0 3.7 convolution_convert_fusion
  267.8 23.9 %collective-permute-done.20.refs_3_ = bf16[160,2048]{1,0:T(8,128)(2,1)S(1)} collective-permute-done((bf16[160,2048]{1,0:T(8,128)(2,1)}, bf16[160,2048]{1,0:T(8,128)(2,1)S(1)}, u32[]{:S(2)}, u32[]{:S(2)}) %collective-permute-start.20) | collective-permute-done | bytes 655392 | tf_op jit(solution)/shard_map/ppermute | solution.py:591
  291.7 18.0 %collective-permute-done.27.refs_0_ = bf16[320,2048]{1,0:T(8,128)(2,1)S(1)} collective-permute-done((bf16[320,2048]{1,0:T(8,128)(2,1)}, bf16[320,2048]{1,0:T(8,128)(2,1)S(1)}, u32[]{:S(2)}, u32[]{:S(2)}) %collective-permute-start.27) | collective-permute-done | bytes 1310752 | tf_op jit(solution)/shard_map/ppermute | solution.py:586
  315.9 7.0 collective-permute-done.30.refs_6_
  323.3 4.2 collective-permute-done.22.refs_0_
  333.1 4.8 pad_maximum_fusion.refs_1_.refs_7_
  339.4 3.2 pad_maximum_fusion.2.refs_0_.refs_6_.refs_4_
  342.7 53.1 %shard_map.362 = (bf16[832,704]{1,0:T(8,128)(2,1)}, bf16[832,704]{1,0:T(8,128)(2,1)}, bf16[832,704]{1,0:T(8,128)(2,1)}, bf16[832,704]{1,0:T(8,128)(2,1)}, bf16[8...) custom-call(bf16[832,2048]{1,0:T(8,128)(2,1)} %pad_maximum_fusion.2., ...), custom_call_target="tpu_custom_call" | custom-call | flops 23000000512 | tf_op jit(solution)/shard_map/pallas_call | solution.py:385
  396.1 9.3 %shard_map.363 = (bf16[416,2048]{1,0:T(8,128)(2,1)}, bf16[416,2048]{1,0:T(8,128)(2,1)}) custom-call(bf16[416,2048]{1,0:T(8,128)(2,1)} %get-tuple-element.64.refs_0_, bf16[1408,2048]{1,0:T(8,128)(2,1)} %all-gather.11.cloned.1.call-done.refs_1_.refs_3_, bf16[832,704]{1,0:T(8,128)(2,1)} %get-tuple-element.65.refs_2_.refs_3_, ...), custom_call_target="tpu_custom_call" | custom-call | flops 8049999872 | tf_op jit(solution)/shard_map/pallas_call | solution.py:430
  405.4 33.8 %shard_map.364 = (bf16[640,2048]{1,0:T(8,128)(2,1)}, bf16[640,2048]{1,0:T(8,128)(2,1)}, bf16[1280,704]{1,0:T(8,128)(2,1)}, bf16[1280,704]{1,0:T(8,128)(2,1)}, bf...) custom-call(bf16[416,2048]{1,0:T(8,128)(2,1)} %get-tuple-element.69.refs_0_, ...), custom_call_target="tpu_custom_call" | custom-call | flops 39099998208 | tf_op jit(solution)/shard_map/pallas_call | solution.py:523
  439.3 3.1 fusion.19
  446.2 5.1 collective-permute-start.42
  452.8 3.3 fusion.10.refs_0_
  456.1 17.0 %shard_map.367 = (bf16[2112,2048]{1,0:T(8,128)(2,1)}, f32[8,128]{1,0:T(8,128)}) custom-call(bf16[2,160,2048]{2,1,0:T(8,128)(2,1)} %fusion.10.refs_0_, bf16[160,2048]{1,0:T(8,128)(2,1)} %get-tuple-element.226.refs_1_, bf16[160,2048]{1,0:T(8,128)(2,1)} %get-tuple-element.224.refs_2_, bf16[160,2048]{1,0:T(8,128)(2,1)} %get-tuple-element.225.refs_3_.refs_2_, ...), custom_call_target="tpu_custom_call" | custom-call | flops 19872000000 | tf_op jit(solution)/shard_map/pallas_call | solution.py:463
  475.5 3.3 collective-permute-start.41
  478.8 13.7 %shard_map.369 = (bf16[704,2048]{1,0:T(8,128)(2,1)}, bf16[704,2048]{1,0:T(8,128)(2,1)}, bf16[704,2048]{1,0:T(8,128)(2,1)}, f32[8,128]{1,0:T(8,128)}) custom-call(f32[8,128]{1,0:T(8,128)} %get-tuple-element.77.refs_1_.refs_0_, bf16[160,2048]{1,0:T(8,128)(2,1)} %add_convert_fusion.10.refs_1_, bf16[160,2048]{1,0:T(8,128)(2,1)} %get-tuple-element.225.refs_3_.refs_2_, ...), custom_call_target="tpu_custom_call" | custom-call | flops 12916799488 | tf_op jit(solution)/shard_map/pallas_call | solution.py:463
  499.8 13.4 %shard_map.371 = (bf16[704,2048]{1,0:T(8,128)(2,1)}, bf16[704,2048]{1,0:T(8,128)(2,1)}, bf16[704,2048]{1,0:T(8,128)(2,1)}, f32[8,128]{1,0:T(8,128)}) custom-call(f32[8,128]{1,0:T(8,128)} %get-tuple-element.81.refs_1_.refs_0_, bf16[832,704]{1,0:T(8,128)(2,1)} %get-tuple-element.82.refs_1_, bf16[832,704]{1,0:T(8,128)(2,1)} %get-tuple-element.83.refs_2_, ...), custom_call_target="tpu_custom_call" | custom-call | flops 12916799488 | tf_op jit(solution)/shard_map/pallas_call | solution.py:463
  514.1 12.4 %collective-permute-done.41.refs_0_ = bf16[160,2048]{1,0:T(8,128)(2,1)} collective-permute-done((bf16[160,2048]{1,0:T(8,128)(2,1)}, bf16[160,2048]{1,0:T(8,128)(2,1)}, u32[]{:S(2)}, u32[]{:S(2)}) %collective-permute-start.41) | collective-permute-done | bytes 655392 | tf_op jit(solution)/shard_map/ppermute | solution.py:591
  526.6 2.8 multiply_reduce_fusion
  532.8 7.8 collective-permute-done.46
  542.8 3.1 add_convert_fusion.2.refs_3_.refs_0_
  546.0 3.1 add_convert_fusion.3.refs_2_.refs_0_
  549.1 3.0 add_convert_fusion.4.refs_1_.refs_0_
  552.1 6.0 collective-permute-done.44
  561.5 3.9 fusion.80
  567.1 4.0 pad_maximum_fusion.4.refs_2_
  573.1 34.8 %shard_map.376 = (bf16[640,2048]{1,0:T(8,128)(2,1)}, bf16[640,2048]{1,0:T(8,128)(2,1)}, bf16[1024,2048]{1,0:T(8,128)(2,1)}, f32[1,768]{1,0:T(1,128)}) custom-call(bf16[416,2048]{1,0:T(8,128)(2,1)} %get-tuple-element.68.refs_0_, bf16[1280,1024]{1,0:T(8,128)(2,1)} %copy-done, bf16[1280,1024]{1,0:T(8,128)(2,1)} %pad_maximum_fusion.4.refs_2_, ...), custom_call_target="tpu_custom_call" | custom-call | flops 40249999360 | tf_op jit(solution)/shard_map/pallas_call | solution.py:245
  607.9 9.7 %shard_map.379 = (bf16[640,2048]{1,0:T(8,128)(2,1)}, bf16[640,2048]{1,0:T(8,128)(2,1)}) custom-call(bf16[640,2048]{1,0:T(8,128)(2,1)} %get-tuple-element.95.refs_0_.refs_1_, bf16[1280,704]{1,0:T(8,128)(2,1)} %get-tuple-element.75.refs_6_.refs_1_, bf16[704,2048]{1,0:T(8,128)(2,1)} %all-gather.9.cloned.1.call-done.refs_1_.refs_4_.refs_2_, ...), custom_call_target="tpu_custom_call" | custom-call | flops 6899999744 | tf_op jit(solution)/shard_map/pallas_call | solution.py:557
  620.6 3.4 convolution_reduce_fusion
  628.8 7.8 collective-permute-done.60.refs_0_
  636.7 4.3 add_bitcast_fusion.1
  640.9 4.2 add_bitcast_fusion.2
  645.2 2.9 fusion.11
  659.0 9.4 %collective-permute-done.52.refs_0_ = bf16[416,2048]{1,0:T(8,128)(2,1)} collective-permute-done((bf16[416,2048]{1,0:T(8,128)(2,1)}, bf16[416,2048]{1,0:T(8,128)(2,1)}, u32[]{:S(2)}, u32[]{:S(2)}) %collective-permute-start.52) | collective-permute-done | bytes 1703968 | tf_op jit(solution)/shard_map/ppermute | solution.py:586
  669.7 3.2 fusion.18
  676.8 18.8 %collective-permute-done.57.refs_0_ = bf16[2,160,2048]{2,1,0:T(8,128)(2,1)} collective-permute-done((bf16[2,160,2048]{2,1,0:T(8,128)(2,1)}, bf16[2,160,2048]{2,1,0:T(8,128)(2,1)}, u32[]{:S(2)}, u32[]{:S(2)}) %collective-permute-start.57) | collective-permute-done | bytes 1310752 | tf_op jit(solution)/shard_map/ppermute | solution.py:586
  695.9 4.7 add_bitcast_fusion
  706.6 2.9 collective-permute-done.65
  712.0 25.1 %collective-permute-done.53 = bf16[160,2048]{1,0:T(8,128)(2,1)} collective-permute-done((bf16[160,2048]{1,0:T(8,128)(2,1)S(1)}, bf16[160,2048]{1,0:T(8,128)(2,1)}, u32[]{:S(2)}, u32[]{:S(2)}) %collective-permute-start.53) | collective-permute-done | bytes 655392 | tf_op jit(solution)/shard_map/ppermute | solution.py:591
  741.2 3.2 collective-permute-done.66.refs_0_
  749.0 2.7 fusion.6
  754.9 4.7 collective-permute-done.68
  760.6 4.2 collective-permute-done.69
  772.7 3.4 fusion.14
  782.1 10.0 %collective-permute-done.72 = bf16[1024,256]{1,0:T(8,128)(2,1)S(1)} collective-permute-done((bf16[1024,256]{1,0:T(8,128)(2,1)S(1)}, bf16[1024,256]{1,0:T(8,128)(2,1)S(1)}, u32[]{:S(2)}, u32[]{:S(2)}) %collective-permute-start.72) | collective-permute-done | bytes 524320 | tf_op jit(solution)/shard_map/ppermute | solution.py:586
  (539 shorter events, 203.0 us)
Async XLA Ops:
  7.2 106.3 %all-gather.5.cloned.1.call-start = ((), (), s32[]{:S(2)}) async-start(), calls=%async_computation.2 | async-start | bytes 5242880 | tf_op jit(solution)/shard_map/all_gather | solution.py:744
  13.8 15.0 %collective-permute-start.11 = (bf16[1024,256]{1,0:T(8,128)(2,1)S(1)}, bf16[1024,256]{1,0:T(8,128)(2,1)S(1)}, u32[]{:S(2)}, u32[]{:S(2)}) collective-permute-start(bf16[1024,256]{1,0:T(8,128)(2,1)S(1)} %get-tuple-element.241), channel_id=1, source_target_pairs={{0,4},{4,0},{1,5},{5,1},{2,6},{6,2},{3,7},{7,3},{8,12},{12,8},{9,1... | collective-permute-start | bytes 1572872 | tf_op jit(solution)/shard_map/ppermute | solution.py:586
  30.0 137.5 %all-gather.7.cloned.1.call-start = ((), (), s32[]{:S(2)}) async-start(), calls=%async_computation.3 | async-start | bytes 3276800 | tf_op jit(solution)/shard_map/all_gather | solution.py:837
  30.1 50.1 %collective-permute-start.8 = (s32[4,160]{1,0:T(4,128)S(1)}, s32[4,160]{1,0:T(4,128)S(1)}, u32[]{:S(2)}, u32[]{:S(2)}) collective-permute-start(s32[4,160]{1,0:T(4,128)S(1)} %bitcast.259), channel_id=1, source_target_pairs={{0,8},{8,16},{16,24},{24,0},{1,9},{9,17},{17,25},{25,1},{2,10},{10... | collective-permute-start | bytes 7688 | tf_op jit(solution)/shard_map/ppermute | solution.py:591
  31.9 49.3 %collective-permute-start.9 = (s32[4,160]{1,0:T(4,128)S(1)}, s32[4,160]{1,0:T(4,128)S(1)}, u32[]{:S(2)}, u32[]{:S(2)}) collective-permute-start(s32[4,160]{1,0:T(4,128)S(1)} %bitcast.260), channel_id=1, source_target_pairs={{0,24},{8,0},{16,8},{24,16},{1,25},{9,1},{17,9},{25,17},{2,26},{10... | collective-permute-start | bytes 7688 | tf_op jit(solution)/shard_map/ppermute | solution.py:591
  34.0 19.3 %collective-permute-start.12 = (s32[4,8]{1,0:T(4,128)S(1)}, s32[4,8]{1,0:T(4,128)S(1)}, u32[]{:S(2)}, u32[]{:S(2)}) collective-permute-start(s32[4,8]{1,0:T(4,128)S(1)} %copy-done.94), channel_id=1, source_target_pairs={{0,4},{4,0},{1,5},{5,1},{2,6},{6,2},{3,7},{7,3},{8,12},{12,8},{9,1... | collective-permute-start | bytes 392 | tf_op jit(solution)/shard_map/ppermute | solution.py:586
  37.6 17.7 %collective-permute-start.4 = (bf16[160,2048]{1,0:T(8,128)(2,1)S(1)}, bf16[160,2048]{1,0:T(8,128)(2,1)S(1)}, u32[]{:S(2)}, u32[]{:S(2)}) collective-permute-start(bf16[160,2048]{1,0:T(8,128)(2,1)S(1)} %get-tuple-element.210), channel_id=1, source_target_pairs={{0,4},{4,0},{1,5},{5,1},{2,6},{6,2},{3,7},{7,3},{8,12},{12,8},{9,1... | collective-permute-start | bytes 1966088 | tf_op jit(solution)/shard_map/ppermute | solution.py:586
  40.3 29.1 %collective-permute-start = (bf16[160,2048]{1,0:T(8,128)(2,1)S(1)}, bf16[160,2048]{1,0:T(8,128)(2,1)}, u32[]{:S(2)}, u32[]{:S(2)}) collective-permute-start(bf16[160,2048]{1,0:T(8,128)(2,1)S(1)} %get-tuple-element.215), channel_id=1, source_target_pairs={{0,4},{4,0},{1,5},{5,1},{2,6},{6,2},{3,7},{7,3},{8,12},{12,8},{9,1... | collective-permute-start | bytes 1966088 | tf_op jit(solution)/shard_map/ppermute | solution.py:586
  53.3 43.2 %collective-permute-start.3 = (bf16[1408,256]{1,0:T(8,128)(2,1)}, bf16[1408,256]{1,0:T(8,128)(2,1)}, u32[]{:S(2)}, u32[]{:S(2)}) collective-permute-start(bf16[1408,256]{1,0:T(8,128)(2,1)} %get-tuple-element.230), channel_id=1, source_target_pairs={{0,4},{4,0},{1,5},{5,1},{2,6},{6,2},{3,7},{7,3},{8,12},{12,8},{9,1... | collective-permute-start | bytes 2162696 | tf_op jit(solution)/shard_map/ppermute | solution.py:586
  55.3 26.6 %collective-permute-start.5 = (bf16[160,2048]{1,0:T(8,128)(2,1)S(1)}, bf16[160,2048]{1,0:T(8,128)(2,1)S(1)}, u32[]{:S(2)}, u32[]{:S(2)}) collective-permute-start(bf16[160,2048]{1,0:T(8,128)(2,1)S(1)} %collective-permute-done.4), channel_id=1, source_target_pairs={{0,2},{1,3},{2,0},{3,1},{4,6},{5,7},{6,4},{7,5},{8,10},{9,11},{10,... | collective-permute-start | bytes 1966088 | tf_op jit(solution)/shard_map/ppermute | solution.py:586
  69.4 20.3 %collective-permute-start.1 = (bf16[160,2048]{1,0:T(8,128)(2,1)}, bf16[160,2048]{1,0:T(8,128)(2,1)S(1)}, u32[]{:S(2)}, u32[]{:S(2)}) collective-permute-start(bf16[160,2048]{1,0:T(8,128)(2,1)} %collective-permute-done), channel_id=1, source_target_pairs={{0,2},{1,3},{2,0},{3,1},{4,6},{5,7},{6,4},{7,5},{8,10},{9,11},{10,... | collective-permute-start | bytes 1966088 | tf_op jit(solution)/shard_map/ppermute | solution.py:586
  80.1 16.4 %collective-permute-start.7 = (bf16[704,256]{1,0:T(8,128)(2,1)}, bf16[704,256]{1,0:T(8,128)(2,1)}, u32[]{:S(2)}, u32[]{:S(2)}) collective-permute-start(bf16[704,256]{1,0:T(8,128)(2,1)} %get-tuple-element.243), channel_id=1, source_target_pairs={{0,4},{4,0},{1,5},{5,1},{2,6},{6,2},{3,7},{7,3},{8,12},{12,8},{9,1... | collective-permute-start | bytes 1081352 | tf_op jit(solution)/shard_map/ppermute | solution.py:586
  88.3 225.6 %all-gather.9.cloned.1.call-start = ((), (), s32[]{:S(2)}) async-start(), calls=%async_computation.4 | async-start | bytes 3604480 | tf_op jit(solution)/shard_map/all_gather | solution.py:744
  93.0 13.5 %collective-permute-start.2 = (bf16[320,2048]{1,0:T(8,128)(2,1)}, bf16[320,2048]{1,0:T(8,128)(2,1)S(1)}, u32[]{:S(2)}, u32[]{:S(2)}) collective-permute-start(bf16[320,2048]{1,0:T(8,128)(2,1)} %pad_maximum_fusion.6), channel_id=1, source_target_pairs={{0,1},{1,0},{2,3},{3,2},{4,5},{5,4},{6,7},{7,6},{8,9},{9,8},{10,11... | collective-permute-start | bytes 3932168 | tf_op jit(solution)/shard_map/ppermute | solution.py:586
  136.9 259.3 %all-gather.11.cloned.1.call-start = ((), (), s32[]{:S(2)}) async-start(), calls=%async_computation.5 | async-start | bytes 7208960 | tf_op jit(solution)/shard_map/all_gather | solution.py:744
  140.3 16.7 %collective-permute-start.14 = (bf16[2,160,1024]{2,1,0:T(8,128)(2,1)S(1)}, bf16[2,160,1024]{2,1,0:T(8,128)(2,1)S(1)}, u32[]{:S(2)}, u32[]{:S(2)}) collective-permute-start(bf16[2,160,1024]{2,1,0:T(8,128)(2,1)S(1)} %bitcast.244), channel_id=1, source_target_pairs={{0,4},{4,0},{1,5},{5,1},{2,6},{6,2},{3,7},{7,3},{8,12},{12,8},{9,1... | collective-permute-start | bytes 1966088 | tf_op jit(solution)/shard_map/ppermute | solution.py:586
  142.4 17.1 %collective-permute-start.16 = (bf16[2,160,1024]{2,1,0:T(8,128)(2,1)S(1)}, bf16[2,160,1024]{2,1,0:T(8,128)(2,1)S(1)}, u32[]{:S(2)}, u32[]{:S(2)}) collective-permute-start(bf16[2,160,1024]{2,1,0:T(8,128)(2,1)S(1)} %fusion.24), channel_id=1, source_target_pairs={{0,2},{1,3},{2,0},{3,1},{4,6},{5,7},{6,4},{7,5},{8,10},{9,11},{10,... | collective-permute-start | bytes 1966088 | tf_op jit(solution)/shard_map/ppermute | solution.py:586
  159.1 14.3 %collective-permute-start.15 = (bf16[160,1024]{1,0:T(8,128)(2,1)}, bf16[160,1024]{1,0:T(8,128)(2,1)}, u32[]{:S(2)}, u32[]{:S(2)}) collective-permute-start(bf16[160,1024]{1,0:T(8,128)(2,1)} %fusion.34), channel_id=1, source_target_pairs={{0,2},{1,3},{2,0},{3,1},{4,6},{5,7},{6,4},{7,5},{8,10},{9,11},{10,... | collective-permute-start | bytes 983048 | tf_op jit(solution)/shard_map/ppermute | solution.py:586
  160.3 14.5 %collective-permute-start.17 = (bf16[160,1024]{1,0:T(8,128)(2,1)S(1)}, bf16[160,1024]{1,0:T(8,128)(2,1)}, u32[]{:S(2)}, u32[]{:S(2)}) collective-permute-start(bf16[160,1024]{1,0:T(8,128)(2,1)S(1)} %fusion.32), channel_id=1, source_target_pairs={{0,4},{4,0},{1,5},{5,1},{2,6},{6,2},{3,7},{7,3},{8,12},{12,8},{9,1... | collective-permute-start | bytes 983048 | tf_op jit(solution)/shard_map/ppermute | solution.py:586
  171.9 80.6 %collective-permute-start.26 = (bf16[416,2048]{1,0:T(8,128)(2,1)}, bf16[416,2048]{1,0:T(8,128)(2,1)S(1)}, u32[]{:S(2)}, u32[]{:S(2)}) collective-permute-start(bf16[416,2048]{1,0:T(8,128)(2,1)} %convolution_convert_fusion.1), channel_id=1, source_target_pairs={{0,4},{4,0},{1,5},{5,1},{2,6},{6,2},{3,7},{7,3},{8,12},{12,8},{9,1... | collective-permute-start | bytes 5111816 | tf_op jit(solution)/shard_map/ppermute | solution.py:586
  178.9 33.6 %collective-permute-start.18 = (bf16[160,2048]{1,0:T(8,128)(2,1)S(1)}, bf16[160,2048]{1,0:T(8,128)(2,1)}, u32[]{:S(2)}, u32[]{:S(2)}) collective-permute-start(bf16[160,2048]{1,0:T(8,128)(2,1)S(1)} %multiply_convert_fusion), channel_id=1, source_target_pairs={{0,8},{8,16},{16,24},{24,0},{1,9},{9,17},{17,25},{25,1},{2,10},{10... | collective-permute-start | bytes 1966088 | tf_op jit(solution)/shard_map/ppermute | solution.py:591
  179.1 73.4 %collective-permute-start.24 = (bf16[352,2048]{1,0:T(8,128)(2,1)}, bf16[352,2048]{1,0:T(8,128)(2,1)}, u32[]{:S(2)}, u32[]{:S(2)}) collective-permute-start(bf16[352,2048]{1,0:T(8,128)(2,1)} %shard_map.354.refs_4_), channel_id=1, source_target_pairs={{0,2},{1,3},{2,0},{3,1},{4,6},{5,7},{6,4},{7,5},{8,10},{9,11},{10,... | collective-permute-start | bytes 4325384 | tf_op jit(solution)/shard_map/ppermute | solution.py:586
  180.5 72.0 %collective-permute-start.25 = (bf16[352,2048]{1,0:T(8,128)(2,1)}, bf16[352,2048]{1,0:T(8,128)(2,1)}, u32[]{:S(2)}, u32[]{:S(2)}) collective-permute-start(bf16[352,2048]{1,0:T(8,128)(2,1)} %shard_map.355.refs_8_), channel_id=1, source_target_pairs={{0,2},{1,3},{2,0},{3,1},{4,6},{5,7},{6,4},{7,5},{8,10},{9,11},{10,... | collective-permute-start | bytes 4325384 | tf_op jit(solution)/shard_map/ppermute | solution.py:586
  184.0 63.9 %collective-permute-start.19 = (bf16[160,2048]{1,0:T(8,128)(2,1)S(1)}, bf16[160,2048]{1,0:T(8,128)(2,1)}, u32[]{:S(2)}, u32[]{:S(2)}) collective-permute-start(bf16[160,2048]{1,0:T(8,128)(2,1)S(1)} %multiply_convert_fusion), channel_id=1, source_target_pairs={{0,24},{8,0},{16,8},{24,16},{1,25},{9,1},{17,9},{25,17},{2,26},{10... | collective-permute-start | bytes 1966088 | tf_op jit(solution)/shard_map/ppermute | solution.py:591
  212.5 37.0 %collective-permute-start.23 = (bf16[160,2048]{1,0:T(8,128)(2,1)S(1)}, bf16[160,2048]{1,0:T(8,128)(2,1)S(1)}, u32[]{:S(2)}, u32[]{:S(2)}) collective-permute-start(bf16[160,2048]{1,0:T(8,128)(2,1)S(1)} %multiply_convert_fusion), channel_id=1, source_target_pairs={{0,4},{4,0},{1,5},{5,1},{2,6},{6,2},{3,7},{7,3},{8,12},{12,8},{9,1... | collective-permute-start | bytes 1966088 | tf_op jit(solution)/shard_map/ppermute | solution.py:586
  217.0 431.8 %reduce-scatter.3.cloned.1.call-start = ((), (), s32[]{:S(2)}) async-start(), calls=%async_computation.6 | async-start | bytes 10813440 | tf_op jit(solution)/shard_map/reduce_scatter | solution.py:747
  248.0 43.7 %collective-permute-start.28 = (bf16[352,2048]{1,0:T(8,128)(2,1)}, bf16[352,2048]{1,0:T(8,128)(2,1)}, u32[]{:S(2)}, u32[]{:S(2)}) collective-permute-start(bf16[352,2048]{1,0:T(8,128)(2,1)} %shard_map.358.refs_12_.refs_5_), channel_id=1, source_target_pairs={{0,2},{1,3},{2,0},{3,1},{4,6},{5,7},{6,4},{7,5},{8,10},{9,11},{10,... | collective-permute-start | bytes 4325384 | tf_op jit(solution)/shard_map/ppermute | solution.py:586
  253.7 56.0 %collective-permute-start.27 = (bf16[320,2048]{1,0:T(8,128)(2,1)}, bf16[320,2048]{1,0:T(8,128)(2,1)S(1)}, u32[]{:S(2)}, u32[]{:S(2)}) collective-permute-start(bf16[320,2048]{1,0:T(8,128)(2,1)} %shard_map.357), channel_id=1, source_target_pairs={{0,2},{1,3},{2,0},{3,1},{4,6},{5,7},{6,4},{7,5},{8,10},{9,11},{10,... | collective-permute-start | bytes 3932168 | tf_op jit(solution)/shard_map/ppermute | solution.py:586
  257.5 34.2 %collective-permute-start.21 = (bf16[304,2048]{1,0:T(8,128)(2,1)}, bf16[304,2048]{1,0:T(8,128)(2,1)}, u32[]{:S(2)}, u32[]{:S(2)}) collective-permute-start(bf16[304,2048]{1,0:T(8,128)(2,1)} %convolution_convert_fusion.2), channel_id=1, source_target_pairs={{0,4},{4,0},{1,5},{5,1},{2,6},{6,2},{3,7},{7,3},{8,12},{12,8},{9,1... | collective-permute-start | bytes 3735560 | tf_op jit(solution)/shard_map/ppermute | solution.py:586
  261.9 29.8 %collective-permute-start.20 = (bf16[160,2048]{1,0:T(8,128)(2,1)}, bf16[160,2048]{1,0:T(8,128)(2,1)S(1)}, u32[]{:S(2)}, u32[]{:S(2)}) collective-permute-start(bf16[160,2048]{1,0:T(8,128)(2,1)} %shard_map.352), channel_id=1, source_target_pairs={{0,8},{8,16},{16,24},{24,0},{1,9},{9,17},{17,25},{25,1},{2,10},{10... | collective-permute-start | bytes 1966088 | tf_op jit(solution)/shard_map/ppermute | solution.py:591
  313.9 13.5 %collective-permute-start.29 = (bf16[640,2048]{1,0:T(8,128)(2,1)}, bf16[640,2048]{1,0:T(8,128)(2,1)}, u32[]{:S(2)}, u32[]{:S(2)}) collective-permute-start(bf16[640,2048]{1,0:T(8,128)(2,1)} %shard_map.360), channel_id=1, source_target_pairs={{0,1},{1,0},{2,3},{3,2},{4,5},{5,4},{6,7},{7,6},{8,9},{9,8},{10,11... | collective-permute-start | bytes 7864328 | tf_op jit(solution)/shard_map/ppermute | solution.py:586
  315.3 27.3 %collective-permute-start.32 = (bf16[352,2048]{1,0:T(8,128)(2,1)}, bf16[352,2048]{1,0:T(8,128)(2,1)}, u32[]{:S(2)}, u32[]{:S(2)}) collective-permute-start(bf16[352,2048]{1,0:T(8,128)(2,1)} %shard_map.355.refs_8_), channel_id=1, source_target_pairs={{0,1},{1,0},{2,3},{3,2},{4,5},{5,4},{6,7},{7,6},{8,9},{9,8},{10,11... | collective-permute-start | bytes 4325384 | tf_op jit(solution)/shard_map/ppermute | solution.py:586
  315.4 27.2 %collective-permute-start.34 = (bf16[352,2048]{1,0:T(8,128)(2,1)}, bf16[352,2048]{1,0:T(8,128)(2,1)}, u32[]{:S(2)}, u32[]{:S(2)}) collective-permute-start(bf16[352,2048]{1,0:T(8,128)(2,1)} %shard_map.358.refs_12_.refs_5_), channel_id=1, source_target_pairs={{0,1},{1,0},{2,3},{3,2},{4,5},{5,4},{6,7},{7,6},{8,9},{9,8},{10,11... | collective-permute-start | bytes 4325384 | tf_op jit(solution)/shard_map/ppermute | solution.py:586
  322.9 19.7 %collective-permute-start.31 = (bf16[352,2048]{1,0:T(8,128)(2,1)}, bf16[352,2048]{1,0:T(8,128)(2,1)}, u32[]{:S(2)}, u32[]{:S(2)}) collective-permute-start(bf16[352,2048]{1,0:T(8,128)(2,1)} %collective-permute-done.24.refs_1_.refs_5_), channel_id=1, source_target_pairs={{0,1},{1,0},{2,3},{3,2},{4,5},{5,4},{6,7},{7,6},{8,9},{9,8},{10,11... | collective-permute-start | bytes 4325384 | tf_op jit(solution)/shard_map/ppermute | solution.py:586
  327.5 15.2 %collective-permute-start.33 = (bf16[352,2048]{1,0:T(8,128)(2,1)}, bf16[352,2048]{1,0:T(8,128)(2,1)}, u32[]{:S(2)}, u32[]{:S(2)}) collective-permute-start(bf16[352,2048]{1,0:T(8,128)(2,1)} %collective-permute-done.25.refs_2_.refs_9_), channel_id=1, source_target_pairs={{0,1},{1,0},{2,3},{3,2},{4,5},{5,4},{6,7},{7,6},{8,9},{9,8},{10,11... | collective-permute-start | bytes 4325384 | tf_op jit(solution)/shard_map/ppermute | solution.py:586
  327.5 15.2 %collective-permute-start.35 = (bf16[352,2048]{1,0:T(8,128)(2,1)}, bf16[352,2048]{1,0:T(8,128)(2,1)}, u32[]{:S(2)}, u32[]{:S(2)}) collective-permute-start(bf16[352,2048]{1,0:T(8,128)(2,1)} %collective-permute-done.28.refs_2_.refs_13_.refs_6_), channel_id=1, source_target_pairs={{0,1},{1,0},{2,3},{3,2},{4,5},{5,4},{6,7},{7,6},{8,9},{9,8},{10,11... | collective-permute-start | bytes 4325384 | tf_op jit(solution)/shard_map/ppermute | solution.py:586
  395.8 43.5 %collective-permute-start.37 = (bf16[416,2048]{1,0:T(8,128)(2,1)}, bf16[416,2048]{1,0:T(8,128)(2,1)}, u32[]{:S(2)}, u32[]{:S(2)}) collective-permute-start(bf16[416,2048]{1,0:T(8,128)(2,1)} %get-tuple-element.64.refs_0_), channel_id=1, source_target_pairs={{0,4},{4,0},{1,5},{5,1},{2,6},{6,2},{3,7},{7,3},{8,12},{12,8},{9,1... | collective-permute-start | bytes 5111816 | tf_op jit(solution)/shard_map/ppermute | solution.py:586
  446.2 27.0 %collective-permute-start.39 = (bf16[160,2048]{1,0:T(8,128)(2,1)}, bf16[160,2048]{1,0:T(8,128)(2,1)}, u32[]{:S(2)}, u32[]{:S(2)}) collective-permute-start(bf16[160,2048]{1,0:T(8,128)(2,1)} %get-tuple-element.224.refs_2_), channel_id=1, source_target_pairs={{0,24},{8,0},{16,8},{24,16},{1,25},{9,1},{17,9},{25,17},{2,26},{10... | collective-permute-start | bytes 1966088 | tf_op jit(solution)/shard_map/ppermute | solution.py:591
  446.2 67.0 %collective-permute-start.42 = (bf16[160,2048]{1,0:T(8,128)(2,1)}, bf16[160,2048]{1,0:T(8,128)(2,1)S(1)}, u32[]{:S(2)}, u32[]{:S(2)}) collective-permute-start(bf16[160,2048]{1,0:T(8,128)(2,1)} %get-tuple-element.225.refs_3_.refs_2_), channel_id=1, source_target_pairs={{0,8},{8,16},{16,24},{24,0},{1,9},{9,17},{17,25},{25,1},{2,10},{10... | collective-permute-start | bytes 1966088 | tf_op jit(solution)/shard_map/ppermute | solution.py:591
  456.1 36.9 %collective-permute-start.38 = (bf16[2,160,2048]{2,1,0:T(8,128)(2,1)}, bf16[2,160,2048]{2,1,0:T(8,128)(2,1)}, u32[]{:S(2)}, u32[]{:S(2)}) collective-permute-start(bf16[2,160,2048]{2,1,0:T(8,128)(2,1)} %fusion.10.refs_0_), channel_id=1, source_target_pairs={{0,2},{1,3},{2,0},{3,1},{4,6},{5,7},{6,4},{7,5},{8,10},{9,11},{10,... | collective-permute-start | bytes 3932168 | tf_op jit(solution)/shard_map/ppermute | solution.py:586
  473.1 305.0 %reduce-scatter.5.cloned.1.call-start = ((), (), s32[]{:S(2)}) async-start(), calls=%async_computation.7 | async-start | bytes 5242880 | tf_op jit(solution)/shard_map/reduce_scatter | solution.py:747
  475.5 51.0 %collective-permute-start.41 = (bf16[160,2048]{1,0:T(8,128)(2,1)}, bf16[160,2048]{1,0:T(8,128)(2,1)}, u32[]{:S(2)}, u32[]{:S(2)}) collective-permute-start(bf16[160,2048]{1,0:T(8,128)(2,1)} %add_convert_fusion.10.refs_1_), channel_id=1, source_target_pairs={{0,24},{8,0},{16,8},{24,16},{1,25},{9,1},{17,9},{25,17},{2,26},{10... | collective-permute-start | bytes 1966088 | tf_op jit(solution)/shard_map/ppermute | solution.py:591
  492.5 50.3 %collective-permute-start.50 = (bf16[704,2048]{1,0:T(8,128)(2,1)}, bf16[704,2048]{1,0:T(8,128)(2,1)}, u32[]{:S(2)}, u32[]{:S(2)}) collective-permute-start(bf16[704,2048]{1,0:T(8,128)(2,1)} %get-tuple-element.90), channel_id=1, source_target_pairs={{0,1},{1,0},{2,3},{3,2},{4,5},{5,4},{6,7},{7,6},{8,9},{9,8},{10,11... | collective-permute-start | bytes 8650760 | tf_op jit(solution)/shard_map/ppermute | solution.py:586
  492.5 53.5 %collective-permute-start.49 = (bf16[704,2048]{1,0:T(8,128)(2,1)}, bf16[704,2048]{1,0:T(8,128)(2,1)}, u32[]{:S(2)}, u32[]{:S(2)}) collective-permute-start(bf16[704,2048]{1,0:T(8,128)(2,1)} %get-tuple-element.88), channel_id=1, source_target_pairs={{0,1},{1,0},{2,3},{3,2},{4,5},{5,4},{6,7},{7,6},{8,9},{9,8},{10,11... | collective-permute-start | bytes 8650760 | tf_op jit(solution)/shard_map/ppermute | solution.py:586
  498.2 28.4 %collective-permute-start.40 = (bf16[160,2048]{1,0:T(8,128)(2,1)S(1)}, bf16[160,2048]{1,0:T(8,128)(2,1)S(1)}, u32[]{:S(2)}, u32[]{:S(2)}) collective-permute-start(bf16[160,2048]{1,0:T(8,128)(2,1)S(1)} %fusion.26), channel_id=1, source_target_pairs={{0,4},{4,0},{1,5},{5,1},{2,6},{6,2},{3,7},{7,3},{8,12},{12,8},{9,1... | collective-permute-start | bytes 1966088 | tf_op jit(solution)/shard_map/ppermute | solution.py:586
  513.3 35.8 %collective-permute-start.48 = (bf16[704,2048]{1,0:T(8,128)(2,1)}, bf16[704,2048]{1,0:T(8,128)(2,1)}, u32[]{:S(2)}, u32[]{:S(2)}) collective-permute-start(bf16[704,2048]{1,0:T(8,128)(2,1)} %get-tuple-element.86), channel_id=1, source_target_pairs={{0,1},{1,0},{2,3},{3,2},{4,5},{5,4},{6,7},{7,6},{8,9},{9,8},{10,11... | collective-permute-start | bytes 8650760 | tf_op jit(solution)/shard_map/ppermute | solution.py:586
  540.6 18.8 %collective-permute-start.47 = (bf16[320,1024]{1,0:T(8,128)(2,1)S(1)}, bf16[320,1024]{1,0:T(8,128)(2,1)S(1)}, u32[]{:S(2)}, u32[]{:S(2)}) collective-permute-start(bf16[320,1024]{1,0:T(8,128)(2,1)S(1)} %pad_maximum_fusion.17), channel_id=1, source_target_pairs={{0,4},{4,0},{1,5},{5,1},{2,6},{6,2},{3,7},{7,3},{8,12},{12,8},{9,1... | collective-permute-start | bytes 1966088 | tf_op jit(solution)/shard_map/ppermute | solution.py:586
  542.5 15.7 %collective-permute-start.44 = (bf16[320,1024]{1,0:T(8,128)(2,1)S(1)}, bf16[320,1024]{1,0:T(8,128)(2,1)S(1)}, u32[]{:S(2)}, u32[]{:S(2)}) collective-permute-start(bf16[320,1024]{1,0:T(8,128)(2,1)S(1)} %pad_maximum_fusion.16), channel_id=1, source_target_pairs={{0,2},{1,3},{2,0},{3,1},{4,6},{5,7},{6,4},{7,5},{8,10},{9,11},{10,... | collective-permute-start | bytes 1966088 | tf_op jit(solution)/shard_map/ppermute | solution.py:586
  571.1 56.8 %collective-permute-start.61 = (bf16[352,2048]{1,0:T(8,128)(2,1)}, bf16[352,2048]{1,0:T(8,128)(2,1)}, u32[]{:S(2)}, u32[]{:S(2)}) collective-permute-start(bf16[352,2048]{1,0:T(8,128)(2,1)} %shard_map.383), channel_id=1, source_target_pairs={{0,2},{1,3},{2,0},{3,1},{4,6},{5,7},{6,4},{7,5},{8,10},{9,11},{10,... | collective-permute-start | bytes 4325384 | tf_op jit(solution)/shard_map/ppermute | solution.py:586
  571.8 64.9 %collective-permute-start.60 = (bf16[352,2048]{1,0:T(8,128)(2,1)}, bf16[352,2048]{1,0:T(8,128)(2,1)}, u32[]{:S(2)}, u32[]{:S(2)}) collective-permute-start(bf16[352,2048]{1,0:T(8,128)(2,1)} %shard_map.381), channel_id=1, source_target_pairs={{0,2},{1,3},{2,0},{3,1},{4,6},{5,7},{6,4},{7,5},{8,10},{9,11},{10,... | collective-permute-start | bytes 4325384 | tf_op jit(solution)/shard_map/ppermute | solution.py:586
  617.6 27.6 %collective-permute-start.56 = (bf16[640,2048]{1,0:T(8,128)(2,1)}, bf16[640,2048]{1,0:T(8,128)(2,1)}, u32[]{:S(2)}, u32[]{:S(2)}) collective-permute-start(bf16[640,2048]{1,0:T(8,128)(2,1)} %get-tuple-element.98), channel_id=1, source_target_pairs={{0,1},{1,0},{2,3},{3,2},{4,5},{5,4},{6,7},{7,6},{8,9},{9,8},{10,11... | collective-permute-start | bytes 7864328 | tf_op jit(solution)/shard_map/ppermute | solution.py:586
  618.9 33.0 %collective-permute-start.59 = (bf16[640,2048]{1,0:T(8,128)(2,1)}, bf16[640,2048]{1,0:T(8,128)(2,1)}, u32[]{:S(2)}, u32[]{:S(2)}) collective-permute-start(bf16[640,2048]{1,0:T(8,128)(2,1)} %get-tuple-element.99), channel_id=1, source_target_pairs={{0,1},{1,0},{2,3},{3,2},{4,5},{5,4},{6,7},{7,6},{8,9},{9,8},{10,11... | collective-permute-start | bytes 7864328 | tf_op jit(solution)/shard_map/ppermute | solution.py:586
  625.9 50.1 %collective-permute-start.64 = (bf16[352,2048]{1,0:T(8,128)(2,1)}, bf16[352,2048]{1,0:T(8,128)(2,1)}, u32[]{:S(2)}, u32[]{:S(2)}) collective-permute-start(bf16[352,2048]{1,0:T(8,128)(2,1)} %shard_map.386), channel_id=1, source_target_pairs={{0,2},{1,3},{2,0},{3,1},{4,6},{5,7},{6,4},{7,5},{8,10},{9,11},{10,... | collective-permute-start | bytes 4325384 | tf_op jit(solution)/shard_map/ppermute | solution.py:586
  627.9 40.5 %collective-permute-start.52 = (bf16[416,2048]{1,0:T(8,128)(2,1)}, bf16[416,2048]{1,0:T(8,128)(2,1)}, u32[]{:S(2)}, u32[]{:S(2)}) collective-permute-start(bf16[416,2048]{1,0:T(8,128)(2,1)} %shard_map.375), channel_id=1, source_target_pairs={{0,4},{4,0},{1,5},{5,1},{2,6},{6,2},{3,7},{7,3},{8,12},{12,8},{9,1... | collective-permute-start | bytes 5111816 | tf_op jit(solution)/shard_map/ppermute | solution.py:586
  648.0 47.6 %collective-permute-start.57 = (bf16[2,160,2048]{2,1,0:T(8,128)(2,1)}, bf16[2,160,2048]{2,1,0:T(8,128)(2,1)}, u32[]{:S(2)}, u32[]{:S(2)}) collective-permute-start(bf16[2,160,2048]{2,1,0:T(8,128)(2,1)} %fusion.11), channel_id=1, source_target_pairs={{0,2},{1,3},{2,0},{3,1},{4,6},{5,7},{6,4},{7,5},{8,10},{9,11},{10,... | collective-permute-start | bytes 3932168 | tf_op jit(solution)/shard_map/ppermute | solution.py:586
  651.1 100.7 %collective-permute-start.73 = (bf16[2112,256]{1,0:T(8,128)(2,1)}, bf16[2112,256]{1,0:T(8,128)(2,1)}, u32[]{:S(2)}, u32[]{:S(2)}) collective-permute-start(bf16[2112,256]{1,0:T(8,128)(2,1)} %constant_dynamic-slice_fusion), channel_id=1, source_target_pairs={{0,4},{4,0},{1,5},{5,1},{2,6},{6,2},{3,7},{7,3},{8,12},{12,8},{9,1... | collective-permute-start | bytes 3244040 | tf_op jit(solution)/shard_map/ppermute | solution.py:586
  656.3 48.0 %collective-permute-start.62 = (bf16[2,160,1024]{2,1,0:T(8,128)(2,1)}, bf16[2,160,1024]{2,1,0:T(8,128)(2,1)}, u32[]{:S(2)}, u32[]{:S(2)}) collective-permute-start(bf16[2,160,1024]{2,1,0:T(8,128)(2,1)} %bitcast.49), channel_id=1, source_target_pairs={{0,4},{4,0},{1,5},{5,1},{2,6},{6,2},{3,7},{7,3},{8,12},{12,8},{9,1... | collective-permute-start | bytes 1966088 | tf_op jit(solution)/shard_map/ppermute | solution.py:586
  668.4 41.0 %collective-permute-start.65 = (bf16[2,160,1024]{2,1,0:T(8,128)(2,1)}, bf16[2,160,1024]{2,1,0:T(8,128)(2,1)}, u32[]{:S(2)}, u32[]{:S(2)}) collective-permute-start(bf16[2,160,1024]{2,1,0:T(8,128)(2,1)} %fusion.25), channel_id=1, source_target_pairs={{0,2},{1,3},{2,0},{3,1},{4,6},{5,7},{6,4},{7,5},{8,10},{9,11},{10,... | collective-permute-start | bytes 1966088 | tf_op jit(solution)/shard_map/ppermute | solution.py:586
  676.5 60.6 %collective-permute-start.53 = (bf16[160,2048]{1,0:T(8,128)(2,1)S(1)}, bf16[160,2048]{1,0:T(8,128)(2,1)}, u32[]{:S(2)}, u32[]{:S(2)}) collective-permute-start(bf16[160,2048]{1,0:T(8,128)(2,1)S(1)} %get-tuple-element.223.refs_3_), channel_id=1, source_target_pairs={{0,24},{8,0},{16,8},{24,16},{1,25},{9,1},{17,9},{25,17},{2,26},{10... | collective-permute-start | bytes 1966088 | tf_op jit(solution)/shard_map/ppermute | solution.py:591
  695.6 77.1 %collective-permute-start.55 = (bf16[160,2048]{1,0:T(8,128)(2,1)}, bf16[160,2048]{1,0:T(8,128)(2,1)}, u32[]{:S(2)}, u32[]{:S(2)}) collective-permute-start(bf16[160,2048]{1,0:T(8,128)(2,1)} %get-tuple-element.222.refs_4_), channel_id=1, source_target_pairs={{0,8},{8,16},{16,24},{24,0},{1,9},{9,17},{17,25},{25,1},{2,10},{10... | collective-permute-start | bytes 1966088 | tf_op jit(solution)/shard_map/ppermute | solution.py:591
  704.4 68.3 %collective-permute-start.58 = (bf16[160,2048]{1,0:T(8,128)(2,1)}, bf16[160,2048]{1,0:T(8,128)(2,1)}, u32[]{:S(2)}, u32[]{:S(2)}) collective-permute-start(bf16[160,2048]{1,0:T(8,128)(2,1)} %fusion.27), channel_id=1, source_target_pairs={{0,4},{4,0},{1,5},{5,1},{2,6},{6,2},{3,7},{7,3},{8,12},{12,8},{9,1... | collective-permute-start | bytes 1966088 | tf_op jit(solution)/shard_map/ppermute | solution.py:586
  709.4 30.8 %collective-permute-start.63 = (bf16[160,1024]{1,0:T(8,128)(2,1)S(1)}, bf16[160,1024]{1,0:T(8,128)(2,1)S(1)}, u32[]{:S(2)}, u32[]{:S(2)}) collective-permute-start(bf16[160,1024]{1,0:T(8,128)(2,1)S(1)} %fusion.30), channel_id=1, source_target_pairs={{0,2},{1,3},{2,0},{3,1},{4,6},{5,7},{6,4},{7,5},{8,10},{9,11},{10,... | collective-permute-start | bytes 983048 | tf_op jit(solution)/shard_map/ppermute | solution.py:586
  741.0 31.7 %collective-permute-start.54 = (bf16[160,2048]{1,0:T(8,128)(2,1)}, bf16[160,2048]{1,0:T(8,128)(2,1)}, u32[]{:S(2)}, u32[]{:S(2)}) collective-permute-start(bf16[160,2048]{1,0:T(8,128)(2,1)} %add_convert_fusion.9), channel_id=1, source_target_pairs={{0,24},{8,0},{16,8},{24,16},{1,25},{9,1},{17,9},{25,17},{2,26},{10... | collective-permute-start | bytes 1966088 | tf_op jit(solution)/shard_map/ppermute | solution.py:591
  779.2 12.8 %collective-permute-start.72 = (bf16[1024,256]{1,0:T(8,128)(2,1)S(1)}, bf16[1024,256]{1,0:T(8,128)(2,1)S(1)}, u32[]{:S(2)}, u32[]{:S(2)}) collective-permute-start(bf16[1024,256]{1,0:T(8,128)(2,1)S(1)} %constant_dynamic-slice_fusion.1), channel_id=1, source_target_pairs={{0,4},{4,0},{1,5},{5,1},{2,6},{6,2},{3,7},{7,3},{8,12},{12,8},{9,1... | collective-permute-start | bytes 1572872 | tf_op jit(solution)/shard_map/ppermute | solution.py:586
  (113 other events, 1493.3 us)
Sparse Core Ops, SparseCore 0:
  30.1 82.3 all-gather.4
  114.1 53.4 all-gather.6
  169.1 85.5 all-gather.8
  256.7 115.4 all-gather.10
  473.2 165.1 reduce-scatter.2
  652.0 115.0 reduce-scatter.4
